TPU v7x, 256 devices: a whole 4x4x8 slice. The times are simulated.
256 devices in a mesh: tm: 16 (over x_lo, z), space: 16 (over x_hi, y, core).
Axes of the slice: x: 4 (x_hi: 2, x_lo: 2; x = x_hi * 2 + x_lo), y: 4, z: 8, core: 2. Of those that a mesh axis runs over, the one named last changes fastest.
Arguments:
- latent: bfloat16 [2, 16, 2048, 1152], P(None, 'tm', 'space'), may hold values from -6 to 6
- spatial_cache: bfloat16 [2, 16, 2048, 1152], P(None, 'tm', 'space'), may hold values from -6 to 6
- modulation: float32 [2, 2, 3, 1152], replicated, may hold values from -3 to 3
- weights: bfloat16 [2, 1152, 4608], P(None, 'tm'), may hold values from -0.1875 to 0.1875
Outputs:
- block_out: bfloat16 [2, 16, 2048, 1152], P(None, 'tm', 'space')
- new_spatial: bfloat16 [2, 16, 2048, 1152], P(None, 'tm', 'space')
- new_temporal: bfloat16 [2, 16, 2048, 1152], P(None, 'tm', 'space')
All inputs are finite; a program needn't handle non-finite values.
Results may differ from a plain program's by a relative error of at most 0.015.
Values may be sent and summed in bfloat16 or wider, within the bound.
No kernel may reach another device: no remote copies, remote signals or barrier semaphores. Data moves between devices by JAX's collectives and lax.ppermute only.
A program may use at most 128 MiB of HBM per device.

v0:
```python
import jax
import jax.numpy as jnp
from jax import lax
from jax.sharding import PartitionSpec as P

D = 1152
HEAD_DIM = 72


def layer_norm(h):
    x = h.astype(jnp.float32)
    mean = jnp.mean(x, axis=-1, keepdims=True)
    var = jnp.mean((x - mean) ** 2, axis=-1, keepdims=True)
    return (x - mean) * lax.rsqrt(var + 1e-06)


def modulate(h, mods):
    return (layer_norm(h) * (1.0 + mods[1]) + mods[0]).astype(jnp.bfloat16)


def rms_norm(v):
    return v * lax.rsqrt(jnp.mean(v * v, axis=-1, keepdims=True) + 1e-06)


def pack_heads(qkv):
    lead = qkv.shape[:-1]
    split = qkv.reshape(lead + (qkv.shape[-1] // (3 * HEAD_DIM), 3, HEAD_DIM))
    normed = jnp.stack(
        [rms_norm(split[..., 0, :]), rms_norm(split[..., 1, :]), split[..., 2, :]], axis=-2
    )
    return normed.astype(jnp.bfloat16).reshape(qkv.shape)


def attend(packed):
    count, length, width = packed.shape
    heads_here = width // (3 * HEAD_DIM)
    split = packed.reshape(count, length, heads_here, 3, HEAD_DIM)
    scores = jnp.einsum(
        "nlhd,nmhd->nhlm", split[..., 0, :], split[..., 1, :], preferred_element_type=jnp.float32
    )
    expo = jnp.exp(scores / jnp.sqrt(jnp.float32(HEAD_DIM)))
    probs = (expo / jnp.sum(expo, axis=-1, keepdims=True)).astype(jnp.bfloat16)
    out = jnp.einsum("nhlm,nmhd->nlhd", probs, split[..., 2, :], preferred_element_type=jnp.float32)
    return out.astype(jnp.bfloat16).reshape(count, length, heads_here * HEAD_DIM)


def spatial_attend(packed):
    out = lax.map(attend, packed)
    return out


def temporal_attend(packed):
    batch, frames, tokens, width = packed.shape
    tokens_major = jnp.transpose(packed, (0, 2, 1, 3)).reshape(batch * tokens, frames, width)
    out = attend(tokens_major)
    return jnp.transpose(out.reshape(batch, tokens, frames, out.shape[-1]), (0, 2, 1, 3))


def fetch_weight(shard):
    return lax.all_gather(shard, "tm", axis=0, tiled=True)


def project_out(attn, weight):
    shape = attn.shape
    proj = jnp.dot(
        attn.reshape(-1, shape[-1]), weight[:, 3 * D :], preferred_element_type=jnp.float32
    )
    return proj.astype(jnp.bfloat16).reshape(shape)


def project_all(modin, weight):
    shape = modin.shape
    qkv = jnp.dot(
        modin.reshape(-1, shape[-1]), weight[:, : 3 * D], preferred_element_type=jnp.float32
    )
    return pack_heads(qkv).reshape(shape[:-1] + (3 * D,))


def add_gated(h, gate, branch):
    return (h.astype(jnp.float32) + gate * branch.astype(jnp.float32)).astype(jnp.bfloat16)


def shards(latent, spatial_cache, modulation, weights):
    h = add_gated(latent, modulation[0, 0, 2], spatial_cache)
    temporal_weight = fetch_weight(weights[1])
    packed = project_all(modulate(h, modulation[0, 1]), temporal_weight)
    attn = temporal_attend(lax.all_to_all(packed, "tm", split_axis=2, concat_axis=1, tiled=True))
    attn = lax.all_to_all(attn, "tm", split_axis=1, concat_axis=2, tiled=True)
    new_temporal = project_out(attn, temporal_weight)
    h = add_gated(h, modulation[0, 1, 2], new_temporal)
    spatial_weight = fetch_weight(weights[0])
    modin = modulate(h, modulation[1, 0])
    packed = project_all(modin, spatial_weight)
    attn = spatial_attend(lax.all_to_all(packed, "space", split_axis=3, concat_axis=2, tiled=True))
    attn = lax.all_to_all(attn, "space", split_axis=2, concat_axis=3, tiled=True)
    new_spatial = project_out(attn, spatial_weight)
    h = add_gated(h, modulation[1, 0, 2], new_spatial)
    block_out = add_gated(h, modulation[1, 1, 2], new_temporal)
    return (block_out, new_spatial, new_temporal)


def solution(mesh):
    in_specs = (
        P(None, "tm", "space", None),
        P(None, "tm", "space", None),
        P(),
        P(None, "tm", None),
    )
    out_specs = (
        P(None, "tm", "space", None),
        P(None, "tm", "space", None),
        P(None, "tm", "space", None),
    )
    return jax.shard_map(shards, mesh=mesh, in_specs=in_specs, out_specs=out_specs, check_vma=False)
```

profile of v0, /device:TPU:1, one launch (start us, length us, event | category | flops | bytes accessed | tf_op | source)
XLA Modules:
  0.0 425.0 jit_solution(11456495705538441762)
XLA Ops:
  7.2 2.6 fusion.42
  9.9 0.7 all-gather.7.cloned.1.call-update
  10.6 0.7 slice_reduce_fusion.2
  11.3 0.3 convert_reduce_fusion.1
  11.6 0.3 fusion.27
  11.9 0.3 fusion.30
  12.2 125.0 %all-gather.5.cloned.1.call-done = bf16[1,1152,4608]{2,1,0:T(8,128)(2,1)} async-done(((bf16[1,72,4608]{2,1,0:T(8,128)(2,1)}), bf16[1,1152,4608]{2,1,0:T(8,128)(2,1)}) %all-gather.5.cloned.1.call-update) | async-done | bytes 10616848 | tf_op jit(solution)/shard_map/all_gather | solution.py:60
  137.2 6.9 %slice_bitcast_fusion.7 = bf16[3456,1152]{0,1:T(8,128)(2,1)} fusion(bf16[1152,4608]{1,0:T(8,128)(2,1)} %bitcast.124), kind=kLoop, calls=%fused_computation.14 | loop fusion | bytes 15925248 | tf_op jit(solution)/shard_map/dot_general | solution.py:73
  144.1 11.6 %copy.72 = bf16[3456,1152]{1,0:T(8,128)(2,1)} copy(bf16[3456,1152]{0,1:T(8,128)(2,1)} %slice_bitcast_fusion.7) | data formatting | bytes 15925248 | tf_op jit(solution)/shard_map/dot_general | solution.py:73
  155.7 5.9 %fusion.43 = f32[256,16,3,72]{0,3,2,1:T(8,128)S(1)} fusion(bf16[256,1152,1,1]{1,0,3,2:T(8,128)(2,1)S(1)} %bitcast.131, bf16[16,3,72,1152]{3,2,1,0:T(8,128)(2,1)} %bitcast.118), kind=kOutput, calls=%fused_computation.90 | convolution fusion | flops 2038431744 | bytes 12091392 | tf_op jit(solution)/shard_map/dot_general | solution.py:73
  161.9 0.2 multiply_convert_fusion.3
  162.3 1.9 convert_element_type.117
  164.3 5.9 %copy.73 = bf16[2,1,128,3456]{3,0,1,2:T(2,128)(2,1)S(1)} copy(bf16[2,1,128,3456]{2,0,3,1:T(2,128)(2,1)} %convert_element_type.117) | data formatting | bytes 3538944 | tf_op jit(solution)/shard_map/convert_element_type | solution.py:31
  170.2 65.3 %all_to_all.54 = bf16[2,1,128,3456]{3,0,1,2:T(2,128)(2,1)S(1)} all-to-all(bf16[2,1,128,3456]{3,0,1,2:T(2,128)(2,1)S(1)} %copy.73), channel_id=1, replica_groups=mesh['tm'=16,'space'=16] {'tm'}, dimensions={2} | all-to-all | bytes 3538944 | tf_op jit(solution)/shard_map/all_to_all | solution.py:87
  235.8 7.4 %reshape_reshape.8 = bf16[16,16,16,3,72]{4,3,2,1,0:T(4,128)(2,1)} reshape(bf16[2,8,16,3456]{3,2,1,0:T(8,128)(2,1)S(1)} %copy.75) | data formatting | bytes 3538944 | tf_op jit(solution)/shard_map/reshape;reshape | solution.py:37
  243.3 10.6 %fusion.41 = (bf16[16,16,16,1,72]{4,3,2,1,0:T(2,128)(2,1)S(1)}, bf16[16,16,16,1,72]{4,3,2,1,0:T(2,128)(2,1)S(1)}, bf16[16,16,16,1,72]{4,3,2,1,0:T(2,128)(2,1)S(1)}) fusion(bf16[16,16,16,3,72]{4,3,2,1,0:T(4,128)(2,1)} %reshape_reshape.8), kind=kLoop, calls=%fused_computation.88 | loop fusion | bytes 3538944 | tf_op jit(solution)/shard_map/slice | solution.py:39
  253.9 1.6 fusion.17
  255.6 1.0 fusion.22
  256.6 0.3 copy.80
  256.9 1.3 reshape_reshape.9
  258.1 0.9 copy.81
  259.1 4.4 %all-to-all-start.1 = ((bf16[2,16,8,1152]{3,2,0,1:T(8,128)(2,1)}), bf16[2,16,8,1152]{3,2,0,1:T(8,128)(2,1)S(1)}, u32[]{:S(2)}, u32[]{:S(2)}) async-start(bf16[2,16,8,1152]{3,2,0,1:T(8,128)(2,1)} %copy.81), calls=%async_computation.1 | async-start | bytes 1179648 | tf_op jit(solution)/shard_map/all_to_all | solution.py:88
  263.5 47.1 %all-gather.7.cloned.1.call-done = bf16[1,1152,4608]{2,1,0:T(8,128)(2,1)} async-done(((bf16[1,72,4608]{2,1,0:T(8,128)(2,1)}), bf16[1,1152,4608]{2,1,0:T(8,128)(2,1)}) %all-gather.7.cloned.1.call-update) | async-done | bytes 10616848 | tf_op jit(solution)/shard_map/all_gather | solution.py:60
  310.6 6.9 %slice_bitcast_fusion.6 = bf16[3456,1152]{0,1:T(8,128)(2,1)} fusion(bf16[1152,4608]{1,0:T(8,128)(2,1)} %bitcast.122), kind=kLoop, calls=%fused_computation.13 | loop fusion | bytes 15925248 | tf_op jit(solution)/shard_map/dot_general | solution.py:73
  317.6 11.5 %copy.84 = bf16[3456,1152]{1,0:T(8,128)(2,1)} copy(bf16[3456,1152]{0,1:T(8,128)(2,1)} %slice_bitcast_fusion.6) | data formatting | bytes 15925248 | tf_op jit(solution)/shard_map/dot_general | solution.py:73
  329.1 2.9 fusion.11
  332.0 0.3 convert_reduce_fusion
  332.3 0.3 fusion.23
  332.6 0.3 fusion.26
  332.9 0.4 copy-done
  333.4 2.6 fusion.44
  336.3 0.2 multiply_convert_fusion.1
  336.7 1.9 convert_element_type.126
  338.6 7.1 %all-to-all-start.2 = ((bf16[2,1,128,3456]{2,0,1,3:T(2,128)(2,1)}), bf16[2,1,128,3456]{2,0,1,3:T(2,128)(2,1)S(1)}, u32[]{:S(2)}, u32[]{:S(2)}) async-start(bf16[2,1,128,3456]{2,0,1,3:T(2,128)(2,1)} %bitcast.120), calls=%async_computation.2 | async-start | bytes 3538944 | tf_op jit(solution)/shard_map/all_to_all | solution.py:94
  345.7 25.0 %all-to-all-done.2 = bf16[2,1,128,3456]{2,0,1,3:T(2,128)(2,1)S(1)} async-done(((bf16[2,1,128,3456]{2,0,1,3:T(2,128)(2,1)}), bf16[2,1,128,3456]{2,0,1,3:T(2,128)(2,1)S(1)}, u32[]{:S(2)}, u32[]{:S(2)}) %all-to-all-start.2) | async-done | bytes 1769504 | tf_op jit(solution)/shard_map/all_to_all | solution.py:94
  370.7 1.7 copy.86
  372.4 2.7 all_to_all.46
  375.0 12.8 %while.10 = (s32[]{:T(128)}, bf16[2,1,2048,72]{2,3,1,0:T(8,128)(2,1)}, bf16[2,1,2048,216]{2,3,1,0:T(8,128)(2,1)S(1)}, s32[]{:T(128)}) while((s32[]{:T(128)}, bf16[2,1,2048,72]{2,3,1,0:T(8,128)(2,1)}, bf16[2,1,2048,216]{2,3,1,0:T(8,128)(2,1)S(1)}, s32[]{:T(128)}) %tuple.48), condition=%wide.region_11.12_spmd, body=%wide.region_9.11_spmd.sunk | while | flops 1229076480 | bytes 36520504 | solution.py:48
  375.1 2.5 fusion.52
  377.7 3.7 fusion.53
  381.5 2.5 fusion.52
  384.0 3.7 fusion.53
  387.8 2.4 copy.87
  390.2 22.7 %all_to_all.55 = bf16[2,1,2048,72]{3,0,1,2:T(2,128)(2,1)S(1)} all-to-all(bf16[2,1,2048,72]{3,0,1,2:T(2,128)(2,1)S(1)} %copy.87), channel_id=1, replica_groups=mesh['tm'=16,'space'=16] {'space'}, dimensions={2} | all-to-all | bytes 1179648 | tf_op jit(solution)/shard_map/all_to_all | solution.py:95
  412.8 0.7 copy.96
  413.5 0.6 copy.89
  414.2 2.8 fusion.14
  417.0 1.1 fusion.32
  (38 shorter events, 1.6 us)
Async XLA Ops:
  7.2 3.4 copy-start.7
  7.2 4.1 copy-start.3
  7.2 4.1 copy-start.2
  7.2 130.0 %all-gather.5.cloned.1.call-start = ((), (), s32[]{:S(2)}) async-start(), calls=%async_computation.4 | async-start | bytes 11280384 | tf_op jit(solution)/shard_map/all_gather | solution.py:60
  9.8 300.8 %all-gather.7.cloned.1.call-start = ((), (), s32[]{:S(2)}) async-start(), calls=%async_computation.5 | async-start | bytes 11280384 | tf_op jit(solution)/shard_map/all_gather | solution.py:60
  259.1 70.0 %all-to-all-start.1 = ((bf16[2,16,8,1152]{3,2,0,1:T(8,128)(2,1)}), bf16[2,16,8,1152]{3,2,0,1:T(8,128)(2,1)S(1)}, u32[]{:S(2)}, u32[]{:S(2)}) async-start(bf16[2,16,8,1152]{3,2,0,1:T(8,128)(2,1)} %copy.81), calls=%async_computation.1 | async-start | bytes 1179648 | tf_op jit(solution)/shard_map/all_to_all | solution.py:88
  329.1 4.3 %copy-start = (bf16[3456,1152]{1,0:T(8,128)(2,1)S(1)}, bf16[3456,1152]{1,0:T(8,128)(2,1)}, u32[]{:S(2)}) copy-start(bf16[3456,1152]{1,0:T(8,128)(2,1)} %copy.84) | copy-start | bytes 23887876
  332.0 85.0 %copy-start.1 = (bf16[256,1152]{1,0:T(8,128)(2,1)}, bf16[256,1152]{1,0:T(8,128)(2,1)S(1)}, u32[]{:S(2)}) copy-start(bf16[256,1152]{1,0:T(8,128)(2,1)S(1)} %fusion.11) | copy-start | bytes 1769476
  338.6 32.1 %all-to-all-start.2 = ((bf16[2,1,128,3456]{2,0,1,3:T(2,128)(2,1)}), bf16[2,1,128,3456]{2,0,1,3:T(2,128)(2,1)S(1)}, u32[]{:S(2)}, u32[]{:S(2)}) async-start(bf16[2,1,128,3456]{2,0,1,3:T(2,128)(2,1)} %bitcast.120), calls=%async_computation.2 | async-start | bytes 3538944 | tf_op jit(solution)/shard_map/all_to_all | solution.py:94
  414.2 2.8 copy-start.5
  414.2 2.8 copy-start.6
  417.0 1.2 copy-start.4
Sparse Core Ops, SparseCore 0:
  10.0 127.1 all-gather.4
  139.0 171.6 all-gather.6
where the time goes:
time: 426 us; the launch traced here: 425 us
  waiting for transfers between devices  198 us (46%)
  blocking collectives  88 us (21%)
  local copies, waits for them, and re-layouts  79 us (19%)
  matrix products  29.4 us (7%)
  between operations  14.4 us (3%)
  starting transfers between devices  11.6 us (3%)
  other arithmetic  4.93 us (1%)
    all_gather x2, waiting for transfers between devices, fetch_weight(): return lax.all_gather(shard, 'tm', axis=0, tiled=True)  172 us
    all_to_all x1, blocking collectives, shards(): lax.all_to_all(packed, 'tm', split_axis=2, concat_axis=1, tiled=True)  65.3 us
    dot_general x4, local copies, waits for them, and re-layouts, project_all(): jnp.dot(modin.reshape(-1, shape[-1]), weight[:, :3 * D], preferred_elemen...  37 us
    all_to_all x1, waiting for transfers between devices, shards(): lax.all_to_all(packed, 'space', split_axis=3, concat_axis=2, tiled=True)  25 us
    all_to_all x1, blocking collectives, shards(): lax.all_to_all(attn, 'space', split_axis=2, concat_axis=3, tiled=True)  22.7 us
    slice x1, local copies, waits for them, and re-layouts, attend(): split[..., 0, :]  10.6 us
    convert_element_type x3, local copies, waits for them, and re-layouts, pack_heads(): return normed.astype(jnp.bfloat16).reshape(qkv.shape)  9.77 us
    dot_general x3, matrix products, attend(): jnp.einsum('nhlm,nmhd->nlhd', probs, split[..., 2, :], preferred_element_...  8.52 us
  transfers between devices with their start and end apart: 4, of which 3 were waited for; matrix products, arithmetic and copies ran while one was open for 18% of the time, Pallas kernels for 0%

commit v1 on v0

v1 whole, which is shorter than its diff:
```python
import math

import jax
import jax.numpy as jnp
from jax import lax
from jax.experimental import pallas as pl
from jax.experimental.pallas import tpu as pltpu
from jax.sharding import Mesh, PartitionSpec as P

D = 1152
HD = 72
HALF = D // 2
QKV = 3 * HALF
TOK = 256
SCALE = math.log2(math.e) / math.sqrt(HD)
TM = ("xl", "z")
SPACE = ("xh", "y", "c")
XX = ("xl", "xh")
BF = jnp.bfloat16
F32 = jnp.float32
VMEM = pl.BlockSpec(memory_space=pltpu.VMEM)
SMEM = pl.BlockSpec(memory_space=pltpu.SMEM)


def x_pairs(step):
    place = lambda x: (x % 2) * 2 + x // 2
    return [(place(x), place((x + step) % 4)) for x in range(4)]


CORE = [(0, 1), (1, 0)]
X_UP, X_DOWN = x_pairs(1), x_pairs(-1)


def call(body, name, outs, ins, scratch=(), flops=0, nbytes=0, trans=0):
    return pl.pallas_call(
        body,
        name=name,
        out_shape=outs,
        in_specs=ins,
        out_specs=jax.tree.map(lambda _: VMEM, outs),
        scratch_shapes=scratch,
        cost_estimate=pl.CostEstimate(flops=flops, bytes_accessed=nbytes, transcendentals=trans),
        compiler_params=pltpu.CompilerParams(vmem_limit_bytes=48 * 2**20),
    )


def sds(*shape, dtype=BF):
    return jax.ShapeDtypeStruct(shape, dtype)


def normed(h, scale, shift):
    x = h.astype(F32)
    mean = jnp.mean(x, axis=-1, keepdims=True)
    x = x - mean
    var = jnp.mean(x * x, axis=-1, keepdims=True)
    return (x * lax.rsqrt(var + 1e-06) * (1.0 + scale) + shift).astype(BF)


def gated(h, gate, branch):
    return (h.astype(F32) + gate * branch.astype(F32)).astype(BF)


def first_kernel(lat, cache, mods, h_out, modin_out):
    h = gated(lat[...], mods[2:3], cache[...])
    h_out[...] = h
    modin = normed(h, mods[4:5], mods[3:4]).astype(F32)
    by_dest = jnp.transpose(modin.reshape(2, 16, 8, D), (1, 0, 2, 3))
    modin_out[...] = by_dest.reshape(16, 16, D).astype(BF)


def middle_kernel(h1, chunks, mods, nt_out, h_out, modin_out):
    nt = chunks[...].astype(F32).reshape(16, 2, 8, D)
    nt = jnp.transpose(nt, (1, 0, 2, 3)).reshape(TOK, D).astype(BF)
    nt_out[...] = nt
    h = gated(h1[...], mods[5:6], nt)
    h_out[...] = h
    modin_out[...] = normed(h, mods[7:8], mods[6:7])


def project(flags, x_own, x_other, w_own, w_a, w_b, w_all, y_t):
    w_all[:HALF] = w_own[...]
    w_all[HALF : HALF + 288] = w_a[...]
    w_all[HALF + 288 :] = w_b[...]
    x = jnp.concatenate([x_own[...], x_other[...]], axis=0)
    low, high = x[:, :HALF], x[:, HALF:]
    swap = flags[0] == 1
    x = jnp.concatenate([jnp.where(swap, high, low), jnp.where(swap, low, high)], axis=1)
    for start in range(0, QKV, 256):
        stop = min(start + 256, QKV)
        y = jnp.dot(x, w_all[:, start:stop], preferred_element_type=F32)
        y_t[start:stop] = y.T


def unit(v, factor):
    mean = jnp.mean(v * v, axis=0, keepdims=True)
    return (v * (lax.rsqrt(mean + 1e-06) * factor)).astype(BF)


def head_qkv(y_t, head):
    base = head * 3 * HD
    return (
        unit(y_t[base : base + HD], SCALE),
        unit(y_t[base + HD : base + 2 * HD], 1.0),
        y_t[base + 2 * HD : base + 3 * HD].astype(BF),
    )


def spatial_qkv_kernel(flags, x_own, x_other, w_own, w_a, w_b, out, w_all, y_t):
    project(flags, x_own, x_other, w_own, w_a, w_b, w_all, y_t)
    for head in range(8):
        q, k, v = head_qkv(y_t, head)
        out[head, 0] = q
        out[head, 1] = k
        out[head, 2] = v


def attend(k, q, v, mask=None):
    s = lax.dot_general(k, q, (((0,), (0,)), ((), ())), preferred_element_type=F32)
    p = jnp.exp2(s)
    if mask is not None:
        p = jnp.where(mask, p, 0.0)
    total = jnp.sum(p, axis=0, keepdims=True)
    o = jnp.dot(v, p.astype(BF), preferred_element_type=F32)
    return (o * (1.0 / total)).astype(BF)


def temporal_kernel(flags, x_own, x_other, w_own, w_a, w_b, own_out, other_out, w_all, y_t):
    project(flags, x_own, x_other, w_own, w_a, w_b, w_all, y_t)
    key = lax.broadcasted_iota(jnp.int32, (TOK, TOK), 0)
    query = lax.broadcasted_iota(jnp.int32, (TOK, TOK), 1)
    mask = (key & 15) == (query & 15)
    for head in range(8):
        q, k, v = head_qkv(y_t, head)
        own_out[head] = attend(k[:, :TOK], q[:, :TOK], v[:, :TOK], mask)
        other_out[head] = attend(k[:, TOK:], q[:, TOK:], v[:, TOK:], mask)


def spatial_kernel(q_ref, all_ref, out, keys, values):
    @pl.when(pl.program_id(0) == 0)
    def _():
        for b in range(2):
            for src in range(8):
                for rel in range(2):
                    lanes = slice(rel * 256 + b * 128, rel * 256 + b * 128 + 128)
                    rows = slice(src * 256 + rel * 128, src * 256 + rel * 128 + 128)
                    keys[b, rows] = all_ref[src, 1, :, lanes].astype(F32).T.astype(BF)
                    values[b, :, rows] = all_ref[src, 2, :, lanes]

    for b in range(2):
        parts = [q_ref[0, 0, :, rel * 256 + b * 128 : rel * 256 + b * 128 + 128] for rel in range(2)]
        q = jnp.concatenate(parts, axis=1)
        s = jnp.dot(keys[b], q, preferred_element_type=F32)
        p = jnp.exp2(s)
        total = jnp.sum(p, axis=0, keepdims=True)
        o = jnp.dot(values[b], p.astype(BF), preferred_element_type=F32)
        o = (o * (1.0 / total)).astype(BF)
        for rel in range(2):
            out[0, :, rel * 256 + b * 128 : rel * 256 + b * 128 + 128] = o[:, rel * 128 : rel * 128 + 128]


def spatial_attend(packed):
    return pl.pallas_call(
        spatial_kernel,
        name="spatial_attend",
        grid=(8,),
        out_shape=sds(8, HD, 512),
        in_specs=[
            pl.BlockSpec((1, 3, HD, 512), lambda j: (j, 0, 0, 0)),
            pl.BlockSpec((8, 3, HD, 512), lambda j: (0, 0, 0, 0)),
        ],
        out_specs=pl.BlockSpec((1, HD, 512), lambda j: (j, 0, 0)),
        scratch_shapes=[pltpu.VMEM((2, 2048, HD), BF), pltpu.VMEM((2, HD, 2048), BF)],
        cost_estimate=pl.CostEstimate(flops=2 * 2**34, bytes_accessed=3 * 2**20, transcendentals=2**23),
        compiler_params=pltpu.CompilerParams(vmem_limit_bytes=48 * 2**20),
    )(packed, packed)


def out_project(flags, a_own, a_rec, w_mine, w_partner):
    same = flags[0] == flags[1]
    mine, received = a_own[...], a_rec[...]
    a = jnp.concatenate([jnp.where(same, mine, received), jnp.where(same, received, mine)], axis=0)
    a = a.astype(F32).T.astype(BF)
    halves = []
    for own, other_a, other_b in (w_mine, w_partner):
        w = jnp.concatenate([own[...], other_a[...], other_b[...]], axis=0)
        halves.append(jnp.dot(a, w, preferred_element_type=F32).astype(BF))
    first = flags[1] == 0
    return jnp.concatenate(
        [jnp.where(first, halves[0], halves[1]), jnp.where(first, halves[1], halves[0])], axis=1
    )


def temporal_out_kernel(flags, a_own, a_rec, m0, m1, m2, p0, p1, p2, out):
    out[...] = out_project(flags, a_own, a_rec, (m0, m1, m2), (p0, p1, p2))


def last_kernel(flags, a_own, a_rec, m0, m1, m2, p0, p1, p2, h2, nt, mods, block_out, ns_out):
    ns = out_project(flags, a_own, a_rec, (m0, m1, m2), (p0, p1, p2))
    ns_out[...] = ns
    h = gated(h2[...], mods[8:9], ns)
    block_out[...] = gated(h, mods[11:12], nt[...])


def core_swap(a):
    return lax.ppermute(a, "c", CORE)


def half_columns(w, c):
    low = jnp.concatenate([w[:, :QKV], w[:, 3 * D : 3 * D + HALF]], axis=1)
    high = jnp.concatenate([w[:, QKV : 3 * D], w[:, 3 * D + HALF :]], axis=1)
    return jnp.where(c == 0, low, high)


def from_x(own):
    return (
        own,
        lax.ppermute(own[:288], XX, X_UP),
        lax.ppermute(own[288:], XX, X_DOWN),
    )


def after(value, *deps):
    return lax.optimization_barrier((value, *deps))[0]


def shards(latent, spatial_cache, modulation, weights):
    c, xl = lax.axis_index("c"), lax.axis_index("xl")
    flags = jnp.stack([xl, c]).astype(jnp.int32)
    mods = modulation.reshape(12, D)
    w1 = lax.all_gather(half_columns(weights[1], c), "z", axis=0, tiled=True)
    w0 = lax.all_gather(half_columns(weights[0], c), "z", axis=0, tiled=True)

    h1, modin = call(first_kernel, "first", (sds(TOK, D), sds(16, 16, D)), [VMEM] * 3, nbytes=2**21)(
        latent.reshape(TOK, D), spatial_cache.reshape(TOK, D), mods
    )
    modin = lax.all_to_all(modin, TM, 0, 0, tiled=True).reshape(TOK, D)
    modin_other = core_swap(modin)

    scratch = [pltpu.VMEM((D, QKV), BF), pltpu.VMEM((QKV, 512), F32)]
    w1_qkv = from_x(w1[:, :QKV])
    w1_out = from_x(after(w1[:, QKV:], *w1_qkv[1:]))
    w1_out_partner = tuple(core_swap(w) for w in w1_out)
    a_own, a_other = call(
        temporal_kernel,
        "temporal",
        (sds(8, HD, TOK), sds(8, HD, TOK)),
        [SMEM] + [VMEM] * 5,
        scratch,
        flops=2 * 2**30,
        nbytes=6 * 2**20,
        trans=2**20,
    )(flags, modin, modin_other, *w1_qkv)
    a_rec = core_swap(a_other)
    nt = call(
        temporal_out_kernel,
        "temporal_out",
        sds(TOK, D),
        [SMEM] + [VMEM] * 8,
        flops=2**30,
        nbytes=4 * 2**20,
    )(flags, a_own.reshape(HALF, TOK), a_rec.reshape(HALF, TOK), *w1_out, *w1_out_partner)
    w0 = after(w0, nt)
    w0_qkv = from_x(w0[:, :QKV])
    w0_out = from_x(after(w0[:, QKV:], *w0_qkv[1:]))
    w0_out_partner = tuple(core_swap(w) for w in w0_out)

    chunks = lax.all_to_all(nt.reshape(16, 16, D), TM, 0, 0, tiled=True)
    nt, h2, modin = call(
        middle_kernel, "middle", (sds(TOK, D), sds(TOK, D), sds(TOK, D)), [VMEM] * 3, nbytes=2**21
    )(h1, chunks, mods)
    modin_other = core_swap(modin)
    packed = call(
        spatial_qkv_kernel,
        "spatial_qkv",
        sds(8, 3, HD, 512),
        [SMEM] + [VMEM] * 5,
        scratch,
        flops=2 * 2**30,
        nbytes=6 * 2**20,
    )(flags, modin, modin_other, *w0_qkv)
    packed = lax.all_to_all(packed, ("xh", "y"), 0, 0, tiled=True)
    attn = spatial_attend(packed)
    attn = lax.all_to_all(attn, ("xh", "y"), 0, 0, tiled=True).reshape(HALF, 512)
    a_rec = core_swap(attn[:, TOK:])
    block_out, ns = call(
        last_kernel,
        "last",
        (sds(TOK, D), sds(TOK, D)),
        [SMEM] + [VMEM] * 11,
        flops=2**30,
        nbytes=6 * 2**20,
    )(flags, attn[:, :TOK], a_rec, *w0_out, *w0_out_partner, h2, nt, mods)
    whole = (2, 1, 128, D)
    return block_out.reshape(whole), ns.reshape(whole), nt.reshape(whole)


def solution(mesh):
    fine = Mesh(mesh.devices.reshape(2, 8, 2, 4, 2), ("xl", "z", "xh", "y", "c"))
    tokens = P(None, TM, SPACE, None)
    return jax.shard_map(
        shards,
        mesh=fine,
        in_specs=(tokens, tokens, P(), P(None, TM, None)),
        out_specs=(tokens, tokens, tokens),
        check_vma=False,
    )
```

time: 426 us -> 243 us (0.57)
  blocking collectives: 88 us -> 0 us
  waiting for transfers between devices: 198 us -> 116 us
  local copies, waits for them, and re-layouts: 79 us -> 19.4 us
  starting transfers between devices: 11.6 us -> 55.8 us
  Pallas kernels: 0 us -> 35.2 us
  matrix products: 29.4 us -> 0 us
    all_gather x2, waiting for transfers between devices: 172 us -> 41.9 us  [the longest x1 41.9 us: shards(): w1 = lax.all_gather(half_columns(weights[1], c), 'z', axis=0, tiled=True)]
    all_to_all x2 -> x0, blocking collectives: 88 us -> none  [the longest x1 65.3 us: shards(): lax.all_to_all(packed, 'tm', split_axis=2, concat_axis=1, tiled=True)]
    ppermute x0 -> x18, waiting for transfers between devices: none -> 43.7 us  [the longest x4 38.8 us: from_x(): lax.ppermute(own[:288], XX, X_UP)]
    dot_general x4 -> x0, local copies, waits for them, and re-layouts: 37 us -> none  [project_all(): jnp.dot(modin.reshape(-1, shape[-1]), weight[:, :3 * D], preferred_elemen...]
    pallas_call x0 -> x7, Pallas kernels: none -> 35.2 us  [the longest x1 12.8 us: spatial_attend(): pl.pallas_call(spatial_kernel, name='spatial_attend', grid=(8,), out_shap...]
    dot_general x10 -> x0, matrix products: 29.4 us -> none  [the longest x3 8.52 us: attend(): jnp.einsum('nhlm,nmhd->nlhd', probs, split[..., 2, :], preferred_element_...]
    ppermute x0 -> x18, starting transfers between devices: none -> 28.1 us  [the longest x10 16.7 us: core_swap(): return lax.ppermute(a, 'c', CORE)]
    all_to_all x2 -> x4, starting transfers between devices: 11.5 us -> 27.7 us  [the longest x1 10 us: shards(): modin = lax.all_to_all(modin, TM, 0, 0, tiled=True).reshape(TOK, D)]
  transfers between devices with their start and end apart: 4 -> 24, of which waited for: 3 -> 10; matrix products, arithmetic and copies ran while one was open for 18% -> 7% of each run, Pallas kernels for 0% -> 5%
where the time goes in v1:
time: 243 us
  waiting for transfers between devices  116 us (48%)
  starting transfers between devices  55.8 us (23%)
  Pallas kernels  35.2 us (14%)
  local copies, waits for them, and re-layouts  19.4 us (8%)
  between operations  14.3 us (6%)
    all_gather x1, waiting for transfers between devices, shards(): w1 = lax.all_gather(half_columns(weights[1], c), 'z', axis=0, tiled=True)  41.9 us
    ppermute x4, waiting for transfers between devices, from_x(): lax.ppermute(own[:288], XX, X_UP)  38.8 us
    all_to_all x1, waiting for transfers between devices, shards(): packed = lax.all_to_all(packed, ('xh', 'y'), 0, 0, tiled=True)  21.1 us
    ppermute x10, starting transfers between devices, core_swap(): return lax.ppermute(a, 'c', CORE)  16.7 us
    pallas_call x1, Pallas kernels, spatial_attend(): pl.pallas_call(spatial_kernel, name='spatial_attend', grid=(8,), out_shap...  12.8 us
    all_to_all x1, starting transfers between devices, shards(): modin = lax.all_to_all(modin, TM, 0, 0, tiled=True).reshape(TOK, D)  10 us
    all_to_all x1, waiting for transfers between devices, shards(): chunks = lax.all_to_all(nt.reshape(16, 16, D), TM, 0, 0, tiled=True)  9.4 us
    ppermute x4, starting transfers between devices, from_x(): lax.ppermute(own[288:], XX, X_DOWN)  8.35 us
  transfers between devices with their start and end apart: 24, of which 10 were waited for; matrix products, arithmetic and copies ran while one was open for 7% of the time, Pallas kernels for 5%

profile of v1, /device:TPU:1, one launch (start us, length us, event | category | flops | bytes accessed | tf_op | source)
XLA Modules:
  0.0 242.6 jit_solution(603119225814412745)
XLA Ops:
  7.2 1.4 slice_bitcast_fusion
  9.0 0.9 maximum_select_fusion
  10.0 0.9 maximum_select_fusion.1
  10.9 0.6 first.1
  11.6 0.8 copy-done.4
  12.4 10.0 %all-to-all-start = ((bf16[16,16,1152]{2,1,0:T(8,128)(2,1)}), bf16[16,16,1152]{2,1,0:T(8,128)(2,1)S(1)}, u32[]{:S(2)}, u32[]{:S(2)}) async-start(bf16[16,16,1152]{2,1,0:T(8,128)(2,1)} %copy-done.4), calls=%async_computation | async-start | bytes 1179648 | tf_op jit(solution)/shard_map/all_to_all | solution.py:236
  22.5 41.9 %all-gather.3.cloned.1.call-done = bf16[576,2304]{1,0:T(8,128)(2,1)} async-done(((bf16[72,2304]{1,0:T(8,128)(2,1)}), bf16[576,2304]{1,0:T(8,128)(2,1)}) %all-gather.3.cloned.1.call-update) | async-done | bytes 2654224 | tf_op jit(solution)/shard_map/all_gather | solution.py:230
  64.4 3.0 %fusion.1 = (bf16[288,1728]{1,0:T(8,128)(2,1)}, bf16[288,1728]{1,0:T(8,128)(2,1)}) fusion(bf16[576,2304]{1,0:T(8,128)(2,1)} %all-gather.3.cloned.1.call-done), kind=kLoop, calls=%fused_computation.6 | loop fusion | bytes 3981312 | tf_op jit(solution)/shard_map/slice | solution.py:218
  67.4 1.1 collective-permute-start.1
  68.5 1.6 collective-permute-start.2
  70.1 3.3 %collective-permute-start = (bf16[256,1152]{1,0:T(8,128)(2,1)S(1)}, bf16[256,1152]{1,0:T(8,128)(2,1)}, u32[]{:S(2)}, u32[]{:S(2)}) collective-permute-start(bf16[256,1152]{1,0:T(8,128)(2,1)S(1)} %bitcast.25), channel_id=1, source_target_pairs={{0,1},{1,0},{2,3},{3,2},{4,5},{5,4},{6,7},{7,6},{8,9},{9,8},{10,11... | collective-permute-start | bytes 1769480 | tf_op jit(solution)/shard_map/ppermute | solution.py:205
  73.3 1.5 slice.107.m0
  74.8 15.7 %collective-permute-done.1.w_a = bf16[288,1728]{1,0:T(8,128)(2,1)} collective-permute-done((bf16[288,1728]{1,0:T(8,128)(2,1)}, bf16[288,1728]{1,0:T(8,128)(2,1)}, u32[]{:S(2)}, u32[]{:S(2)}) %collective-permute-start.1) | collective-permute-done | bytes 995360 | tf_op jit(solution)/shard_map/ppermute | solution.py:217
  90.5 0.9 fusion.3
  91.5 0.4 collective-permute-start.4
  91.9 2.2 collective-permute-start.5
  94.1 4.2 %collective-permute-start.6 = (bf16[576,576]{1,0:T(8,128)(2,1)S(1)}, bf16[576,576]{1,0:T(8,128)(2,1)S(1)}, u32[]{:S(2)}, u32[]{:S(2)}) collective-permute-start(bf16[576,576]{1,0:T(8,128)(2,1)S(1)} %slice.107.m0), channel_id=1, source_target_pairs={{0,1},{1,0},{2,3},{3,2},{4,5},{5,4},{6,7},{7,6},{8,9},{9,8},{10,11... | collective-permute-start | bytes 1990664 | tf_op jit(solution)/shard_map/ppermute | solution.py:205
  98.4 1.7 slice.104.w_own
  100.1 3.9 %collective-permute-start.7 = (bf16[288,576]{1,0:T(8,128)(2,1)S(1)}, bf16[288,576]{1,0:T(8,128)(2,1)S(1)}, u32[]{:S(2)}, u32[]{:S(2)}) collective-permute-start(bf16[288,576]{1,0:T(8,128)(2,1)S(1)} %collective-permute-done.4.m1), channel_id=1, source_target_pairs={{0,1},{1,0},{2,3},{3,2},{4,5},{5,4},{6,7},{7,6},{8,9},{9,8},{10,11... | collective-permute-start | bytes 995336 | tf_op jit(solution)/shard_map/ppermute | solution.py:205
  104.0 7.8 %temporal.1 = (bf16[8,72,256]{2,1,0:T(8,128)(2,1)S(1)}, bf16[8,72,256]{2,1,0:T(8,128)(2,1)S(1)}) custom-call(s32[2]{0:T(128)S(1)} %pad_add_fusion.flags, bf16[256,1152]{1,0:T(8,128)(2,1)S(1)} %bitcast.26, bf16[256,1152]{1,0:T(8,128)(2,1)} %collective-permute-done.x_other, bf16[576,1728]{1,0:T(8,128)(2,1)S(1)} %slice.104.w_own, ...), custom_call_target="tpu_custom_call" | custom-call | flops 2147483648 | bytes 6291456 | tf_op jit(solution)/shard_map/temporal/pallas_call | solution.py:243
  111.8 0.6 collective-permute-start.3
  112.5 1.2 collective-permute-done.3
  113.7 2.7 %temporal_out.1 = bf16[256,1152]{1,0:T(8,128)(2,1)} custom-call(s32[2]{0:T(128)S(1)} %pad_add_fusion.flags, bf16[576,256]{1,0:T(8,128)(2,1)S(1)} %bitcast.27, bf16[576,256]{1,0:T(8,128)(2,1)S(1)} %bitcast.28, bf16[576,576]{1,0:T(8,128)(2,1)S(1)} %slice.107.m0, bf16[288,576]{1,0:T(8,128)(2,1)S(1)} %collective-permute-done.4.m1, ...), custom_call_target="tpu_custom_call" | custom-call | flops 1073741824 | bytes 4194304 | tf_op jit(solution)/shard_map/temporal_out/pallas_call | solution.py:254
  116.3 5.0 %all-to-all-start.1 = ((bf16[16,16,1152]{2,1,0:T(8,128)(2,1)}), bf16[16,16,1152]{2,1,0:T(8,128)(2,1)S(1)}, u32[]{:S(2)}, u32[]{:S(2)}) async-start(bf16[16,16,1152]{2,1,0:T(8,128)(2,1)} %bitcast.8), calls=%async_computation.1 | async-start | bytes 1179648 | tf_op jit(solution)/shard_map/all_to_all | solution.py:267
  121.4 3.0 %fusion = (bf16[288,1728]{1,0:T(8,128)(2,1)}, bf16[288,1728]{1,0:T(8,128)(2,1)}) fusion(bf16[576,2304]{1,0:T(8,128)(2,1)} %all-gather.5.cloned.1.call-done), kind=kLoop, calls=%fused_computation.5 | loop fusion | bytes 3981312 | tf_op jit(solution)/shard_map/slice | solution.py:218
  124.4 1.4 collective-permute-start.10
  125.8 1.9 collective-permute-start.11
  127.6 9.4 %all-to-all-done.1.chunks = bf16[16,16,1152]{2,1,0:T(8,128)(2,1)S(1)} async-done(((bf16[16,16,1152]{2,1,0:T(8,128)(2,1)}), bf16[16,16,1152]{2,1,0:T(8,128)(2,1)S(1)}, u32[]{:S(2)}, u32[]{:S(2)}) %all-to-all-start.1) | async-done | bytes 589856 | tf_op jit(solution)/shard_map/all_to_all | solution.py:267
  137.0 1.1 middle.1
  138.2 1.9 collective-permute-start.9
  140.1 3.1 %slice.92.w_own = bf16[576,1728]{1,0:T(8,128)(2,1)} slice(bf16[576,2304]{1,0:T(8,128)(2,1)} %all-gather.5.cloned.1.call-done), slice={[0:576], [0:1728]} | slice | bytes 3981312 | tf_op jit(solution)/shard_map/slice | solution.py:263
  143.2 9.5 %collective-permute-done.10.w_a = bf16[288,1728]{1,0:T(8,128)(2,1)} collective-permute-done((bf16[288,1728]{1,0:T(8,128)(2,1)}, bf16[288,1728]{1,0:T(8,128)(2,1)}, u32[]{:S(2)}, u32[]{:S(2)}) %collective-permute-start.10) | collective-permute-done | bytes 995360 | tf_op jit(solution)/shard_map/ppermute | solution.py:217
  152.7 2.4 collective-permute-done.11.w_b
  155.1 6.6 %spatial_qkv.1 = bf16[8,3,72,512]{3,2,1,0:T(8,128)(2,1)} custom-call(s32[2]{0:T(128)S(1)} %pad_add_fusion.flags, bf16[256,1152]{1,0:T(8,128)(2,1)S(1)} %get-tuple-element.20.x_own, bf16[256,1152]{1,0:T(8,128)(2,1)S(1)} %collective-permute-done.9.x_other, bf16[576,1728]{1,0:T(8,128)(2,1)} %slice.92.w_own, bf16[288,1728]{1,0:T(8,128)(2,1)} %collective-permute-done.10.w_a, ...), custom_call_target="tpu_custom_call" | custom-call | flops 2147483648 | bytes 6291456 | tf_op jit(solution)/shard_map/spatial_qkv/pallas_call | solution.py:272
  161.7 7.3 %all-to-all-start.2 = ((bf16[8,3,72,512]{3,2,1,0:T(8,128)(2,1)}), bf16[8,3,72,512]{3,2,1,0:T(8,128)(2,1)S(1)}, u32[]{:S(2)}, u32[]{:S(2)}) async-start(bf16[8,3,72,512]{3,2,1,0:T(8,128)(2,1)} %spatial_qkv.1), calls=%async_computation.2 | async-start | bytes 3538944 | tf_op jit(solution)/shard_map/all_to_all | solution.py:281
  169.0 1.5 slice.97.m0
  170.5 21.1 %all-to-all-done.2.q_ref.all_ref = bf16[8,3,72,512]{3,2,1,0:T(8,128)(2,1)S(1)} async-done(((bf16[8,3,72,512]{3,2,1,0:T(8,128)(2,1)}), bf16[8,3,72,512]{3,2,1,0:T(8,128)(2,1)S(1)}, u32[]{:S(2)}, u32[]{:S(2)}) %all-to-all-start.2) | async-done | bytes 1769504 | tf_op jit(solution)/shard_map/all_to_all | solution.py:281
  191.6 12.8 %spatial_attend.1 = bf16[8,72,512]{2,1,0:T(8,128)(2,1)S(1)} custom-call(bf16[8,3,72,512]{3,2,1,0:T(8,128)(2,1)S(1)} %all-to-all-done.2.q_ref.all_ref, bf16[8,3,72,512]{3,2,1,0:T(8,128)(2,1)S(1)} %all-to-all-done.2.q_ref.all_ref), custom_call_target="tpu_custom_call" | custom-call | flops 34359738368 | bytes 3145728 | tf_op jit(solution)/shard_map/spatial_attend/pallas_call | solution.py:162
  204.4 0.8 copy-done.3
  205.2 5.4 %all-to-all-start.3 = ((bf16[8,72,512]{2,1,0:T(8,128)(2,1)}), bf16[8,72,512]{2,1,0:T(8,128)(2,1)}, u32[]{:S(2)}, u32[]{:S(2)}) async-start(bf16[8,72,512]{2,1,0:T(8,128)(2,1)} %copy-done.3), calls=%async_computation.3 | async-start | bytes 1179648 | tf_op jit(solution)/shard_map/all_to_all | solution.py:283
  210.8 2.7 %collective-permute-start.14 = (bf16[288,576]{1,0:T(8,128)(2,1)S(1)}, bf16[288,576]{1,0:T(8,128)(2,1)S(1)}, u32[]{:S(2)}, u32[]{:S(2)}) collective-permute-start(bf16[288,576]{1,0:T(8,128)(2,1)S(1)} %get-tuple-element.39), channel_id=1, source_target_pairs={{0,136},{128,0},{8,128},{136,8},{1,137},{129,1},{9,129},{137,9},{2... | collective-permute-start | bytes 995336 | tf_op jit(solution)/shard_map/ppermute | solution.py:218
  213.4 1.3 collective-permute-start.15
  214.8 13.6 %collective-permute-done.13.m1 = bf16[288,576]{1,0:T(8,128)(2,1)S(1)} collective-permute-done((bf16[288,576]{1,0:T(8,128)(2,1)S(1)}, bf16[288,576]{1,0:T(8,128)(2,1)S(1)}, u32[]{:S(2)}, u32[]{:S(2)}) %collective-permute-start.13) | collective-permute-done | bytes 331808 | tf_op jit(solution)/shard_map/ppermute | solution.py:217
  228.4 0.9 collective-permute-start.16
  229.3 1.1 fusion.8
  230.4 0.6 collective-permute-start.12
  231.2 0.9 collective-permute-done.12.a_rec
  232.2 3.6 %last.1 = (bf16[256,1152]{1,0:T(8,128)(2,1)}, bf16[256,1152]{1,0:T(8,128)(2,1)}) custom-call(s32[2]{0:T(128)S(1)} %pad_add_fusion.flags, bf16[576,256]{1,0:T(8,128)(2,1)S(1)} %get-tuple-element.52.a_own, bf16[576,256]{1,0:T(8,128)(2,1)S(1)} %collective-permute-done.12.a_rec, bf16[576,576]{1,0:T(8,128)(2,1)S(1)} %slice.97.m0, ...), custom_call_target="tpu_custom_call" | custom-call | flops 1073741824 | bytes 6291456 | tf_op jit(solution)/shard_map/last/pallas_call | solution.py:285
  (38 shorter events, 1.1 us)
Async XLA Ops:
  7.2 57.2 %all-gather.3.cloned.1.call-start = ((), (), s32[]{:S(2)}) async-start(), calls=%async_computation.4 | async-start | bytes 2985984 | tf_op jit(solution)/shard_map/all_gather | solution.py:230
  8.7 2.1 copy-start.5
  8.7 2.2 copy-start.1
  8.7 2.2 copy-start.2
  9.9 111.4 %all-gather.5.cloned.1.call-start = ((), (), s32[]{:S(2)}) async-start(), calls=%async_computation.5 | async-start | bytes 2985984 | tf_op jit(solution)/shard_map/all_gather | solution.py:231
  11.6 0.8 copy-start.4
  12.4 57.7 %all-to-all-start = ((bf16[16,16,1152]{2,1,0:T(8,128)(2,1)}), bf16[16,16,1152]{2,1,0:T(8,128)(2,1)S(1)}, u32[]{:S(2)}, u32[]{:S(2)}) async-start(bf16[16,16,1152]{2,1,0:T(8,128)(2,1)} %copy-done.4), calls=%async_computation | async-start | bytes 1179648 | tf_op jit(solution)/shard_map/all_to_all | solution.py:236
  67.4 23.1 %collective-permute-start.1 = (bf16[288,1728]{1,0:T(8,128)(2,1)}, bf16[288,1728]{1,0:T(8,128)(2,1)}, u32[]{:S(2)}, u32[]{:S(2)}) collective-permute-start(bf16[288,1728]{1,0:T(8,128)(2,1)} %get-tuple-element.36), channel_id=1, source_target_pairs={{0,128},{128,8},{8,136},{136,0},{1,129},{129,9},{9,137},{137,1},{2... | collective-permute-start | bytes 2985992 | tf_op jit(solution)/shard_map/ppermute | solution.py:217
  68.5 22.0 %collective-permute-start.2 = (bf16[288,1728]{1,0:T(8,128)(2,1)}, bf16[288,1728]{1,0:T(8,128)(2,1)}, u32[]{:S(2)}, u32[]{:S(2)}) collective-permute-start(bf16[288,1728]{1,0:T(8,128)(2,1)} %get-tuple-element.35), channel_id=1, source_target_pairs={{0,136},{128,0},{8,128},{136,8},{1,137},{129,1},{9,129},{137,9},{2... | collective-permute-start | bytes 2985992 | tf_op jit(solution)/shard_map/ppermute | solution.py:218
  70.1 33.9 %collective-permute-start = (bf16[256,1152]{1,0:T(8,128)(2,1)S(1)}, bf16[256,1152]{1,0:T(8,128)(2,1)}, u32[]{:S(2)}, u32[]{:S(2)}) collective-permute-start(bf16[256,1152]{1,0:T(8,128)(2,1)S(1)} %bitcast.25), channel_id=1, source_target_pairs={{0,1},{1,0},{2,3},{3,2},{4,5},{5,4},{6,7},{7,6},{8,9},{9,8},{10,11... | collective-permute-start | bytes 1769480 | tf_op jit(solution)/shard_map/ppermute | solution.py:205
  91.5 8.7 %collective-permute-start.4 = (bf16[288,576]{1,0:T(8,128)(2,1)}, bf16[288,576]{1,0:T(8,128)(2,1)S(1)}, u32[]{:S(2)}, u32[]{:S(2)}) collective-permute-start(bf16[288,576]{1,0:T(8,128)(2,1)} %get-tuple-element.42), channel_id=1, source_target_pairs={{0,128},{128,8},{8,136},{136,0},{1,129},{129,9},{9,137},{137,1},{2... | collective-permute-start | bytes 995336 | tf_op jit(solution)/shard_map/ppermute | solution.py:217
  91.9 12.1 %collective-permute-start.5 = (bf16[288,576]{1,0:T(8,128)(2,1)}, bf16[288,576]{1,0:T(8,128)(2,1)S(1)}, u32[]{:S(2)}, u32[]{:S(2)}) collective-permute-start(bf16[288,576]{1,0:T(8,128)(2,1)} %get-tuple-element.41), channel_id=1, source_target_pairs={{0,136},{128,0},{8,128},{136,8},{1,137},{129,1},{9,129},{137,9},{2... | collective-permute-start | bytes 995336 | tf_op jit(solution)/shard_map/ppermute | solution.py:218
  94.1 19.5 %collective-permute-start.6 = (bf16[576,576]{1,0:T(8,128)(2,1)S(1)}, bf16[576,576]{1,0:T(8,128)(2,1)S(1)}, u32[]{:S(2)}, u32[]{:S(2)}) collective-permute-start(bf16[576,576]{1,0:T(8,128)(2,1)S(1)} %slice.107.m0), channel_id=1, source_target_pairs={{0,1},{1,0},{2,3},{3,2},{4,5},{5,4},{6,7},{7,6},{8,9},{9,8},{10,11... | collective-permute-start | bytes 1990664 | tf_op jit(solution)/shard_map/ppermute | solution.py:205
  100.1 13.5 %collective-permute-start.7 = (bf16[288,576]{1,0:T(8,128)(2,1)S(1)}, bf16[288,576]{1,0:T(8,128)(2,1)S(1)}, u32[]{:S(2)}, u32[]{:S(2)}) collective-permute-start(bf16[288,576]{1,0:T(8,128)(2,1)S(1)} %collective-permute-done.4.m1), channel_id=1, source_target_pairs={{0,1},{1,0},{2,3},{3,2},{4,5},{5,4},{6,7},{7,6},{8,9},{9,8},{10,11... | collective-permute-start | bytes 995336 | tf_op jit(solution)/shard_map/ppermute | solution.py:205
  104.0 9.6 %collective-permute-start.8 = (bf16[288,576]{1,0:T(8,128)(2,1)S(1)}, bf16[288,576]{1,0:T(8,128)(2,1)S(1)}, u32[]{:S(2)}, u32[]{:S(2)}) collective-permute-start(bf16[288,576]{1,0:T(8,128)(2,1)S(1)} %collective-permute-done.5.m2), channel_id=1, source_target_pairs={{0,1},{1,0},{2,3},{3,2},{4,5},{5,4},{6,7},{7,6},{8,9},{9,8},{10,11... | collective-permute-start | bytes 995336 | tf_op jit(solution)/shard_map/ppermute | solution.py:205
  111.8 1.8 collective-permute-start.3
  116.3 20.7 %all-to-all-start.1 = ((bf16[16,16,1152]{2,1,0:T(8,128)(2,1)}), bf16[16,16,1152]{2,1,0:T(8,128)(2,1)S(1)}, u32[]{:S(2)}, u32[]{:S(2)}) async-start(bf16[16,16,1152]{2,1,0:T(8,128)(2,1)} %bitcast.8), calls=%async_computation.1 | async-start | bytes 1179648 | tf_op jit(solution)/shard_map/all_to_all | solution.py:267
  124.4 28.3 %collective-permute-start.10 = (bf16[288,1728]{1,0:T(8,128)(2,1)}, bf16[288,1728]{1,0:T(8,128)(2,1)}, u32[]{:S(2)}, u32[]{:S(2)}) collective-permute-start(bf16[288,1728]{1,0:T(8,128)(2,1)} %get-tuple-element.34), channel_id=1, source_target_pairs={{0,128},{128,8},{8,136},{136,0},{1,129},{129,9},{9,137},{137,1},{2... | collective-permute-start | bytes 2985992 | tf_op jit(solution)/shard_map/ppermute | solution.py:217
  125.8 29.3 %collective-permute-start.11 = (bf16[288,1728]{1,0:T(8,128)(2,1)}, bf16[288,1728]{1,0:T(8,128)(2,1)}, u32[]{:S(2)}, u32[]{:S(2)}) collective-permute-start(bf16[288,1728]{1,0:T(8,128)(2,1)} %get-tuple-element.33), channel_id=1, source_target_pairs={{0,136},{128,0},{8,128},{136,8},{1,137},{129,1},{9,129},{137,9},{2... | collective-permute-start | bytes 2985992 | tf_op jit(solution)/shard_map/ppermute | solution.py:218
  138.2 16.9 %collective-permute-start.9 = (bf16[256,1152]{1,0:T(8,128)(2,1)S(1)}, bf16[256,1152]{1,0:T(8,128)(2,1)S(1)}, u32[]{:S(2)}, u32[]{:S(2)}) collective-permute-start(bf16[256,1152]{1,0:T(8,128)(2,1)S(1)} %get-tuple-element.20.x_own), channel_id=1, source_target_pairs={{0,1},{1,0},{2,3},{3,2},{4,5},{5,4},{6,7},{7,6},{8,9},{9,8},{10,11... | collective-permute-start | bytes 1769480 | tf_op jit(solution)/shard_map/ppermute | solution.py:205
  161.7 29.9 %all-to-all-start.2 = ((bf16[8,3,72,512]{3,2,1,0:T(8,128)(2,1)}), bf16[8,3,72,512]{3,2,1,0:T(8,128)(2,1)S(1)}, u32[]{:S(2)}, u32[]{:S(2)}) async-start(bf16[8,3,72,512]{3,2,1,0:T(8,128)(2,1)} %spatial_qkv.1), calls=%async_computation.2 | async-start | bytes 3538944 | tf_op jit(solution)/shard_map/all_to_all | solution.py:281
  204.4 0.8 copy-start.3
  205.2 26.9 %copy-start = (bf16[256,1152]{1,0:T(8,128)(2,1)S(1)}, bf16[256,1152]{1,0:T(8,128)(2,1)}, u32[]{:S(2)}) copy-start(bf16[256,1152]{1,0:T(8,128)(2,1)} %get-tuple-element.24.nt) | copy-start | bytes 1769476
  205.2 24.0 %all-to-all-start.3 = ((bf16[8,72,512]{2,1,0:T(8,128)(2,1)}), bf16[8,72,512]{2,1,0:T(8,128)(2,1)}, u32[]{:S(2)}, u32[]{:S(2)}) async-start(bf16[8,72,512]{2,1,0:T(8,128)(2,1)} %copy-done.3), calls=%async_computation.3 | async-start | bytes 1179648 | tf_op jit(solution)/shard_map/all_to_all | solution.py:283
  210.7 17.7 %collective-permute-start.13 = (bf16[288,576]{1,0:T(8,128)(2,1)S(1)}, bf16[288,576]{1,0:T(8,128)(2,1)S(1)}, u32[]{:S(2)}, u32[]{:S(2)}) collective-permute-start(bf16[288,576]{1,0:T(8,128)(2,1)S(1)} %get-tuple-element.40), channel_id=1, source_target_pairs={{0,128},{128,8},{8,136},{136,0},{1,129},{129,9},{9,137},{137,1},{2... | collective-permute-start | bytes 995336 | tf_op jit(solution)/shard_map/ppermute | solution.py:217
  210.8 18.5 %collective-permute-start.14 = (bf16[288,576]{1,0:T(8,128)(2,1)S(1)}, bf16[288,576]{1,0:T(8,128)(2,1)S(1)}, u32[]{:S(2)}, u32[]{:S(2)}) collective-permute-start(bf16[288,576]{1,0:T(8,128)(2,1)S(1)} %get-tuple-element.39), channel_id=1, source_target_pairs={{0,136},{128,0},{8,128},{136,8},{1,137},{129,1},{9,129},{137,9},{2... | collective-permute-start | bytes 995336 | tf_op jit(solution)/shard_map/ppermute | solution.py:218
  213.4 17.6 %collective-permute-start.15 = (bf16[576,576]{1,0:T(8,128)(2,1)S(1)}, bf16[576,576]{1,0:T(8,128)(2,1)S(1)}, u32[]{:S(2)}, u32[]{:S(2)}) collective-permute-start(bf16[576,576]{1,0:T(8,128)(2,1)S(1)} %slice.97.m0), channel_id=1, source_target_pairs={{0,1},{1,0},{2,3},{3,2},{4,5},{5,4},{6,7},{7,6},{8,9},{9,8},{10,11... | collective-permute-start | bytes 1990664 | tf_op jit(solution)/shard_map/ppermute | solution.py:205
  228.4 2.6 %collective-permute-start.16 = (bf16[288,576]{1,0:T(8,128)(2,1)S(1)}, bf16[288,576]{1,0:T(8,128)(2,1)}, u32[]{:S(2)}, u32[]{:S(2)}) collective-permute-start(bf16[288,576]{1,0:T(8,128)(2,1)S(1)} %collective-permute-done.13.m1), channel_id=1, source_target_pairs={{0,1},{1,0},{2,3},{3,2},{4,5},{5,4},{6,7},{7,6},{8,9},{9,8},{10,11... | collective-permute-start | bytes 995336 | tf_op jit(solution)/shard_map/ppermute | solution.py:205
  229.3 2.0 collective-permute-start.17
  230.4 1.8 collective-permute-start.12
Sparse Core Ops, SparseCore 0:
  10.4 53.9 all-gather.2
  66.7 39.8 all-gather.4

commit v2 on v1

v2 whole, which is shorter than its diff:
```python
import math

import jax
import jax.numpy as jnp
from jax import lax
from jax.experimental import pallas as pl
from jax.experimental.pallas import tpu as pltpu
from jax.sharding import Mesh, PartitionSpec as P

D = 1152
HD = 72
HALF = D // 2
QKV = 3 * HALF
WIDE = QKV // 2
PAD = 896
BOTH = 1536
TOK = 256
SCALE = math.log2(math.e) / math.sqrt(HD)
TM = ("xl", "z")
SPACE = ("xh", "y", "c")
XX = ("xl", "xh")
BF = jnp.bfloat16
F32 = jnp.float32
VMEM = pl.BlockSpec(memory_space=pltpu.VMEM)
SMEM = pl.BlockSpec(memory_space=pltpu.SMEM)


def x_pairs(step):
    place = lambda x: (x % 2) * 2 + x // 2
    return [(place(x), place((x + step) % 4)) for x in range(4)]


CORE = [(0, 1), (1, 0)]
Y_UP = [(i, (i + 1) % 4) for i in range(4)]
Y_DOWN = [(i, (i - 1) % 4) for i in range(4)]
X_UP, X_DOWN = x_pairs(1), x_pairs(-1)


def call(body, name, outs, ins, scratch=(), flops=0, nbytes=0, trans=0):
    return pl.pallas_call(
        body,
        name=name,
        out_shape=outs,
        in_specs=ins,
        out_specs=jax.tree.map(lambda _: VMEM, outs),
        scratch_shapes=scratch,
        cost_estimate=pl.CostEstimate(flops=flops, bytes_accessed=nbytes, transcendentals=trans),
        compiler_params=pltpu.CompilerParams(vmem_limit_bytes=24 * 2**20),
    )


def sds(*shape, dtype=BF):
    return jax.ShapeDtypeStruct(shape, dtype)


def normed(h, scale, shift):
    x = h.astype(F32)
    mean = jnp.mean(x, axis=-1, keepdims=True)
    x = x - mean
    var = jnp.mean(x * x, axis=-1, keepdims=True)
    return (x * lax.rsqrt(var + 1e-06) * (1.0 + scale) + shift).astype(BF)


def gated(h, gate, branch):
    return (h.astype(F32) + gate * branch.astype(F32)).astype(BF)


def prepare_kernel(flags, w, first_out, second_out, third_out):
    c, color = flags[1], flags[2]

    def choose(layer, start, width, count, index):
        part = w[layer, :, start : start + width]
        for i in range(1, count):
            part = jnp.where(index == i, w[layer, :, start + i * width : start + (i + 1) * width], part)
        return part

    first_out[...] = choose(1, 0, QKV, 2, c)
    second_out[:, :WIDE] = choose(0, 0, WIDE, 4, 2 * c + color)
    second_out[:, WIDE:PAD] = jnp.zeros((HD, PAD - WIDE), BF)
    second_out[:, PAD : PAD + HALF] = choose(1, 3 * D, HALF, 2, c)
    second_out[:, PAD + HALF :] = jnp.zeros((HD, BOTH - PAD - HALF), BF)
    third_out[...] = w[0, :, 3 * D :]


def first_kernel(lat, cache, mods, h_out, modin_out):
    h = gated(lat[...], mods[2:3], cache[...])
    h_out[...] = h
    modin = normed(h, mods[4:5], mods[3:4]).astype(F32)
    by_dest = jnp.transpose(modin.reshape(2, 16, 8, D), (1, 0, 2, 3))
    modin_out[...] = by_dest.reshape(16, 16, D).astype(BF)


def multiply(x, w_all, y_t):
    width = w_all.shape[1]
    for start in range(0, width, 256):
        stop = min(start + 256, width)
        y = jnp.dot(x, w_all[:, start:stop], preferred_element_type=F32)
        y_t[start:stop] = y.T


def own_first(x, flags):
    low, high = x[:, :HALF], x[:, HALF:]
    swap = flags[0] == 1
    return jnp.concatenate([jnp.where(swap, high, low), jnp.where(swap, low, high)], axis=1)


def unit(v, factor):
    mean = jnp.mean(v * v, axis=0, keepdims=True)
    return (v * (lax.rsqrt(mean + 1e-06) * factor)).astype(BF)


def head_qkv(y_t, head):
    base = head * 3 * HD
    return (
        unit(y_t[base : base + HD], SCALE),
        unit(y_t[base + HD : base + 2 * HD], 1.0),
        y_t[base + 2 * HD : base + 3 * HD].astype(BF),
    )


def project(x_own, x_other, gathered, low, high, w_all, y_t):
    x = jnp.concatenate([x_own[...], x_other[...]], axis=0)
    w_all[0, :HALF] = gathered[:, :WIDE]
    w_all[0, HALF:] = gathered[:, BOTH : BOTH + WIDE]
    w_all[1, :HALF] = low[...]
    w_all[1, HALF:] = high[...]
    for group in range(2):
        multiply(x, w_all.at[group], y_t.at[group])


def spatial_qkv_kernel(flags, x_own, x_other, gathered, low, high, out, w_all, y_t):
    project(x_own, x_other, gathered, low, high, w_all, y_t)
    for head in range(8):
        place = 4 * (flags[2] ^ (head // 4)) + head % 4
        q, k, v = head_qkv(y_t.at[head // 4], head % 4)
        out[place, 0] = q
        out[place, 1] = k
        out[place, 2] = v


def attend(k, q, v, mask=None):
    s = lax.dot_general(k, q, (((0,), (0,)), ((), ())), preferred_element_type=F32)
    p = jnp.exp2(s)
    if mask is not None:
        p = jnp.where(mask, p, 0.0)
    total = jnp.sum(p, axis=0, keepdims=True)
    o = jnp.dot(v, p.astype(BF), preferred_element_type=F32)
    return o * (1.0 / total)


def temporal_kernel(flags, x_own, x_other, w_own, w_a, w_b, own_out, other_out, w_all, y_t, o_t):
    w_all[:HALF] = w_own[...]
    w_all[HALF : HALF + 288] = w_a[...]
    w_all[HALF + 288 :] = w_b[...]
    multiply(own_first(jnp.concatenate([x_own[...], x_other[...]], axis=0), flags), w_all, y_t)
    key = lax.broadcasted_iota(jnp.int32, (TOK, TOK), 0)
    query = lax.broadcasted_iota(jnp.int32, (TOK, TOK), 1)
    mask = (key & 15) == (query & 15)
    for head in range(8):
        q, k, v = head_qkv(y_t, head)
        o_t[head, :, :TOK] = attend(k[:, :TOK], q[:, :TOK], v[:, :TOK], mask)
        o_t[head, :, TOK:] = attend(k[:, TOK:], q[:, TOK:], v[:, TOK:], mask)
    o = o_t[...].reshape(HALF, 512)
    own_out[...] = o[:, :TOK].T.astype(BF)
    other_out[...] = o[:, TOK:].T.astype(BF)


def spatial_kernel(q_ref, all_ref, out, keys, values):
    @pl.when(pl.program_id(0) == 0)
    def _():
        for b in range(2):
            for src in range(8):
                for rel in range(2):
                    lanes = slice(rel * 256 + b * 128, rel * 256 + b * 128 + 128)
                    rows = slice(src * 256 + rel * 128, src * 256 + rel * 128 + 128)
                    keys[b, rows] = all_ref[src, 1, :, lanes].astype(F32).T.astype(BF)
                    values[b, :, rows] = all_ref[src, 2, :, lanes]

    places = [(j, b) for j in range(2) for b in range(2)]

    def lanes(b, rel):
        return slice(rel * 256 + b * 128, rel * 256 + b * 128 + 128)

    def scores(j, b):
        q = jnp.concatenate([q_ref[j, 0, :, lanes(b, rel)] for rel in range(2)], axis=1)
        return jnp.dot(keys[b], q, preferred_element_type=F32)

    s = scores(*places[0])
    for i, (j, b) in enumerate(places):
        following = scores(*places[i + 1]) if i < 3 else None
        p = jnp.exp2(s)
        total = jnp.sum(p, axis=0, keepdims=True)
        o = jnp.dot(values[b], p.astype(BF), preferred_element_type=F32)
        o = (o * (1.0 / total)).astype(BF)
        for rel in range(2):
            out[j, :, lanes(b, rel)] = o[:, rel * 128 : rel * 128 + 128]
        s = following


def spatial_attend(packed):
    return pl.pallas_call(
        spatial_kernel,
        name="spatial_attend",
        grid=(4,),
        out_shape=sds(8, HD, 512),
        in_specs=[
            pl.BlockSpec((2, 3, HD, 512), lambda j: (j, 0, 0, 0)),
            pl.BlockSpec((8, 3, HD, 512), lambda j: (0, 0, 0, 0)),
        ],
        out_specs=pl.BlockSpec((2, HD, 512), lambda j: (j, 0, 0)),
        scratch_shapes=[pltpu.VMEM((2, 2048, HD), BF), pltpu.VMEM((2, HD, 2048), BF)],
        cost_estimate=pl.CostEstimate(flops=2**33, bytes_accessed=3 * 2**20, transcendentals=2**23),
        compiler_params=pltpu.CompilerParams(vmem_limit_bytes=24 * 2**20),
    )(packed, packed)


def middle_kernel(flags, h1, chunks, m0, m1, p0, p1, mods, nt_out, h_out, modin_out):
    a = jnp.transpose(chunks[...].astype(F32).reshape(16, 2, 8, D), (1, 0, 2, 3)).reshape(TOK, D).astype(BF)
    low, high = a[:, :HALF], a[:, HALF:]
    first = flags[1] == 0
    a = jnp.concatenate([jnp.where(first, low, high), jnp.where(first, high, low)], axis=1)
    halves = []
    for xl0, xl1 in ((m0, m1), (p0, p1)):
        w = jnp.concatenate([xl0[...], xl1[...]], axis=0)
        halves.append(jnp.dot(a, w, preferred_element_type=F32).astype(BF))
    low = jnp.where(first, halves[0], halves[1])
    high = jnp.where(first, halves[1], halves[0])
    nt = jnp.concatenate([low, high], axis=1)
    nt_out[...] = nt
    h = gated(h1[...], mods[5:6], nt)
    h_out[...] = h
    modin_out[...] = normed(h, mods[7:8], mods[6:7])


def last_kernel(flags, a_own, a_rec, w_own, w_a, w_b, h2, nt, mods, block_out, ns_out):
    same = flags[0] == flags[1]
    mine, received = a_own[...], a_rec[...]
    a = jnp.concatenate([jnp.where(same, mine, received), jnp.where(same, received, mine)], axis=0)
    a = a.astype(F32).T.astype(BF)
    w = jnp.concatenate([w_own[...], w_a[...], w_b[...]], axis=0)
    ns = jnp.dot(a, w, preferred_element_type=F32).astype(BF)
    ns_out[...] = ns
    h = gated(h2[...], mods[8:9], ns)
    block_out[...] = gated(h, mods[11:12], nt[...])


def core_swap(a):
    return lax.ppermute(a, "c", CORE)


def from_x(own):
    return (
        own,
        lax.ppermute(own[:288], XX, X_UP),
        lax.ppermute(own[288:], XX, X_DOWN),
    )


def gather_z(w):
    return lax.all_gather(w, "z", axis=0, tiled=True)


def after(value, *deps):
    return lax.optimization_barrier((value, *deps))[0]


def shards(latent, spatial_cache, modulation, weights):
    c, xl, z = lax.axis_index("c"), lax.axis_index("xl"), lax.axis_index("z")
    color = lax.axis_index("y") % 2
    flags = jnp.stack([xl, c, color]).astype(jnp.int32)
    mods = modulation.reshape(12, D)
    first_w, second_w, third_w = call(
        prepare_kernel,
        "prepare",
        (sds(HD, QKV), sds(HD, BOTH), sds(HD, D)),
        [SMEM, VMEM],
        nbytes=2**21,
    )(flags, weights)
    w1_own = gather_z(first_w)
    partner = lax.ppermute(second_w, "xl", CORE)
    low, high = jnp.where(xl == 0, second_w, partner), jnp.where(xl == 0, partner, second_w)
    second_w = gather_z(jnp.concatenate([low, high], axis=1))
    w0_out = gather_z(third_w)

    h1, modin = call(first_kernel, "first", (sds(TOK, D), sds(16, 16, D)), [VMEM] * 3, nbytes=2**21)(
        latent.reshape(TOK, D), spatial_cache.reshape(TOK, D), mods
    )
    w1_qkv = from_x(w1_own)
    modin = after(modin, w1_own)
    modin = lax.all_to_all(modin, TM, 0, 0, tiled=True).reshape(TOK, D)
    modin_other = core_swap(modin)
    own, other = call(
        temporal_kernel,
        "temporal",
        (sds(TOK, HALF), sds(TOK, HALF)),
        [SMEM] + [VMEM] * 5,
        [pltpu.VMEM((D, QKV), BF), pltpu.VMEM((QKV, 512), F32), pltpu.VMEM((8, HD, 512), F32)],
        flops=2 * 2**30,
        nbytes=6 * 2**20,
        trans=2**20,
    )(flags, modin, modin_other, *w1_qkv)
    attn = jnp.concatenate([own, core_swap(other)], axis=1)
    second_w = after(second_w, attn)
    chunks = lax.all_to_all(attn.reshape(16, 16, D), TM, 0, 0, tiled=True)
    w1_out = second_w[:, PAD : PAD + HALF], second_w[:, BOTH + PAD : BOTH + PAD + HALF]
    w1_partner = tuple(core_swap(w) for w in w1_out)
    far = (
        lax.ppermute(second_w[:, :WIDE], "y", Y_UP),
        lax.ppermute(second_w[:, BOTH : BOTH + WIDE], "y", Y_DOWN),
    )
    nt, h2, modin = call(
        middle_kernel,
        "middle",
        (sds(TOK, D), sds(TOK, D), sds(TOK, D)),
        [SMEM] + [VMEM] * 7,
        flops=2**30,
        nbytes=5 * 2**20,
    )(flags, h1, chunks, *w1_out, *w1_partner, mods)
    modin = after(modin, *far)
    modin_other = core_swap(modin)
    packed = call(
        spatial_qkv_kernel,
        "spatial_qkv",
        sds(8, 3, HD, 512),
        [SMEM] + [VMEM] * 5,
        [pltpu.VMEM((2, D, WIDE), BF), pltpu.VMEM((2, WIDE, 512), F32)],
        flops=2 * 2**30,
        nbytes=6 * 2**20,
    )(flags, modin, modin_other, second_w, *far)
    packed = lax.all_to_all(packed, ("xh", "y"), 0, 0, tiled=True)
    w0_out = from_x(after(w0_out, packed))
    attn = after(spatial_attend(packed), *w0_out)
    attn = lax.all_to_all(attn, ("xh", "y"), 0, 0, tiled=True).reshape(HALF, 512)
    a_rec = core_swap(attn[:, TOK:])
    block_out, ns = call(
        last_kernel,
        "last",
        (sds(TOK, D), sds(TOK, D)),
        [SMEM] + [VMEM] * 8,
        flops=2**30,
        nbytes=6 * 2**20,
    )(flags, attn[:, :TOK], a_rec, *w0_out, h2, nt, mods)
    whole = (2, 1, 128, D)
    return block_out.reshape(whole), ns.reshape(whole), nt.reshape(whole)


def solution(mesh):
    fine = Mesh(mesh.devices.reshape(2, 8, 2, 4, 2), ("xl", "z", "xh", "y", "c"))
    tokens = P(None, TM, SPACE, None)
    return jax.shard_map(
        shards,
        mesh=fine,
        in_specs=(tokens, tokens, P(), P(None, TM, None)),
        out_specs=(tokens, tokens, tokens),
        check_vma=False,
    )
```

time: 243 us -> 221 us (0.909)
  waiting for transfers between devices: 116 us -> 97.1 us
  blocking collectives: 0 us -> 13.5 us
  starting transfers between devices: 55.8 us -> 47.2 us
  Pallas kernels: 35.2 us -> 31.3 us
  local copies, waits for them, and re-layouts: 19.4 us -> 16 us
    ppermute x4 -> x2, waiting for transfers between devices: 38.8 us -> 14.4 us  [from_x(): lax.ppermute(own[:288], XX, X_UP)]
    all_to_all x1, waiting for transfers between devices: 21.1 us -> 1.07 us  [shards(): packed = lax.all_to_all(packed, ('xh', 'y'), 0, 0, tiled=True)]
    all_to_all x0 -> x1, blocking collectives: none -> 13.5 us  [shards(): lax.all_to_all(attn, ('xh', 'y'), 0, 0, tiled=True).reshape(HALF, 512)]
    all_gather x2 -> x3, waiting for transfers between devices: 41.9 us -> 53.7 us  [gather_z(): return lax.all_gather(w, 'z', axis=0, tiled=True)]
    ppermute x0 -> x3, waiting for transfers between devices: none -> 9.3 us  [the longest x1 5.48 us: shards(): lax.ppermute(second_w[:, :WIDE], 'y', Y_UP)]
    unnamed x13 -> x35, local copies, waits for them, and re-layouts: 1.66 us -> 6.87 us
    all_to_all x1, waiting for transfers between devices: 0.01 us -> 5.17 us  [shards(): modin = lax.all_to_all(modin, TM, 0, 0, tiled=True).reshape(TOK, D)]
    all_to_all x2 -> x1, starting transfers between devices: 10.3 us -> 5.23 us  [shards(): chunks = lax.all_to_all(attn.reshape(16, 16, D), TM, 0, 0, tiled=True)]
  transfers between devices with their start and end apart: 24 -> 19, of which waited for: 10 -> 14; matrix products, arithmetic and copies ran while one was open for 7% -> 4% of each run, Pallas kernels for 5% -> 12%
where the time goes in v2:
time: 221 us
  waiting for transfers between devices  97.1 us (44%)
  starting transfers between devices  47.2 us (21%)
  Pallas kernels  31.3 us (14%)
  local copies, waits for them, and re-layouts  16 us (7%)
  between operations  13.9 us (6%)
  blocking collectives  13.5 us (6%)
    all_gather x3, waiting for transfers between devices, gather_z(): return lax.all_gather(w, 'z', axis=0, tiled=True)  53.7 us
    ppermute x6, starting transfers between devices, core_swap(): return lax.ppermute(a, 'c', CORE)  20.3 us
    ppermute x2, waiting for transfers between devices, from_x(): lax.ppermute(own[:288], XX, X_UP)  14.4 us
    all_to_all x1, blocking collectives, shards(): lax.all_to_all(attn, ('xh', 'y'), 0, 0, tiled=True).reshape(HALF, 512)  13.5 us
    pallas_call x1, Pallas kernels, spatial_attend(): pl.pallas_call(spatial_kernel, name='spatial_attend', grid=(4,), out_shap...  8.57 us
    pallas_call x1, Pallas kernels, shards(): call(temporal_kernel, 'temporal', (sds(TOK, HALF), sds(TOK, HALF)), [SMEM...  7.7 us
    all_to_all x1, waiting for transfers between devices, shards(): chunks = lax.all_to_all(attn.reshape(16, 16, D), TM, 0, 0, tiled=True)  7.35 us
    unnamed x35, local copies, waits for them, and re-layouts  6.87 us
  transfers between devices with their start and end apart: 19, of which 14 were waited for; matrix products, arithmetic and copies ran while one was open for 4% of the time, Pallas kernels for 12%

profile of v2, /device:TPU:1, one launch (start us, length us, event | category | flops | bytes accessed | tf_op | source)
XLA Modules:
  0.0 220.9 jit_solution(1736330682613419170)
XLA Ops:
  7.3 1.3 copy-done.4
  8.6 1.4 prepare.1
  10.8 2.1 collective-permute-start.4
  12.9 3.8 %collective-permute-done.4 = bf16[72,1536]{1,0:T(8,128)(2,1)S(1)} collective-permute-done((bf16[72,1536]{1,0:T(8,128)(2,1)S(1)}, bf16[72,1536]{1,0:T(8,128)(2,1)S(1)}, u32[]{:S(2)}, u32[]{:S(2)}) %collective-permute-start.4) | collective-permute-done | bytes 221216 | tf_op jit(solution)/shard_map/ppermute | solution.py:280
  16.8 0.8 pad_maximum_fusion.1
  17.7 1.4 first.1
  19.2 0.8 copy-done.8
  20.0 32.1 %all-gather.4.cloned.1.call-done.w_own = bf16[576,1728]{1,0:T(8,128)(2,1)} async-done(((bf16[72,1728]{1,0:T(8,128)(2,1)}), bf16[576,1728]{1,0:T(8,128)(2,1)}) %all-gather.4.cloned.1.call-update) | async-done | bytes 1990672 | tf_op jit(solution)/shard_map/all_gather | solution.py:260
  52.0 5.0 %all-to-all-start = ((bf16[16,16,1152]{2,1,0:T(8,128)(2,1)}), bf16[16,16,1152]{2,1,0:T(8,128)(2,1)S(1)}, u32[]{:S(2)}, u32[]{:S(2)}) async-start(bf16[16,16,1152]{2,1,0:T(8,128)(2,1)} %get-tuple-element.23), calls=%async_computation | async-start | bytes 1179648 | tf_op jit(solution)/shard_map/all_to_all | solution.py:290
  57.1 3.2 %fusion.2 = (bf16[288,1728]{1,0:T(8,128)(2,1)}, bf16[288,1728]{1,0:T(8,128)(2,1)}) fusion(bf16[576,1728]{1,0:T(8,128)(2,1)} %all-gather.4.cloned.1.call-done.w_own), kind=kLoop, calls=%fused_computation.7 | loop fusion | bytes 3981312 | tf_op jit(solution)/shard_map/slice | solution.py:255
  60.3 1.4 collective-permute-start.1
  61.6 1.3 collective-permute-start.2
  62.9 5.2 %all-to-all-done = bf16[16,16,1152]{2,1,0:T(8,128)(2,1)S(1)} async-done(((bf16[16,16,1152]{2,1,0:T(8,128)(2,1)}), bf16[16,16,1152]{2,1,0:T(8,128)(2,1)S(1)}, u32[]{:S(2)}, u32[]{:S(2)}) %all-to-all-start) | async-done | bytes 589856 | tf_op jit(solution)/shard_map/all_to_all | solution.py:290
  68.1 7.7 %collective-permute-start = (bf16[256,1152]{1,0:T(8,128)(2,1)S(1)}, bf16[256,1152]{1,0:T(8,128)(2,1)S(1)}, u32[]{:S(2)}, u32[]{:S(2)}) collective-permute-start(bf16[256,1152]{1,0:T(8,128)(2,1)S(1)} %bitcast.20), channel_id=1, source_target_pairs={{0,1},{1,0},{2,3},{3,2},{4,5},{5,4},{6,7},{7,6},{8,9},{9,8},{10,11... | collective-permute-start | bytes 1769480 | tf_op jit(solution)/shard_map/ppermute | solution.py:248
  75.8 11.6 %collective-permute-done.1.w_a = bf16[288,1728]{1,0:T(8,128)(2,1)} collective-permute-done((bf16[288,1728]{1,0:T(8,128)(2,1)}, bf16[288,1728]{1,0:T(8,128)(2,1)}, u32[]{:S(2)}, u32[]{:S(2)}) %collective-permute-start.1) | collective-permute-done | bytes 995360 | tf_op jit(solution)/shard_map/ppermute | solution.py:254
  87.4 1.6 collective-permute-done.2.w_b
  89.0 7.7 %temporal.1 = (bf16[256,576]{1,0:T(8,128)(2,1)S(1)}, bf16[256,576]{1,0:T(8,128)(2,1)S(1)}) custom-call(s32[3]{0:T(128)S(1)} %pad_add_fusion.flags, bf16[256,1152]{1,0:T(8,128)(2,1)S(1)} %bitcast.21, bf16[256,1152]{1,0:T(8,128)(2,1)S(1)} %collective-permute-done.x_other, bf16[576,1728]{1,0:T(8,128)(2,1)S(1)} %copy-done.3, ...), custom_call_target="tpu_custom_call" | custom-call | flops 2147483648 | bytes 6291456 | tf_op jit(solution)/shard_map/temporal/pallas_call | solution.py:292
  96.7 3.2 %collective-permute-start.3 = (bf16[256,576]{1,0:T(8,128)(2,1)S(1)}, bf16[256,576]{1,0:T(8,128)(2,1)S(1)}, u32[]{:S(2)}, u32[]{:S(2)}) collective-permute-start(bf16[256,576]{1,0:T(8,128)(2,1)S(1)} %get-tuple-element.25), channel_id=1, source_target_pairs={{0,1},{1,0},{2,3},{3,2},{4,5},{5,4},{6,7},{7,6},{8,9},{9,8},{10,11... | collective-permute-start | bytes 884744 | tf_op jit(solution)/shard_map/ppermute | solution.py:248
  99.9 1.3 collective-permute-done.3
  101.2 1.0 pad_maximum_fusion
  102.2 5.2 %all-to-all-start.1 = ((bf16[16,16,1152]{2,1,0:T(8,128)(2,1)}), bf16[16,16,1152]{2,1,0:T(8,128)(2,1)}, u32[]{:S(2)}, u32[]{:S(2)}) async-start(bf16[16,16,1152]{2,1,0:T(8,128)(2,1)} %bitcast.6), calls=%async_computation.1 | async-start | bytes 1179648 | tf_op jit(solution)/shard_map/all_to_all | solution.py:304
  107.5 3.2 %fusion = (bf16[576,864]{1,0:T(8,128)(2,1)}, bf16[576,864]{1,0:T(8,128)(2,1)}) fusion(bf16[576,3072]{1,0:T(8,128)(2,1)} %all-gather.6.cloned.1.call-done.gathered), kind=kLoop, calls=%fused_computation.5 | loop fusion | bytes 3981312 | tf_op jit(solution)/shard_map/slice | solution.py:309
  110.7 1.2 collective-permute-start.7
  111.9 1.5 collective-permute-start.8
  113.4 1.3 fusion.1
  114.7 1.2 collective-permute-start.5
  115.8 7.4 %all-to-all-done.1.chunks = bf16[16,16,1152]{2,1,0:T(8,128)(2,1)} async-done(((bf16[16,16,1152]{2,1,0:T(8,128)(2,1)}), bf16[16,16,1152]{2,1,0:T(8,128)(2,1)}, u32[]{:S(2)}, u32[]{:S(2)}) %all-to-all-start.1) | async-done | bytes 589856 | tf_op jit(solution)/shard_map/all_to_all | solution.py:304
  123.2 0.9 copy-done.6
  124.1 1.1 copy-done.9
  125.2 4.5 %middle.1 = (bf16[256,1152]{1,0:T(8,128)(2,1)}, bf16[256,1152]{1,0:T(8,128)(2,1)S(1)}, bf16[256,1152]{1,0:T(8,128)(2,1)}) custom-call(s32[3]{0:T(128)S(1)} %pad_add_fusion.flags, bf16[256,1152]{1,0:T(8,128)(2,1)S(1)} %copy-done.9, bf16[16,16,1152]{2,1,0:T(8,128)(2,1)} %all-to-all-done.1.chunks, bf16[576,576]{1,0:T(8,128)(2,1)} %get-tuple-element.46.m0, ...), custom_call_target="tpu_custom_call" | custom-call | flops 1073741824 | bytes 5242880 | tf_op jit(solution)/shard_map/middle/pallas_call | solution.py:311
  129.7 0.8 copy-done.11
  130.5 5.5 %collective-permute-done.7.low = bf16[576,864]{1,0:T(8,128)(2,1)} collective-permute-done((bf16[576,864]{1,0:T(8,128)(2,1)}, bf16[576,864]{1,0:T(8,128)(2,1)}, u32[]{:S(2)}, u32[]{:S(2)}) %collective-permute-start.7) | collective-permute-done | bytes 995360 | tf_op jit(solution)/shard_map/ppermute | solution.py:308
  136.0 1.5 collective-permute-start.9
  137.5 1.9 collective-permute-done.9.x_other
  139.4 4.9 %spatial_qkv.1 = bf16[8,3,72,512]{3,2,1,0:T(8,128)(2,1)S(1)} custom-call(s32[3]{0:T(128)S(1)} %pad_add_fusion.flags, bf16[256,1152]{1,0:T(8,128)(2,1)} %get-tuple-element.29.x_own, bf16[256,1152]{1,0:T(8,128)(2,1)} %collective-permute-done.9.x_other, bf16[576,3072]{1,0:T(8,128)(2,1)S(1)} %copy-done, bf16[576,864]{1,0:T(8,128)(2,1)} %collective-permute-done.7.low, ...), custom_call_target="tpu_custom_call" | custom-call | flops 2147483648 | bytes 6291456 | tf_op jit(solution)/shard_map/spatial_qkv/pallas_call | solution.py:321
  144.4 1.2 copy-done.1
  145.6 6.1 %all-to-all-start.2 = ((bf16[8,3,72,512]{3,2,1,0:T(8,128)(2,1)}), bf16[8,3,72,512]{3,2,1,0:T(8,128)(2,1)S(1)}, u32[]{:S(2)}, u32[]{:S(2)}) async-start(bf16[8,3,72,512]{3,2,1,0:T(8,128)(2,1)} %copy-done.1), calls=%async_computation.2 | async-start | bytes 3538944 | tf_op jit(solution)/shard_map/all_to_all | solution.py:330
  151.7 21.6 %all-gather.8.cloned.1.call-done.w_own = bf16[576,1152]{1,0:T(8,128)(2,1)} async-done(((bf16[72,1152]{1,0:T(8,128)(2,1)}), bf16[576,1152]{1,0:T(8,128)(2,1)}) %all-gather.8.cloned.1.call-update) | async-done | bytes 1327120 | tf_op jit(solution)/shard_map/all_gather | solution.py:260
  173.3 1.1 all-to-all-done.2.q_ref.all_ref
  174.4 1.4 fusion.3
  175.8 0.7 collective-permute-start.10
  176.5 2.2 collective-permute-start.11
  178.7 8.6 %spatial_attend.1 = bf16[8,72,512]{2,1,0:T(8,128)(2,1)S(1)} custom-call(bf16[8,3,72,512]{3,2,1,0:T(8,128)(2,1)S(1)} %all-to-all-done.2.q_ref.all_ref, bf16[8,3,72,512]{3,2,1,0:T(8,128)(2,1)S(1)} %all-to-all-done.2.q_ref.all_ref), custom_call_target="tpu_custom_call" | custom-call | flops 8589934592 | bytes 3145728 | tf_op jit(solution)/shard_map/spatial_attend/pallas_call | solution.py:201
  187.3 2.9 %collective-permute-done.10.w_a = bf16[288,1152]{1,0:T(8,128)(2,1)S(1)} collective-permute-done((bf16[288,1152]{1,0:T(8,128)(2,1)S(1)}, bf16[288,1152]{1,0:T(8,128)(2,1)S(1)}, u32[]{:S(2)}, u32[]{:S(2)}) %collective-permute-start.10) | collective-permute-done | bytes 663584 | tf_op jit(solution)/shard_map/ppermute | solution.py:254
  190.2 13.5 %all_to_all.20 = bf16[8,72,512]{2,1,0:T(8,128)(2,1)S(1)} all-to-all(bf16[8,72,512]{2,1,0:T(8,128)(2,1)S(1)} %spatial_attend.1), channel_id=1, replica_groups=mesh['xl'=2,'z'=8,'xh'=2,'y'=4,'c'=2] {'xh','y'}, dimensions={0} | all-to-all | bytes 1179648 | tf_op jit(solution)/shard_map/all_to_all | solution.py:333
  203.7 6.8 %collective-permute-start.12 = (bf16[576,256]{1,0:T(8,128)(2,1)S(1)}, bf16[576,256]{1,0:T(8,128)(2,1)S(1)}, u32[]{:S(2)}, u32[]{:S(2)}) collective-permute-start(bf16[576,256]{1,0:T(8,128)(2,1)S(1)} %get-tuple-element.51), channel_id=1, source_target_pairs={{0,1},{1,0},{2,3},{3,2},{4,5},{5,4},{6,7},{7,6},{8,9},{9,8},{10,11... | collective-permute-start | bytes 884744 | tf_op jit(solution)/shard_map/ppermute | solution.py:248
  210.5 1.2 collective-permute-done.12.a_rec
  211.7 2.7 %last.1 = (bf16[256,1152]{1,0:T(8,128)(2,1)}, bf16[256,1152]{1,0:T(8,128)(2,1)}) custom-call(s32[3]{0:T(128)S(1)} %pad_add_fusion.flags, bf16[576,256]{1,0:T(8,128)(2,1)S(1)} %get-tuple-element.52.a_own, bf16[576,256]{1,0:T(8,128)(2,1)S(1)} %collective-permute-done.12.a_rec, bf16[576,1152]{1,0:T(8,128)(2,1)S(1)} %copy-done.2, ...), custom_call_target="tpu_custom_call" | custom-call | flops 1073741824 | bytes 6291456 | tf_op jit(solution)/shard_map/last/pallas_call | solution.py:335
  (46 shorter events, 1.2 us)
Async XLA Ops:
  7.2 44.9 %all-gather.4.cloned.1.call-start = ((), (), s32[]{:S(2)}) async-start(), calls=%async_computation.4 | async-start | bytes 2322432 | tf_op jit(solution)/shard_map/all_gather | solution.py:260
  7.3 1.3 copy-start.4
  8.6 9.0 %copy-start.16 = (f32[2,2,3,1152]{3,1,2,0:T(2,128)S(1)}, f32[2,2,3,1152]{3,1,2,0:T(2,128)}, u32[]{:S(2)}) copy-start(f32[2,2,3,1152]{3,1,2,0:T(2,128)} %param.6) | copy-start | bytes 165892
  8.6 9.1 %copy-start.13 = (bf16[2,1,128,1152]{3,2,1,0:T(8,128)(2,1)S(1)}, bf16[2,1,128,1152]{3,2,1,0:T(8,128)(2,1)}, u32[]{:S(2)}) copy-start(bf16[2,1,128,1152]{3,2,1,0:T(8,128)(2,1)} %param.4) | copy-start | bytes 1769476
  8.6 9.1 %copy-start.14 = (bf16[2,1,128,1152]{3,2,1,0:T(8,128)(2,1)S(1)}, bf16[2,1,128,1152]{3,2,1,0:T(8,128)(2,1)}, u32[]{:S(2)}) copy-start(bf16[2,1,128,1152]{3,2,1,0:T(8,128)(2,1)} %param.5) | copy-start | bytes 1769476
  10.1 0.7 copy-start.15
  10.8 96.7 %all-gather.6.cloned.1.call-start = ((), (), s32[]{:S(2)}) async-start(), calls=%async_computation.5 | async-start | bytes 3981312 | tf_op jit(solution)/shard_map/all_gather | solution.py:260
  10.8 5.9 %collective-permute-start.4 = (bf16[72,1536]{1,0:T(8,128)(2,1)S(1)}, bf16[72,1536]{1,0:T(8,128)(2,1)S(1)}, u32[]{:S(2)}, u32[]{:S(2)}) collective-permute-start(bf16[72,1536]{1,0:T(8,128)(2,1)S(1)} %get-tuple-element.26), channel_id=1, source_target_pairs={{0,128},{128,0},{1,129},{129,1},{2,130},{130,2},{3,131},{131,3},{4... | collective-permute-start | bytes 663560 | tf_op jit(solution)/shard_map/ppermute | solution.py:280
  17.7 34.4 %copy-start.5 = (f32[12,1152]{1,0:T(8,128)}, f32[12,1152]{1,0:T(8,128)S(1)}, u32[]{:S(2)}) copy-start(f32[12,1152]{1,0:T(8,128)S(1)} %reshape.35.mods) | copy-start | bytes 165892
  19.2 0.8 copy-start.8
  52.0 16.1 %all-to-all-start = ((bf16[16,16,1152]{2,1,0:T(8,128)(2,1)}), bf16[16,16,1152]{2,1,0:T(8,128)(2,1)S(1)}, u32[]{:S(2)}, u32[]{:S(2)}) async-start(bf16[16,16,1152]{2,1,0:T(8,128)(2,1)} %get-tuple-element.23), calls=%async_computation | async-start | bytes 1179648 | tf_op jit(solution)/shard_map/all_to_all | solution.py:290
  57.1 31.9 %copy-start.3 = (bf16[576,1728]{1,0:T(8,128)(2,1)S(1)}, bf16[576,1728]{1,0:T(8,128)(2,1)}, u32[]{:S(2)}) copy-start(bf16[576,1728]{1,0:T(8,128)(2,1)} %all-gather.4.cloned.1.call-done.w_own) | copy-start | bytes 5971972
  60.3 27.1 %collective-permute-start.1 = (bf16[288,1728]{1,0:T(8,128)(2,1)}, bf16[288,1728]{1,0:T(8,128)(2,1)}, u32[]{:S(2)}, u32[]{:S(2)}) collective-permute-start(bf16[288,1728]{1,0:T(8,128)(2,1)} %get-tuple-element.48), channel_id=1, source_target_pairs={{0,128},{128,8},{8,136},{136,0},{1,129},{129,9},{9,137},{137,1},{2... | collective-permute-start | bytes 2985992 | tf_op jit(solution)/shard_map/ppermute | solution.py:254
  61.6 27.4 %collective-permute-start.2 = (bf16[288,1728]{1,0:T(8,128)(2,1)}, bf16[288,1728]{1,0:T(8,128)(2,1)}, u32[]{:S(2)}, u32[]{:S(2)}) collective-permute-start(bf16[288,1728]{1,0:T(8,128)(2,1)} %get-tuple-element.47), channel_id=1, source_target_pairs={{0,136},{128,0},{8,128},{136,8},{1,137},{129,1},{9,129},{137,9},{2... | collective-permute-start | bytes 2985992 | tf_op jit(solution)/shard_map/ppermute | solution.py:255
  68.1 20.9 %collective-permute-start = (bf16[256,1152]{1,0:T(8,128)(2,1)S(1)}, bf16[256,1152]{1,0:T(8,128)(2,1)S(1)}, u32[]{:S(2)}, u32[]{:S(2)}) collective-permute-start(bf16[256,1152]{1,0:T(8,128)(2,1)S(1)} %bitcast.20), channel_id=1, source_target_pairs={{0,1},{1,0},{2,3},{3,2},{4,5},{5,4},{6,7},{7,6},{8,9},{9,8},{10,11... | collective-permute-start | bytes 1769480 | tf_op jit(solution)/shard_map/ppermute | solution.py:248
  96.7 4.5 %collective-permute-start.3 = (bf16[256,576]{1,0:T(8,128)(2,1)S(1)}, bf16[256,576]{1,0:T(8,128)(2,1)S(1)}, u32[]{:S(2)}, u32[]{:S(2)}) collective-permute-start(bf16[256,576]{1,0:T(8,128)(2,1)S(1)} %get-tuple-element.25), channel_id=1, source_target_pairs={{0,1},{1,0},{2,3},{3,2},{4,5},{5,4},{6,7},{7,6},{8,9},{9,8},{10,11... | collective-permute-start | bytes 884744 | tf_op jit(solution)/shard_map/ppermute | solution.py:248
  102.2 21.0 %all-to-all-start.1 = ((bf16[16,16,1152]{2,1,0:T(8,128)(2,1)}), bf16[16,16,1152]{2,1,0:T(8,128)(2,1)}, u32[]{:S(2)}, u32[]{:S(2)}) async-start(bf16[16,16,1152]{2,1,0:T(8,128)(2,1)} %bitcast.6), calls=%async_computation.1 | async-start | bytes 1179648 | tf_op jit(solution)/shard_map/all_to_all | solution.py:304
  107.4 65.9 %all-gather.8.cloned.1.call-start = ((), (), s32[]{:S(2)}) async-start(), calls=%async_computation.6 | async-start | bytes 1492992 | tf_op jit(solution)/shard_map/all_gather | solution.py:260
  107.5 5.9 %copy-start = (bf16[576,3072]{1,0:T(8,128)(2,1)S(1)}, bf16[576,3072]{1,0:T(8,128)(2,1)}, u32[]{:S(2)}) copy-start(bf16[576,3072]{1,0:T(8,128)(2,1)} %all-gather.6.cloned.1.call-done.gathered) | copy-start | bytes 10616836
  110.7 25.3 %collective-permute-start.7 = (bf16[576,864]{1,0:T(8,128)(2,1)}, bf16[576,864]{1,0:T(8,128)(2,1)}, u32[]{:S(2)}, u32[]{:S(2)}) collective-permute-start(bf16[576,864]{1,0:T(8,128)(2,1)} %get-tuple-element.44), channel_id=1, source_target_pairs={{0,2},{2,4},{4,6},{6,0},{1,3},{3,5},{5,7},{7,1},{8,10},{10,12},{12... | collective-permute-start | bytes 2985992 | tf_op jit(solution)/shard_map/ppermute | solution.py:308
  111.9 24.1 %collective-permute-start.8 = (bf16[576,864]{1,0:T(8,128)(2,1)}, bf16[576,864]{1,0:T(8,128)(2,1)}, u32[]{:S(2)}, u32[]{:S(2)}) collective-permute-start(bf16[576,864]{1,0:T(8,128)(2,1)} %get-tuple-element.43), channel_id=1, source_target_pairs={{0,6},{2,0},{4,2},{6,4},{1,7},{3,1},{5,3},{7,5},{8,14},{10,8},{12,... | collective-permute-start | bytes 2985992 | tf_op jit(solution)/shard_map/ppermute | solution.py:309
  114.7 8.5 %collective-permute-start.5 = (bf16[576,576]{1,0:T(8,128)(2,1)}, bf16[576,576]{1,0:T(8,128)(2,1)}, u32[]{:S(2)}, u32[]{:S(2)}) collective-permute-start(bf16[576,576]{1,0:T(8,128)(2,1)} %get-tuple-element.46.m0), channel_id=1, source_target_pairs={{0,1},{1,0},{2,3},{3,2},{4,5},{5,4},{6,7},{7,6},{8,9},{9,8},{10,11... | collective-permute-start | bytes 1990664 | tf_op jit(solution)/shard_map/ppermute | solution.py:248
  115.8 7.4 %collective-permute-start.6 = (bf16[576,576]{1,0:T(8,128)(2,1)}, bf16[576,576]{1,0:T(8,128)(2,1)}, u32[]{:S(2)}, u32[]{:S(2)}) collective-permute-start(bf16[576,576]{1,0:T(8,128)(2,1)} %get-tuple-element.45.m1), channel_id=1, source_target_pairs={{0,1},{1,0},{2,3},{3,2},{4,5},{5,4},{6,7},{7,6},{8,9},{9,8},{10,11... | collective-permute-start | bytes 1990664 | tf_op jit(solution)/shard_map/ppermute | solution.py:248
  123.2 0.9 copy-start.6
  124.1 1.1 copy-start.9
  129.7 0.8 copy-start.11
  136.0 3.5 %collective-permute-start.9 = (bf16[256,1152]{1,0:T(8,128)(2,1)}, bf16[256,1152]{1,0:T(8,128)(2,1)}, u32[]{:S(2)}, u32[]{:S(2)}) collective-permute-start(bf16[256,1152]{1,0:T(8,128)(2,1)} %get-tuple-element.29.x_own), channel_id=1, source_target_pairs={{0,1},{1,0},{2,3},{3,2},{4,5},{5,4},{6,7},{7,6},{8,9},{9,8},{10,11... | collective-permute-start | bytes 1769480 | tf_op jit(solution)/shard_map/ppermute | solution.py:248
  144.4 1.2 copy-start.1
  145.6 28.8 %all-to-all-start.2 = ((bf16[8,3,72,512]{3,2,1,0:T(8,128)(2,1)}), bf16[8,3,72,512]{3,2,1,0:T(8,128)(2,1)S(1)}, u32[]{:S(2)}, u32[]{:S(2)}) async-start(bf16[8,3,72,512]{3,2,1,0:T(8,128)(2,1)} %copy-done.1), calls=%async_computation.2 | async-start | bytes 3538944 | tf_op jit(solution)/shard_map/all_to_all | solution.py:330
  175.8 14.4 %collective-permute-start.10 = (bf16[288,1152]{1,0:T(8,128)(2,1)S(1)}, bf16[288,1152]{1,0:T(8,128)(2,1)S(1)}, u32[]{:S(2)}, u32[]{:S(2)}) collective-permute-start(bf16[288,1152]{1,0:T(8,128)(2,1)S(1)} %get-tuple-element.50), channel_id=1, source_target_pairs={{0,128},{128,8},{8,136},{136,0},{1,129},{129,9},{9,137},{137,1},{2... | collective-permute-start | bytes 1990664 | tf_op jit(solution)/shard_map/ppermute | solution.py:254
  176.5 13.7 %collective-permute-start.11 = (bf16[288,1152]{1,0:T(8,128)(2,1)S(1)}, bf16[288,1152]{1,0:T(8,128)(2,1)S(1)}, u32[]{:S(2)}, u32[]{:S(2)}) collective-permute-start(bf16[288,1152]{1,0:T(8,128)(2,1)S(1)} %get-tuple-element.49), channel_id=1, source_target_pairs={{0,136},{128,0},{8,128},{136,8},{1,137},{129,1},{9,129},{137,9},{2... | collective-permute-start | bytes 1990664 | tf_op jit(solution)/shard_map/ppermute | solution.py:255
  178.7 33.0 %copy-start.12 = (bf16[256,1152]{1,0:T(8,128)(2,1)S(1)}, bf16[256,1152]{1,0:T(8,128)(2,1)}, u32[]{:S(2)}) copy-start(bf16[256,1152]{1,0:T(8,128)(2,1)} %copy-done.11) | copy-start | bytes 1769476
  187.3 24.4 %copy-start.2 = (bf16[576,1152]{1,0:T(8,128)(2,1)S(1)}, bf16[576,1152]{1,0:T(8,128)(2,1)}, u32[]{:S(2)}) copy-start(bf16[576,1152]{1,0:T(8,128)(2,1)} %all-gather.8.cloned.1.call-done.w_own) | copy-start | bytes 3981316
  187.3 24.4 %copy-start.7 = (f32[12,1152]{1,0:T(8,128)S(1)}, f32[12,1152]{1,0:T(8,128)}, u32[]{:S(2)}) copy-start(f32[12,1152]{1,0:T(8,128)} %copy-done.5) | copy-start | bytes 165892
  187.3 24.4 %copy-start.10 = (bf16[256,1152]{1,0:T(8,128)(2,1)S(1)}, bf16[256,1152]{1,0:T(8,128)(2,1)}, u32[]{:S(2)}) copy-start(bf16[256,1152]{1,0:T(8,128)(2,1)} %get-tuple-element.34.nt) | copy-start | bytes 1769476
  203.7 8.0 %collective-permute-start.12 = (bf16[576,256]{1,0:T(8,128)(2,1)S(1)}, bf16[576,256]{1,0:T(8,128)(2,1)S(1)}, u32[]{:S(2)}, u32[]{:S(2)}) collective-permute-start(bf16[576,256]{1,0:T(8,128)(2,1)S(1)} %get-tuple-element.51), channel_id=1, source_target_pairs={{0,1},{1,0},{2,3},{3,2},{4,5},{5,4},{6,7},{7,6},{8,9},{9,8},{10,11... | collective-permute-start | bytes 884744 | tf_op jit(solution)/shard_map/ppermute | solution.py:248
Sparse Core Ops, SparseCore 0:
  10.9 41.1 all-gather.3
  54.4 53.0 all-gather.5
  137.6 35.6 all-gather.7

commit v3 on v2

--- a/solution.py
+++ b/solution.py
@@ -14,6 +14,7 @@
 WIDE = QKV // 2
 PAD = 896
 BOTH = 1536
+LAST = 640
 TOK = 256
 SCALE = math.log2(math.e) / math.sqrt(HD)
 TM = ("xl", "z")
@@ -79,7 +80,8 @@
     second_out[:, WIDE:PAD] = jnp.zeros((HD, PAD - WIDE), BF)
     second_out[:, PAD : PAD + HALF] = choose(1, 3 * D, HALF, 2, c)
     second_out[:, PAD + HALF :] = jnp.zeros((HD, BOTH - PAD - HALF), BF)
-    third_out[...] = w[0, :, 3 * D :]
+    third_out[:, :HALF] = choose(0, 3 * D, HALF, 2, c)
+    third_out[:, HALF:] = jnp.zeros((HD, LAST - HALF), BF)
 
 
 def first_kernel(lat, cache, mods, h_out, modin_out):
@@ -214,31 +216,34 @@
     )(packed, packed)
 
 
+def out_dot(flags, a, w_mine, w_partner):
+    halves = []
+    for xl0, xl1 in (w_mine, w_partner):
+        w = jnp.concatenate([xl0[...], xl1[...]], axis=0)
+        halves.append(jnp.dot(a, w, preferred_element_type=F32).astype(BF))
+    first = flags[1] == 0
+    low = jnp.where(first, halves[0], halves[1])
+    high = jnp.where(first, halves[1], halves[0])
+    return jnp.concatenate([low, high], axis=1)
+
+
 def middle_kernel(flags, h1, chunks, m0, m1, p0, p1, mods, nt_out, h_out, modin_out):
     a = jnp.transpose(chunks[...].astype(F32).reshape(16, 2, 8, D), (1, 0, 2, 3)).reshape(TOK, D).astype(BF)
     low, high = a[:, :HALF], a[:, HALF:]
     first = flags[1] == 0
     a = jnp.concatenate([jnp.where(first, low, high), jnp.where(first, high, low)], axis=1)
-    halves = []
-    for xl0, xl1 in ((m0, m1), (p0, p1)):
-        w = jnp.concatenate([xl0[...], xl1[...]], axis=0)
-        halves.append(jnp.dot(a, w, preferred_element_type=F32).astype(BF))
-    low = jnp.where(first, halves[0], halves[1])
-    high = jnp.where(first, halves[1], halves[0])
-    nt = jnp.concatenate([low, high], axis=1)
+    nt = out_dot(flags, a, (m0, m1), (p0, p1))
     nt_out[...] = nt
     h = gated(h1[...], mods[5:6], nt)
     h_out[...] = h
     modin_out[...] = normed(h, mods[7:8], mods[6:7])
 
 
-def last_kernel(flags, a_own, a_rec, w_own, w_a, w_b, h2, nt, mods, block_out, ns_out):
-    same = flags[0] == flags[1]
+def last_kernel(flags, a_own, a_rec, m0, m1, p0, p1, h2, nt, mods, block_out, ns_out):
+    first = flags[1] == 0
     mine, received = a_own[...], a_rec[...]
-    a = jnp.concatenate([jnp.where(same, mine, received), jnp.where(same, received, mine)], axis=0)
-    a = a.astype(F32).T.astype(BF)
-    w = jnp.concatenate([w_own[...], w_a[...], w_b[...]], axis=0)
-    ns = jnp.dot(a, w, preferred_element_type=F32).astype(BF)
+    a = jnp.concatenate([jnp.where(first, mine, received), jnp.where(first, received, mine)], axis=0)
+    ns = out_dot(flags, a.astype(F32).T.astype(BF), (m0, m1), (p0, p1))
     ns_out[...] = ns
     h = gated(h2[...], mods[8:9], ns)
     block_out[...] = gated(h, mods[11:12], nt[...])
@@ -254,6 +259,11 @@
         lax.ppermute(own[:288], XX, X_UP),
         lax.ppermute(own[288:], XX, X_DOWN),
     )
+
+
+def both_halves(own, xl):
+    other = lax.ppermute(own, "xl", CORE)
+    return jnp.concatenate([jnp.where(xl == 0, own, other), jnp.where(xl == 0, other, own)], axis=1)
 
 
 def gather_z(w):
@@ -272,15 +282,13 @@
     first_w, second_w, third_w = call(
         prepare_kernel,
         "prepare",
-        (sds(HD, QKV), sds(HD, BOTH), sds(HD, D)),
+        (sds(HD, QKV), sds(HD, BOTH), sds(HD, LAST)),
         [SMEM, VMEM],
         nbytes=2**21,
     )(flags, weights)
     w1_own = gather_z(first_w)
-    partner = lax.ppermute(second_w, "xl", CORE)
-    low, high = jnp.where(xl == 0, second_w, partner), jnp.where(xl == 0, partner, second_w)
-    second_w = gather_z(jnp.concatenate([low, high], axis=1))
-    w0_out = gather_z(third_w)
+    second_w = gather_z(both_halves(second_w, xl))
+    third_w = gather_z(both_halves(third_w, xl))
 
     h1, modin = call(first_kernel, "first", (sds(TOK, D), sds(16, 16, D)), [VMEM] * 3, nbytes=2**21)(
         latent.reshape(TOK, D), spatial_cache.reshape(TOK, D), mods
@@ -316,7 +324,7 @@
         flops=2**30,
         nbytes=5 * 2**20,
     )(flags, h1, chunks, *w1_out, *w1_partner, mods)
-    modin = after(modin, *far)
+    modin = after(modin, far[0])
     modin_other = core_swap(modin)
     packed = call(
         spatial_qkv_kernel,
@@ -328,18 +336,19 @@
         nbytes=6 * 2**20,
     )(flags, modin, modin_other, second_w, *far)
     packed = lax.all_to_all(packed, ("xh", "y"), 0, 0, tiled=True)
-    w0_out = from_x(after(w0_out, packed))
-    attn = after(spatial_attend(packed), *w0_out)
+    attn = spatial_attend(packed)
+    w0_out = third_w[:, :HALF], third_w[:, LAST : LAST + HALF]
+    w0_partner = tuple(core_swap(w) for w in w0_out)
     attn = lax.all_to_all(attn, ("xh", "y"), 0, 0, tiled=True).reshape(HALF, 512)
     a_rec = core_swap(attn[:, TOK:])
     block_out, ns = call(
         last_kernel,
         "last",
         (sds(TOK, D), sds(TOK, D)),
-        [SMEM] + [VMEM] * 8,
+        [SMEM] + [VMEM] * 9,
         flops=2**30,
         nbytes=6 * 2**20,
-    )(flags, attn[:, :TOK], a_rec, *w0_out, h2, nt, mods)
+    )(flags, attn[:, :TOK], a_rec, *w0_out, *w0_partner, h2, nt, mods)
     whole = (2, 1, 128, D)
     return block_out.reshape(whole), ns.reshape(whole), nt.reshape(whole)
 

time: 221 us -> 217 us (0.982)
  waiting for transfers between devices: 97.1 us -> 77.8 us
  blocking collectives: 13.5 us -> 28.1 us
  starting transfers between devices: 47.2 us -> 43.1 us
    all_gather x3, waiting for transfers between devices: 53.7 us -> 32.1 us  [gather_z(): return lax.all_gather(w, 'z', axis=0, tiled=True)]
    all_to_all x1, blocking collectives: 13.5 us -> 28.1 us  [shards(): packed = lax.all_to_all(packed, ('xh', 'y'), 0, 0, tiled=True)]
    all_to_all x1, waiting for transfers between devices: 1.07 us -> 4.9 us  [shards(): lax.all_to_all(attn, ('xh', 'y'), 0, 0, tiled=True).reshape(HALF, 512)]
    ppermute x1 -> x2, waiting for transfers between devices: 3.81 us -> 6.82 us  [both_halves(): other = lax.ppermute(own, 'xl', CORE)]
    ppermute x2 -> x1, waiting for transfers between devices: 14.4 us -> 11.6 us  [from_x(): lax.ppermute(own[:288], XX, X_UP)]
    ppermute x6 -> x8, waiting for transfers between devices: 4.42 us -> 2.47 us  [core_swap(): return lax.ppermute(a, 'c', CORE)]
    slice x2 -> x1, local copies, waits for them, and re-layouts: 4.55 us -> 3.16 us  [from_x(): own[288:]]
    unnamed x35 -> x33, local copies, waits for them, and re-layouts: 6.87 us -> 7.71 us
  transfers between devices with their start and end apart: 19 -> 20, of which waited for: 14 -> 12; matrix products, arithmetic and copies ran while one was open for 4% -> 6% of each run, Pallas kernels for 12% -> 13%
where the time goes in v3:
time: 217 us; the launch traced here: 216 us
  waiting for transfers between devices  77.8 us (36%)
  starting transfers between devices  43.1 us (20%)
  Pallas kernels  32.7 us (15%)
  blocking collectives  28.1 us (13%)
  local copies, waits for them, and re-layouts  17.9 us (8%)
  between operations  13.9 us (6%)
  other arithmetic  2.6 us (1%)
    all_gather x3, waiting for transfers between devices, gather_z(): return lax.all_gather(w, 'z', axis=0, tiled=True)  32.1 us
    all_to_all x1, blocking collectives, shards(): packed = lax.all_to_all(packed, ('xh', 'y'), 0, 0, tiled=True)  28.1 us
    ppermute x8, starting transfers between devices, core_swap(): return lax.ppermute(a, 'c', CORE)  19.7 us
    ppermute x1, waiting for transfers between devices, from_x(): lax.ppermute(own[:288], XX, X_UP)  11.6 us
    pallas_call x1, Pallas kernels, spatial_attend(): pl.pallas_call(spatial_kernel, name='spatial_attend', grid=(4,), out_shap...  9.22 us
    unnamed x33, local copies, waits for them, and re-layouts  7.71 us
    pallas_call x1, Pallas kernels, shards(): call(temporal_kernel, 'temporal', (sds(TOK, HALF), sds(TOK, HALF)), [SMEM...  7.71 us
    all_to_all x1, waiting for transfers between devices, shards(): chunks = lax.all_to_all(attn.reshape(16, 16, D), TM, 0, 0, tiled=True)  7.67 us
  transfers between devices with their start and end apart: 20, of which 12 were waited for; matrix products, arithmetic and copies ran while one was open for 6% of the time, Pallas kernels for 13%

profile of v3, /device:TPU:1, one launch (start us, length us, event | category | flops | bytes accessed | tf_op | source)
XLA Modules:
  0.0 216.1 jit_solution(14909081501003356600)
XLA Ops:
  7.3 1.3 copy-done.2
  8.6 1.8 prepare.1
  11.1 2.1 collective-permute-start.4
  13.3 3.8 %collective-permute-done.4 = bf16[72,1536]{1,0:T(8,128)(2,1)S(1)} collective-permute-done((bf16[72,1536]{1,0:T(8,128)(2,1)S(1)}, bf16[72,1536]{1,0:T(8,128)(2,1)S(1)}, u32[]{:S(2)}, u32[]{:S(2)}) %collective-permute-start.4) | collective-permute-done | bytes 221216 | tf_op jit(solution)/shard_map/ppermute | solution.py:265
  17.1 0.8 pad_maximum_fusion.1
  18.1 1.4 first.1
  19.5 0.8 copy-done.7
  20.3 32.1 %all-gather.4.cloned.1.call-done.w_own = bf16[576,1728]{1,0:T(8,128)(2,1)} async-done(((bf16[72,1728]{1,0:T(8,128)(2,1)}), bf16[576,1728]{1,0:T(8,128)(2,1)}) %all-gather.4.cloned.1.call-update) | async-done | bytes 1990672 | tf_op jit(solution)/shard_map/all_gather | solution.py:270
  52.4 5.0 %all-to-all-start = ((bf16[16,16,1152]{2,1,0:T(8,128)(2,1)}), bf16[16,16,1152]{2,1,0:T(8,128)(2,1)S(1)}, u32[]{:S(2)}, u32[]{:S(2)}) async-start(bf16[16,16,1152]{2,1,0:T(8,128)(2,1)} %get-tuple-element.21), calls=%async_computation | async-start | bytes 1179648 | tf_op jit(solution)/shard_map/all_to_all | solution.py:298
  57.4 3.2 %fusion.2 = (bf16[288,1728]{1,0:T(8,128)(2,1)}, bf16[288,1728]{1,0:T(8,128)(2,1)}) fusion(bf16[576,1728]{1,0:T(8,128)(2,1)} %all-gather.4.cloned.1.call-done.w_own), kind=kLoop, calls=%fused_computation.10 | loop fusion | bytes 3981312 | tf_op jit(solution)/shard_map/slice | solution.py:260
  60.6 1.4 collective-permute-start.1
  62.0 1.3 collective-permute-start.2
  63.3 5.2 %all-to-all-done = bf16[16,16,1152]{2,1,0:T(8,128)(2,1)S(1)} async-done(((bf16[16,16,1152]{2,1,0:T(8,128)(2,1)}), bf16[16,16,1152]{2,1,0:T(8,128)(2,1)S(1)}, u32[]{:S(2)}, u32[]{:S(2)}) %all-to-all-start) | async-done | bytes 589856 | tf_op jit(solution)/shard_map/all_to_all | solution.py:298
  68.5 7.7 %collective-permute-start = (bf16[256,1152]{1,0:T(8,128)(2,1)S(1)}, bf16[256,1152]{1,0:T(8,128)(2,1)S(1)}, u32[]{:S(2)}, u32[]{:S(2)}) collective-permute-start(bf16[256,1152]{1,0:T(8,128)(2,1)S(1)} %bitcast.20), channel_id=1, source_target_pairs={{0,1},{1,0},{2,3},{3,2},{4,5},{5,4},{6,7},{7,6},{8,9},{9,8},{10,11... | collective-permute-start | bytes 1769480 | tf_op jit(solution)/shard_map/ppermute | solution.py:253
  76.2 11.6 %collective-permute-done.1.w_a = bf16[288,1728]{1,0:T(8,128)(2,1)} collective-permute-done((bf16[288,1728]{1,0:T(8,128)(2,1)}, bf16[288,1728]{1,0:T(8,128)(2,1)}, u32[]{:S(2)}, u32[]{:S(2)}) %collective-permute-start.1) | collective-permute-done | bytes 995360 | tf_op jit(solution)/shard_map/ppermute | solution.py:259
  87.7 1.6 collective-permute-done.2.w_b
  89.3 7.7 %temporal.1 = (bf16[256,576]{1,0:T(8,128)(2,1)S(1)}, bf16[256,576]{1,0:T(8,128)(2,1)S(1)}) custom-call(s32[3]{0:T(128)S(1)} %pad_add_fusion.flags, bf16[256,1152]{1,0:T(8,128)(2,1)S(1)} %bitcast.21, bf16[256,1152]{1,0:T(8,128)(2,1)S(1)} %collective-permute-done.x_other, bf16[576,1728]{1,0:T(8,128)(2,1)S(1)} %copy-done.1, ...), custom_call_target="tpu_custom_call" | custom-call | flops 2147483648 | bytes 6291456 | tf_op jit(solution)/shard_map/temporal/pallas_call | solution.py:300
  97.1 3.2 %collective-permute-start.3 = (bf16[256,576]{1,0:T(8,128)(2,1)S(1)}, bf16[256,576]{1,0:T(8,128)(2,1)S(1)}, u32[]{:S(2)}, u32[]{:S(2)}) collective-permute-start(bf16[256,576]{1,0:T(8,128)(2,1)S(1)} %get-tuple-element.23), channel_id=1, source_target_pairs={{0,1},{1,0},{2,3},{3,2},{4,5},{5,4},{6,7},{7,6},{8,9},{9,8},{10,11... | collective-permute-start | bytes 884744 | tf_op jit(solution)/shard_map/ppermute | solution.py:253
  100.3 1.3 collective-permute-done.3
  101.5 1.0 pad_maximum_fusion
  102.5 5.2 %all-to-all-start.1 = ((bf16[16,16,1152]{2,1,0:T(8,128)(2,1)}), bf16[16,16,1152]{2,1,0:T(8,128)(2,1)}, u32[]{:S(2)}, u32[]{:S(2)}) async-start(bf16[16,16,1152]{2,1,0:T(8,128)(2,1)} %bitcast.6), calls=%async_computation.1 | async-start | bytes 1179648 | tf_op jit(solution)/shard_map/all_to_all | solution.py:312
  107.8 3.2 %fusion = (bf16[576,864]{1,0:T(8,128)(2,1)}, bf16[576,864]{1,0:T(8,128)(2,1)}) fusion(bf16[576,3072]{1,0:T(8,128)(2,1)} %all-gather.6.cloned.1.call-done.gathered), kind=kLoop, calls=%fused_computation.8 | loop fusion | bytes 3981312 | tf_op jit(solution)/shard_map/slice | solution.py:317
  111.0 1.2 collective-permute-start.7
  112.2 1.3 fusion.1
  113.5 0.9 collective-permute-start.5
  114.4 1.5 collective-permute-start.9
  115.9 7.7 %all-to-all-done.1.chunks = bf16[16,16,1152]{2,1,0:T(8,128)(2,1)} async-done(((bf16[16,16,1152]{2,1,0:T(8,128)(2,1)}), bf16[16,16,1152]{2,1,0:T(8,128)(2,1)}, u32[]{:S(2)}, u32[]{:S(2)}) %all-to-all-start.1) | async-done | bytes 589856 | tf_op jit(solution)/shard_map/all_to_all | solution.py:312
  123.5 0.9 copy-done.4
  124.4 1.1 copy-done.8
  125.5 4.5 %middle.1 = (bf16[256,1152]{1,0:T(8,128)(2,1)}, bf16[256,1152]{1,0:T(8,128)(2,1)S(1)}, bf16[256,1152]{1,0:T(8,128)(2,1)}) custom-call(s32[3]{0:T(128)S(1)} %pad_add_fusion.flags, bf16[256,1152]{1,0:T(8,128)(2,1)S(1)} %copy-done.8, bf16[16,16,1152]{2,1,0:T(8,128)(2,1)} %all-to-all-done.1.chunks, bf16[576,576]{1,0:T(8,128)(2,1)} %get-tuple-element.42.m0, ...), custom_call_target="tpu_custom_call" | custom-call | flops 1073741824 | bytes 5242880 | tf_op jit(solution)/shard_map/middle/pallas_call | solution.py:319
  130.0 0.8 copy-done.9
  130.8 5.4 %collective-permute-done.7.low = bf16[576,864]{1,0:T(8,128)(2,1)} collective-permute-done((bf16[576,864]{1,0:T(8,128)(2,1)}, bf16[576,864]{1,0:T(8,128)(2,1)}, u32[]{:S(2)}, u32[]{:S(2)}) %collective-permute-start.7) | collective-permute-done | bytes 995360 | tf_op jit(solution)/shard_map/ppermute | solution.py:316
  136.3 1.5 collective-permute-start.8
  137.8 1.3 collective-permute-start.11
  139.0 3.0 %collective-permute-done.11 = bf16[72,640]{1,0:T(8,128)(2,1)S(1)} collective-permute-done((bf16[72,640]{1,0:T(8,128)(2,1)S(1)}, bf16[72,640]{1,0:T(8,128)(2,1)S(1)}, u32[]{:S(2)}, u32[]{:S(2)}) %collective-permute-start.11) | collective-permute-done | bytes 92192 | tf_op jit(solution)/shard_map/ppermute | solution.py:265
  142.8 5.0 %spatial_qkv.1 = bf16[8,3,72,512]{3,2,1,0:T(8,128)(2,1)S(1)} custom-call(s32[3]{0:T(128)S(1)} %pad_add_fusion.flags, bf16[256,1152]{1,0:T(8,128)(2,1)} %get-tuple-element.27.x_own, bf16[256,1152]{1,0:T(8,128)(2,1)} %collective-permute-done.8.x_other, bf16[576,3072]{1,0:T(8,128)(2,1)S(1)} %copy-done, bf16[576,864]{1,0:T(8,128)(2,1)} %collective-permute-done.7.low, ...), custom_call_target="tpu_custom_call" | custom-call | flops 2147483648 | bytes 6291456 | tf_op jit(solution)/shard_map/spatial_qkv/pallas_call | solution.py:329
  147.8 28.1 %all_to_all.20.q_ref.all_ref = bf16[8,3,72,512]{3,2,1,0:T(8,128)(2,1)S(1)} all-to-all(bf16[8,3,72,512]{3,2,1,0:T(8,128)(2,1)S(1)} %spatial_qkv.1), channel_id=1, replica_groups=mesh['xl'=2,'z'=8,'xh'=2,'y'=4,'c'=2] {'xh','y'}, dimensions={0} | all-to-all | bytes 3538944 | tf_op jit(solution)/shard_map/all_to_all | solution.py:338
  175.9 9.2 %spatial_attend.1 = bf16[8,72,512]{2,1,0:T(8,128)(2,1)} custom-call(bf16[8,3,72,512]{3,2,1,0:T(8,128)(2,1)S(1)} %all_to_all.20.q_ref.all_ref, bf16[8,3,72,512]{3,2,1,0:T(8,128)(2,1)S(1)} %all_to_all.20.q_ref.all_ref), custom_call_target="tpu_custom_call" | custom-call | flops 8589934592 | bytes 3145728 | tf_op jit(solution)/shard_map/spatial_attend/pallas_call | solution.py:203
  185.1 4.2 %all-to-all-start.3 = ((bf16[8,72,512]{2,1,0:T(8,128)(2,1)}), bf16[8,72,512]{2,1,0:T(8,128)(2,1)}, u32[]{:S(2)}, u32[]{:S(2)}) async-start(bf16[8,72,512]{2,1,0:T(8,128)(2,1)} %spatial_attend.1), calls=%async_computation.3 | async-start | bytes 1179648 | tf_op jit(solution)/shard_map/all_to_all | solution.py:342
  189.3 1.5 fusion.3
  190.8 2.6 %collective-permute-start.12 = (bf16[576,576]{1,0:T(8,128)(2,1)S(1)}, bf16[576,576]{1,0:T(8,128)(2,1)S(1)}, u32[]{:S(2)}, u32[]{:S(2)}) collective-permute-start(bf16[576,576]{1,0:T(8,128)(2,1)S(1)} %get-tuple-element.46.m0), channel_id=1, source_target_pairs={{0,1},{1,0},{2,3},{3,2},{4,5},{5,4},{6,7},{7,6},{8,9},{9,8},{10,11... | collective-permute-start | bytes 1990664 | tf_op jit(solution)/shard_map/ppermute | solution.py:253
  193.5 4.9 %all-to-all-done.3 = bf16[8,72,512]{2,1,0:T(8,128)(2,1)} async-done(((bf16[8,72,512]{2,1,0:T(8,128)(2,1)}), bf16[8,72,512]{2,1,0:T(8,128)(2,1)}, u32[]{:S(2)}, u32[]{:S(2)}) %all-to-all-start.3) | async-done | bytes 589856 | tf_op jit(solution)/shard_map/all_to_all | solution.py:342
  198.4 1.1 fusion.4
  199.5 3.7 %collective-permute-start.10 = (bf16[576,256]{1,0:T(8,128)(2,1)S(1)}, bf16[576,256]{1,0:T(8,128)(2,1)S(1)}, u32[]{:S(2)}, u32[]{:S(2)}) collective-permute-start(bf16[576,256]{1,0:T(8,128)(2,1)S(1)} %get-tuple-element.47), channel_id=1, source_target_pairs={{0,1},{1,0},{2,3},{3,2},{4,5},{5,4},{6,7},{7,6},{8,9},{9,8},{10,11... | collective-permute-start | bytes 884744 | tf_op jit(solution)/shard_map/ppermute | solution.py:253
  203.2 1.2 collective-permute-done.10.a_rec
  204.4 1.1 copy-done.6
  205.5 1.1 copy-done.10
  206.6 3.0 %last.1 = (bf16[256,1152]{1,0:T(8,128)(2,1)}, bf16[256,1152]{1,0:T(8,128)(2,1)}) custom-call(s32[3]{0:T(128)S(1)} %pad_add_fusion.flags, bf16[576,256]{1,0:T(8,128)(2,1)S(1)} %get-tuple-element.48.a_own, bf16[576,256]{1,0:T(8,128)(2,1)S(1)} %collective-permute-done.10.a_rec, bf16[576,576]{1,0:T(8,128)(2,1)S(1)} %get-tuple-element.46.m0, ...), custom_call_target="tpu_custom_call" | custom-call | flops 1073741824 | bytes 6291456 | tf_op jit(solution)/shard_map/last/pallas_call | solution.py:344
  (48 shorter events, 1.9 us)
Async XLA Ops:
  7.2 45.2 %all-gather.4.cloned.1.call-start = ((), (), s32[]{:S(2)}) async-start(), calls=%async_computation.4 | async-start | bytes 2322432 | tf_op jit(solution)/shard_map/all_gather | solution.py:270
  7.3 1.3 copy-start.2
  8.6 9.3 %copy-start.15 = (f32[2,2,3,1152]{3,1,2,0:T(2,128)S(1)}, f32[2,2,3,1152]{3,1,2,0:T(2,128)}, u32[]{:S(2)}) copy-start(f32[2,2,3,1152]{3,1,2,0:T(2,128)} %param.6) | copy-start | bytes 165892
  8.6 9.4 %copy-start.11 = (bf16[2,1,128,1152]{3,2,1,0:T(8,128)(2,1)S(1)}, bf16[2,1,128,1152]{3,2,1,0:T(8,128)(2,1)}, u32[]{:S(2)}) copy-start(bf16[2,1,128,1152]{3,2,1,0:T(8,128)(2,1)} %param.4) | copy-start | bytes 1769476
  8.6 9.4 %copy-start.12 = (bf16[2,1,128,1152]{3,2,1,0:T(8,128)(2,1)S(1)}, bf16[2,1,128,1152]{3,2,1,0:T(8,128)(2,1)}, u32[]{:S(2)}) copy-start(bf16[2,1,128,1152]{3,2,1,0:T(8,128)(2,1)} %param.5) | copy-start | bytes 1769476
  10.4 0.6 copy-start.13
  11.1 96.7 %all-gather.6.cloned.1.call-start = ((), (), s32[]{:S(2)}) async-start(), calls=%async_computation.5 | async-start | bytes 3981312 | tf_op jit(solution)/shard_map/all_gather | solution.py:270
  11.1 5.9 %collective-permute-start.4 = (bf16[72,1536]{1,0:T(8,128)(2,1)S(1)}, bf16[72,1536]{1,0:T(8,128)(2,1)S(1)}, u32[]{:S(2)}, u32[]{:S(2)}) collective-permute-start(bf16[72,1536]{1,0:T(8,128)(2,1)S(1)} %get-tuple-element.24), channel_id=1, source_target_pairs={{0,128},{128,0},{1,129},{129,1},{2,130},{130,2},{3,131},{131,3},{4... | collective-permute-start | bytes 663560 | tf_op jit(solution)/shard_map/ppermute | solution.py:265
  18.0 34.4 %copy-start.3 = (f32[12,1152]{1,0:T(8,128)}, f32[12,1152]{1,0:T(8,128)S(1)}, u32[]{:S(2)}) copy-start(f32[12,1152]{1,0:T(8,128)S(1)} %reshape.35.mods) | copy-start | bytes 165892
  19.5 0.8 copy-start.7
  52.4 16.1 %all-to-all-start = ((bf16[16,16,1152]{2,1,0:T(8,128)(2,1)}), bf16[16,16,1152]{2,1,0:T(8,128)(2,1)S(1)}, u32[]{:S(2)}, u32[]{:S(2)}) async-start(bf16[16,16,1152]{2,1,0:T(8,128)(2,1)} %get-tuple-element.21), calls=%async_computation | async-start | bytes 1179648 | tf_op jit(solution)/shard_map/all_to_all | solution.py:298
  57.4 31.9 %copy-start.1 = (bf16[576,1728]{1,0:T(8,128)(2,1)S(1)}, bf16[576,1728]{1,0:T(8,128)(2,1)}, u32[]{:S(2)}) copy-start(bf16[576,1728]{1,0:T(8,128)(2,1)} %all-gather.4.cloned.1.call-done.w_own) | copy-start | bytes 5971972
  60.6 27.1 %collective-permute-start.1 = (bf16[288,1728]{1,0:T(8,128)(2,1)}, bf16[288,1728]{1,0:T(8,128)(2,1)}, u32[]{:S(2)}, u32[]{:S(2)}) collective-permute-start(bf16[288,1728]{1,0:T(8,128)(2,1)} %get-tuple-element.44), channel_id=1, source_target_pairs={{0,128},{128,8},{8,136},{136,0},{1,129},{129,9},{9,137},{137,1},{2... | collective-permute-start | bytes 2985992 | tf_op jit(solution)/shard_map/ppermute | solution.py:259
  62.0 27.4 %collective-permute-start.2 = (bf16[288,1728]{1,0:T(8,128)(2,1)}, bf16[288,1728]{1,0:T(8,128)(2,1)}, u32[]{:S(2)}, u32[]{:S(2)}) collective-permute-start(bf16[288,1728]{1,0:T(8,128)(2,1)} %get-tuple-element.43), channel_id=1, source_target_pairs={{0,136},{128,0},{8,128},{136,8},{1,137},{129,1},{9,129},{137,9},{2... | collective-permute-start | bytes 2985992 | tf_op jit(solution)/shard_map/ppermute | solution.py:260
  68.5 20.9 %collective-permute-start = (bf16[256,1152]{1,0:T(8,128)(2,1)S(1)}, bf16[256,1152]{1,0:T(8,128)(2,1)S(1)}, u32[]{:S(2)}, u32[]{:S(2)}) collective-permute-start(bf16[256,1152]{1,0:T(8,128)(2,1)S(1)} %bitcast.20), channel_id=1, source_target_pairs={{0,1},{1,0},{2,3},{3,2},{4,5},{5,4},{6,7},{7,6},{8,9},{9,8},{10,11... | collective-permute-start | bytes 1769480 | tf_op jit(solution)/shard_map/ppermute | solution.py:253
  97.1 4.4 %collective-permute-start.3 = (bf16[256,576]{1,0:T(8,128)(2,1)S(1)}, bf16[256,576]{1,0:T(8,128)(2,1)S(1)}, u32[]{:S(2)}, u32[]{:S(2)}) collective-permute-start(bf16[256,576]{1,0:T(8,128)(2,1)S(1)} %get-tuple-element.23), channel_id=1, source_target_pairs={{0,1},{1,0},{2,3},{3,2},{4,5},{5,4},{6,7},{7,6},{8,9},{9,8},{10,11... | collective-permute-start | bytes 884744 | tf_op jit(solution)/shard_map/ppermute | solution.py:253
  102.5 21.0 %all-to-all-start.1 = ((bf16[16,16,1152]{2,1,0:T(8,128)(2,1)}), bf16[16,16,1152]{2,1,0:T(8,128)(2,1)}, u32[]{:S(2)}, u32[]{:S(2)}) async-start(bf16[16,16,1152]{2,1,0:T(8,128)(2,1)} %bitcast.6), calls=%async_computation.1 | async-start | bytes 1179648 | tf_op jit(solution)/shard_map/all_to_all | solution.py:312
  107.7 81.6 %all-gather.8.cloned.1.call-start = ((), (), s32[]{:S(2)}) async-start(), calls=%async_computation.6 | async-start | bytes 1658880 | tf_op jit(solution)/shard_map/all_gather | solution.py:270
  107.8 4.4 %copy-start = (bf16[576,3072]{1,0:T(8,128)(2,1)S(1)}, bf16[576,3072]{1,0:T(8,128)(2,1)}, u32[]{:S(2)}) copy-start(bf16[576,3072]{1,0:T(8,128)(2,1)} %all-gather.6.cloned.1.call-done.gathered) | copy-start | bytes 10616836
  111.0 25.3 %collective-permute-start.7 = (bf16[576,864]{1,0:T(8,128)(2,1)}, bf16[576,864]{1,0:T(8,128)(2,1)}, u32[]{:S(2)}, u32[]{:S(2)}) collective-permute-start(bf16[576,864]{1,0:T(8,128)(2,1)} %get-tuple-element.40), channel_id=1, source_target_pairs={{0,2},{2,4},{4,6},{6,0},{1,3},{3,5},{5,7},{7,1},{8,10},{10,12},{12... | collective-permute-start | bytes 2985992 | tf_op jit(solution)/shard_map/ppermute | solution.py:316
  113.5 10.1 %collective-permute-start.5 = (bf16[576,576]{1,0:T(8,128)(2,1)}, bf16[576,576]{1,0:T(8,128)(2,1)}, u32[]{:S(2)}, u32[]{:S(2)}) collective-permute-start(bf16[576,576]{1,0:T(8,128)(2,1)} %get-tuple-element.42.m0), channel_id=1, source_target_pairs={{0,1},{1,0},{2,3},{3,2},{4,5},{5,4},{6,7},{7,6},{8,9},{9,8},{10,11... | collective-permute-start | bytes 1990664 | tf_op jit(solution)/shard_map/ppermute | solution.py:253
  114.4 9.2 %collective-permute-start.6 = (bf16[576,576]{1,0:T(8,128)(2,1)}, bf16[576,576]{1,0:T(8,128)(2,1)}, u32[]{:S(2)}, u32[]{:S(2)}) collective-permute-start(bf16[576,576]{1,0:T(8,128)(2,1)} %get-tuple-element.41.m1), channel_id=1, source_target_pairs={{0,1},{1,0},{2,3},{3,2},{4,5},{5,4},{6,7},{7,6},{8,9},{9,8},{10,11... | collective-permute-start | bytes 1990664 | tf_op jit(solution)/shard_map/ppermute | solution.py:253
  114.4 28.4 %collective-permute-start.9 = (bf16[576,864]{1,0:T(8,128)(2,1)}, bf16[576,864]{1,0:T(8,128)(2,1)}, u32[]{:S(2)}, u32[]{:S(2)}) collective-permute-start(bf16[576,864]{1,0:T(8,128)(2,1)} %get-tuple-element.39), channel_id=1, source_target_pairs={{0,6},{2,0},{4,2},{6,4},{1,7},{3,1},{5,3},{7,5},{8,14},{10,8},{12,... | collective-permute-start | bytes 2985992 | tf_op jit(solution)/shard_map/ppermute | solution.py:317
  123.5 0.9 copy-start.4
  124.4 1.1 copy-start.8
  125.5 12.3 %copy-start.14 = (bf16[72,640]{1,0:T(8,128)(2,1)S(1)}, bf16[72,640]{1,0:T(8,128)(2,1)}, u32[]{:S(2)}) copy-start(bf16[72,640]{1,0:T(8,128)(2,1)} %copy-done.13) | copy-start | bytes 276484
  130.0 0.8 copy-start.9
  136.3 6.5 %collective-permute-start.8 = (bf16[256,1152]{1,0:T(8,128)(2,1)}, bf16[256,1152]{1,0:T(8,128)(2,1)}, u32[]{:S(2)}, u32[]{:S(2)}) collective-permute-start(bf16[256,1152]{1,0:T(8,128)(2,1)} %get-tuple-element.27.x_own), channel_id=1, source_target_pairs={{0,1},{1,0},{2,3},{3,2},{4,5},{5,4},{6,7},{7,6},{8,9},{9,8},{10,11... | collective-permute-start | bytes 1769480 | tf_op jit(solution)/shard_map/ppermute | solution.py:253
  137.8 4.3 %collective-permute-start.11 = (bf16[72,640]{1,0:T(8,128)(2,1)S(1)}, bf16[72,640]{1,0:T(8,128)(2,1)S(1)}, u32[]{:S(2)}, u32[]{:S(2)}) collective-permute-start(bf16[72,640]{1,0:T(8,128)(2,1)S(1)} %copy-done.14), channel_id=1, source_target_pairs={{0,128},{128,0},{1,129},{129,1},{2,130},{130,2},{3,131},{131,3},{4... | collective-permute-start | bytes 276488 | tf_op jit(solution)/shard_map/ppermute | solution.py:265
  185.1 13.3 %all-to-all-start.3 = ((bf16[8,72,512]{2,1,0:T(8,128)(2,1)}), bf16[8,72,512]{2,1,0:T(8,128)(2,1)}, u32[]{:S(2)}, u32[]{:S(2)}) async-start(bf16[8,72,512]{2,1,0:T(8,128)(2,1)} %spatial_attend.1), calls=%async_computation.3 | async-start | bytes 1179648 | tf_op jit(solution)/shard_map/all_to_all | solution.py:342
  189.3 15.1 %copy-start.5 = (f32[12,1152]{1,0:T(8,128)S(1)}, f32[12,1152]{1,0:T(8,128)}, u32[]{:S(2)}) copy-start(f32[12,1152]{1,0:T(8,128)} %copy-done.3) | copy-start | bytes 165892
  190.8 12.4 %collective-permute-start.12 = (bf16[576,576]{1,0:T(8,128)(2,1)S(1)}, bf16[576,576]{1,0:T(8,128)(2,1)S(1)}, u32[]{:S(2)}, u32[]{:S(2)}) collective-permute-start(bf16[576,576]{1,0:T(8,128)(2,1)S(1)} %get-tuple-element.46.m0), channel_id=1, source_target_pairs={{0,1},{1,0},{2,3},{3,2},{4,5},{5,4},{6,7},{7,6},{8,9},{9,8},{10,11... | collective-permute-start | bytes 1990664 | tf_op jit(solution)/shard_map/ppermute | solution.py:253
  193.4 9.8 %collective-permute-start.13 = (bf16[576,576]{1,0:T(8,128)(2,1)S(1)}, bf16[576,576]{1,0:T(8,128)(2,1)S(1)}, u32[]{:S(2)}, u32[]{:S(2)}) collective-permute-start(bf16[576,576]{1,0:T(8,128)(2,1)S(1)} %get-tuple-element.45.m1), channel_id=1, source_target_pairs={{0,1},{1,0},{2,3},{3,2},{4,5},{5,4},{6,7},{7,6},{8,9},{9,8},{10,11... | collective-permute-start | bytes 1990664 | tf_op jit(solution)/shard_map/ppermute | solution.py:253
  199.5 4.9 %collective-permute-start.10 = (bf16[576,256]{1,0:T(8,128)(2,1)S(1)}, bf16[576,256]{1,0:T(8,128)(2,1)S(1)}, u32[]{:S(2)}, u32[]{:S(2)}) collective-permute-start(bf16[576,256]{1,0:T(8,128)(2,1)S(1)} %get-tuple-element.47), channel_id=1, source_target_pairs={{0,1},{1,0},{2,3},{3,2},{4,5},{5,4},{6,7},{7,6},{8,9},{9,8},{10,11... | collective-permute-start | bytes 884744 | tf_op jit(solution)/shard_map/ppermute | solution.py:253
  204.4 1.1 copy-start.6
  205.5 1.1 copy-start.10
Sparse Core Ops, SparseCore 0:
  11.2 41.1 all-gather.3
  54.7 53.0 all-gather.5
  142.9 35.5 all-gather.7

commit v4 on v3

--- a/solution.py
+++ b/solution.py
@@ -66,7 +66,7 @@
     return (h.astype(F32) + gate * branch.astype(F32)).astype(BF)
 
 
-def prepare_kernel(flags, w, first_out, second_out, third_out):
+def prepare_kernel(flags, w, first_out, own_out, theirs_out):
     c, color = flags[1], flags[2]
 
     def choose(layer, start, width, count, index):
@@ -76,12 +76,23 @@
         return part
 
     first_out[...] = choose(1, 0, QKV, 2, c)
-    second_out[:, :WIDE] = choose(0, 0, WIDE, 4, 2 * c + color)
-    second_out[:, WIDE:PAD] = jnp.zeros((HD, PAD - WIDE), BF)
-    second_out[:, PAD : PAD + HALF] = choose(1, 3 * D, HALF, 2, c)
-    second_out[:, PAD + HALF :] = jnp.zeros((HD, BOTH - PAD - HALF), BF)
-    third_out[:, :HALF] = choose(0, 3 * D, HALF, 2, c)
-    third_out[:, HALF:] = jnp.zeros((HD, LAST - HALF), BF)
+    w1_half, w0_half = choose(1, 3 * D, HALF, 2, c), choose(0, 3 * D, HALF, 2, c)
+    for out, half in ((own_out, color), (theirs_out, 1 - color)):
+        out[:, :WIDE] = choose(0, 0, WIDE, 4, 2 * c + half)
+        out[:, WIDE:PAD] = jnp.zeros((HD, PAD - WIDE), BF)
+        out[:, PAD : PAD + HALF] = w1_half
+        out[:, PAD + HALF : BOTH] = jnp.zeros((HD, BOTH - PAD - HALF), BF)
+        out[:, BOTH : BOTH + HALF] = w0_half
+        out[:, BOTH + HALF :] = jnp.zeros((HD, LAST - HALF), BF)
+
+
+def join_kernel(flags, own, other, second_out, third_out):
+    first = flags[0] == 0
+    low, high = jnp.where(first, own[...], other[...]), jnp.where(first, other[...], own[...])
+    second_out[:, :BOTH] = low[:, :BOTH]
+    second_out[:, BOTH:] = high[:, :BOTH]
+    third_out[:, :LAST] = low[:, BOTH:]
+    third_out[:, LAST:] = high[:, BOTH:]
 
 
 def first_kernel(lat, cache, mods, h_out, modin_out):
@@ -120,34 +131,24 @@
     )
 
 
-def project(x_own, x_other, gathered, low, high, w_all, y_t):
+def project(x_own, x_other, gathered, blocks, w_all, y_t):
     x = jnp.concatenate([x_own[...], x_other[...]], axis=0)
     w_all[0, :HALF] = gathered[:, :WIDE]
     w_all[0, HALF:] = gathered[:, BOTH : BOTH + WIDE]
-    w_all[1, :HALF] = low[...]
-    w_all[1, HALF:] = high[...]
+    for i, block in enumerate(blocks):
+        w_all[1, 288 * i : 288 * i + 288] = block[...]
     for group in range(2):
         multiply(x, w_all.at[group], y_t.at[group])
 
 
-def spatial_qkv_kernel(flags, x_own, x_other, gathered, low, high, out, w_all, y_t):
-    project(x_own, x_other, gathered, low, high, w_all, y_t)
+def spatial_qkv_kernel(flags, x_own, x_other, gathered, f0, f1, f2, f3, out, w_all, y_t):
+    project(x_own, x_other, gathered, (f0, f1, f2, f3), w_all, y_t)
     for head in range(8):
         place = 4 * (flags[2] ^ (head // 4)) + head % 4
         q, k, v = head_qkv(y_t.at[head // 4], head % 4)
         out[place, 0] = q
         out[place, 1] = k
         out[place, 2] = v
-
-
-def attend(k, q, v, mask=None):
-    s = lax.dot_general(k, q, (((0,), (0,)), ((), ())), preferred_element_type=F32)
-    p = jnp.exp2(s)
-    if mask is not None:
-        p = jnp.where(mask, p, 0.0)
-    total = jnp.sum(p, axis=0, keepdims=True)
-    o = jnp.dot(v, p.astype(BF), preferred_element_type=F32)
-    return o * (1.0 / total)
 
 
 def temporal_kernel(flags, x_own, x_other, w_own, w_a, w_b, own_out, other_out, w_all, y_t, o_t):
@@ -158,10 +159,25 @@
     key = lax.broadcasted_iota(jnp.int32, (TOK, TOK), 0)
     query = lax.broadcasted_iota(jnp.int32, (TOK, TOK), 1)
     mask = (key & 15) == (query & 15)
-    for head in range(8):
-        q, k, v = head_qkv(y_t, head)
-        o_t[head, :, :TOK] = attend(k[:, :TOK], q[:, :TOK], v[:, :TOK], mask)
-        o_t[head, :, TOK:] = attend(k[:, TOK:], q[:, TOK:], v[:, TOK:], mask)
+    units = [(head, half) for head in range(8) for half in range(2)]
+    qkv = {}
+
+    def scores(head, half):
+        if half == 0:
+            qkv[head] = head_qkv(y_t, head)
+        q, k, _ = qkv[head]
+        t = slice(half * TOK, half * TOK + TOK)
+        return lax.dot_general(k[:, t], q[:, t], (((0,), (0,)), ((), ())), preferred_element_type=F32)
+
+    s = scores(0, 0)
+    for i, (head, half) in enumerate(units):
+        following = scores(*units[i + 1]) if i < 15 else None
+        t = slice(half * TOK, half * TOK + TOK)
+        p = jnp.where(mask, jnp.exp2(s), 0.0)
+        total = jnp.sum(p, axis=0, keepdims=True)
+        o = jnp.dot(qkv[head][2][:, t], p.astype(BF), preferred_element_type=F32)
+        o_t[head, :, t] = o * (1.0 / total)
+        s = following
     o = o_t[...].reshape(HALF, 512)
     own_out[...] = o[:, :TOK].T.astype(BF)
     other_out[...] = o[:, TOK:].T.astype(BF)
@@ -216,11 +232,12 @@
     )(packed, packed)
 
 
-def out_dot(flags, a, w_mine, w_partner):
+def out_dot(flags, a_low, a_high, w_mine, w_partner):
     halves = []
     for xl0, xl1 in (w_mine, w_partner):
-        w = jnp.concatenate([xl0[...], xl1[...]], axis=0)
-        halves.append(jnp.dot(a, w, preferred_element_type=F32).astype(BF))
+        low = jnp.dot(a_low, xl0[...], preferred_element_type=F32)
+        high = jnp.dot(a_high, xl1[...], preferred_element_type=F32)
+        halves.append((low + high).astype(BF))
     first = flags[1] == 0
     low = jnp.where(first, halves[0], halves[1])
     high = jnp.where(first, halves[1], halves[0])
@@ -231,19 +248,19 @@
     a = jnp.transpose(chunks[...].astype(F32).reshape(16, 2, 8, D), (1, 0, 2, 3)).reshape(TOK, D).astype(BF)
     low, high = a[:, :HALF], a[:, HALF:]
     first = flags[1] == 0
-    a = jnp.concatenate([jnp.where(first, low, high), jnp.where(first, high, low)], axis=1)
-    nt = out_dot(flags, a, (m0, m1), (p0, p1))
+    nt = out_dot(flags, jnp.where(first, low, high), jnp.where(first, high, low), (m0, m1), (p0, p1))
     nt_out[...] = nt
     h = gated(h1[...], mods[5:6], nt)
     h_out[...] = h
     modin_out[...] = normed(h, mods[7:8], mods[6:7])
 
 
-def last_kernel(flags, a_own, a_rec, m0, m1, p0, p1, h2, nt, mods, block_out, ns_out):
+def last_kernel(flags, attn, a_rec, m0, m1, p0, p1, h2, nt, mods, block_out, ns_out):
     first = flags[1] == 0
-    mine, received = a_own[...], a_rec[...]
-    a = jnp.concatenate([jnp.where(first, mine, received), jnp.where(first, received, mine)], axis=0)
-    ns = out_dot(flags, a.astype(F32).T.astype(BF), (m0, m1), (p0, p1))
+    mine, received = attn[:, :TOK], a_rec[...]
+    low = jnp.where(first, mine, received).astype(F32).T.astype(BF)
+    high = jnp.where(first, received, mine).astype(F32).T.astype(BF)
+    ns = out_dot(flags, low, high, (m0, m1), (p0, p1))
     ns_out[...] = ns
     h = gated(h2[...], mods[8:9], ns)
     block_out[...] = gated(h, mods[11:12], nt[...])
@@ -261,11 +278,6 @@
     )
 
 
-def both_halves(own, xl):
-    other = lax.ppermute(own, "xl", CORE)
-    return jnp.concatenate([jnp.where(xl == 0, own, other), jnp.where(xl == 0, other, own)], axis=1)
-
-
 def gather_z(w):
     return lax.all_gather(w, "z", axis=0, tiled=True)
 
@@ -276,19 +288,21 @@
 
 def shards(latent, spatial_cache, modulation, weights):
     c, xl, z = lax.axis_index("c"), lax.axis_index("xl"), lax.axis_index("z")
-    color = lax.axis_index("y") % 2
+    color = (lax.axis_index("y") + xl) % 2
     flags = jnp.stack([xl, c, color]).astype(jnp.int32)
     mods = modulation.reshape(12, D)
-    first_w, second_w, third_w = call(
+    first_w, own_w, theirs = call(
         prepare_kernel,
         "prepare",
-        (sds(HD, QKV), sds(HD, BOTH), sds(HD, LAST)),
+        (sds(HD, QKV), sds(HD, BOTH + LAST), sds(HD, BOTH + LAST)),
         [SMEM, VMEM],
         nbytes=2**21,
     )(flags, weights)
     w1_own = gather_z(first_w)
-    second_w = gather_z(both_halves(second_w, xl))
-    third_w = gather_z(both_halves(third_w, xl))
+    second_w, third_w = call(
+        join_kernel, "join", (sds(HD, 2 * BOTH), sds(HD, 2 * LAST)), [SMEM, VMEM, VMEM], nbytes=2**20
+    )(flags, own_w, lax.ppermute(theirs, "xl", CORE))
+    second_w = gather_z(second_w)
 
     h1, modin = call(first_kernel, "first", (sds(TOK, D), sds(16, 16, D)), [VMEM] * 3, nbytes=2**21)(
         latent.reshape(TOK, D), spatial_cache.reshape(TOK, D), mods
@@ -310,12 +324,15 @@
     attn = jnp.concatenate([own, core_swap(other)], axis=1)
     second_w = after(second_w, attn)
     chunks = lax.all_to_all(attn.reshape(16, 16, D), TM, 0, 0, tiled=True)
+    low, high = second_w[:, :WIDE], second_w[:, BOTH : BOTH + WIDE]
+    far = (
+        lax.ppermute(low[:288], "y", Y_UP),
+        lax.ppermute(low[288:], "y", Y_DOWN),
+        lax.ppermute(high[:288], XX, X_UP),
+        lax.ppermute(high[288:], XX, X_DOWN),
+    )
     w1_out = second_w[:, PAD : PAD + HALF], second_w[:, BOTH + PAD : BOTH + PAD + HALF]
     w1_partner = tuple(core_swap(w) for w in w1_out)
-    far = (
-        lax.ppermute(second_w[:, :WIDE], "y", Y_UP),
-        lax.ppermute(second_w[:, BOTH : BOTH + WIDE], "y", Y_DOWN),
-    )
     nt, h2, modin = call(
         middle_kernel,
         "middle",
@@ -324,17 +341,18 @@
         flops=2**30,
         nbytes=5 * 2**20,
     )(flags, h1, chunks, *w1_out, *w1_partner, mods)
-    modin = after(modin, far[0])
+    modin = after(modin, *far)
     modin_other = core_swap(modin)
     packed = call(
         spatial_qkv_kernel,
         "spatial_qkv",
         sds(8, 3, HD, 512),
-        [SMEM] + [VMEM] * 5,
+        [SMEM] + [VMEM] * 7,
         [pltpu.VMEM((2, D, WIDE), BF), pltpu.VMEM((2, WIDE, 512), F32)],
         flops=2 * 2**30,
         nbytes=6 * 2**20,
     )(flags, modin, modin_other, second_w, *far)
+    third_w = gather_z(after(third_w, packed))
     packed = lax.all_to_all(packed, ("xh", "y"), 0, 0, tiled=True)
     attn = spatial_attend(packed)
     w0_out = third_w[:, :HALF], third_w[:, LAST : LAST + HALF]
@@ -348,7 +366,7 @@
         [SMEM] + [VMEM] * 9,
         flops=2**30,
         nbytes=6 * 2**20,
-    )(flags, attn[:, :TOK], a_rec, *w0_out, *w0_partner, h2, nt, mods)
+    )(flags, attn, a_rec, *w0_out, *w0_partner, h2, nt, mods)
     whole = (2, 1, 128, D)
     return block_out.reshape(whole), ns.reshape(whole), nt.reshape(whole)
 

time: 217 us -> 205 us (0.945)
  local copies, waits for them, and re-layouts: 17.9 us -> 11.5 us
  waiting for transfers between devices: 77.8 us -> 75 us
    unnamed x33 -> x19, local copies, waits for them, and re-layouts: 7.71 us -> 2.43 us
    all_to_all x1, waiting for transfers between devices: 7.67 us -> 4.12 us  [shards(): chunks = lax.all_to_all(attn.reshape(16, 16, D), TM, 0, 0, tiled=True)]
    ppermute x4 -> x5, starting transfers between devices: 6.09 us -> 7.22 us  [the longest x1 2.41 us: shards(): lax.ppermute(high[288:], XX, X_DOWN)]
    ppermute x4 -> x5, waiting for transfers between devices: 12.2 us -> 11.3 us  [the longest x1 5.79 us: shards(): lax.ppermute(theirs, 'xl', CORE)]
  transfers between devices with their start and end apart: 20 -> 21, of which waited for: 12 -> 13; matrix products, arithmetic and copies ran while one was open for 6% -> 5% of each run, Pallas kernels for 13% -> 11%
where the time goes in v4:
time: 205 us
  waiting for transfers between devices  75 us (37%)
  starting transfers between devices  43.5 us (21%)
  Pallas kernels  32.6 us (16%)
  blocking collectives  26.9 us (13%)
  between operations  13.9 us (7%)
  local copies, waits for them, and re-layouts  11.5 us (6%)
    all_gather x3, waiting for transfers between devices, gather_z(): return lax.all_gather(w, 'z', axis=0, tiled=True)  31.8 us
    all_to_all x1, blocking collectives, shards(): packed = lax.all_to_all(packed, ('xh', 'y'), 0, 0, tiled=True)  26.9 us
    ppermute x8, starting transfers between devices, core_swap(): return lax.ppermute(a, 'c', CORE)  19.7 us
    ppermute x1, waiting for transfers between devices, from_x(): lax.ppermute(own[:288], XX, X_UP)  11.6 us
    pallas_call x1, Pallas kernels, spatial_attend(): pl.pallas_call(spatial_kernel, name='spatial_attend', grid=(4,), out_shap...  9.21 us
    pallas_call x1, Pallas kernels, shards(): call(temporal_kernel, 'temporal', (sds(TOK, HALF), sds(TOK, HALF)), [SMEM...  6.35 us
    ppermute x1, waiting for transfers between devices, shards(): lax.ppermute(theirs, 'xl', CORE)  5.79 us
    all_to_all x1, waiting for transfers between devices, shards(): lax.all_to_all(attn, ('xh', 'y'), 0, 0, tiled=True).reshape(HALF, 512)  5.21 us
  transfers between devices with their start and end apart: 21, of which 13 were waited for; matrix products, arithmetic and copies ran while one was open for 5% of the time, Pallas kernels for 11%

profile of v4, /device:TPU:1, one launch (start us, length us, event | category | flops | bytes accessed | tf_op | source)
XLA Modules:
  0.0 204.6 jit_solution(17110745167836987010)
XLA Ops:
  7.2 0.1 pad_add_fusion.flags
  7.3 1.3 copy-done.2
  8.6 2.0 prepare.1
  10.6 0.0 all-gather.6.cloned.1.call-start
  10.7 2.1 %collective-permute-start.4 = (bf16[72,2176]{1,0:T(8,128)(2,1)S(1)}, bf16[72,2176]{1,0:T(8,128)(2,1)S(1)}, u32[]{:S(2)}, u32[]{:S(2)}) collective-permute-start(bf16[72,2176]{1,0:T(8,128)(2,1)S(1)} %get-tuple-element.28), channel_id=1, source_target_pairs={{0,128},{128,0},{1,129},{129,1},{2,130},{130,2},{3,131},{131,3},{4... | collective-permute-start | bytes 940040 | tf_op jit(solution)/shard_map/ppermute | solution.py:304
  12.8 5.8 %collective-permute-done.4.other = bf16[72,2176]{1,0:T(8,128)(2,1)S(1)} collective-permute-done((bf16[72,2176]{1,0:T(8,128)(2,1)S(1)}, bf16[72,2176]{1,0:T(8,128)(2,1)S(1)}, u32[]{:S(2)}, u32[]{:S(2)}) %collective-permute-start.4) | collective-permute-done | bytes 313376 | tf_op jit(solution)/shard_map/ppermute | solution.py:304
  18.6 1.4 join.1
  20.1 1.4 first.1
  21.6 30.3 %all-gather.4.cloned.1.call-done.w_own = bf16[576,1728]{1,0:T(8,128)(2,1)} async-done(((bf16[72,1728]{1,0:T(8,128)(2,1)}), bf16[576,1728]{1,0:T(8,128)(2,1)}) %all-gather.4.cloned.1.call-update) | async-done | bytes 1990672 | tf_op jit(solution)/shard_map/all_gather | solution.py:282
  51.9 5.0 %all-to-all-start = ((bf16[16,16,1152]{2,1,0:T(8,128)(2,1)}), bf16[16,16,1152]{2,1,0:T(8,128)(2,1)S(1)}, u32[]{:S(2)}, u32[]{:S(2)}) async-start(bf16[16,16,1152]{2,1,0:T(8,128)(2,1)} %get-tuple-element.24), calls=%async_computation | async-start | bytes 1179648 | tf_op jit(solution)/shard_map/all_to_all | solution.py:312
  57.0 3.2 %fusion.2 = (bf16[288,1728]{1,0:T(8,128)(2,1)}, bf16[288,1728]{1,0:T(8,128)(2,1)}) fusion(bf16[576,1728]{1,0:T(8,128)(2,1)} %all-gather.4.cloned.1.call-done.w_own), kind=kLoop, calls=%fused_computation.4 | loop fusion | bytes 3981312 | tf_op jit(solution)/shard_map/slice | solution.py:277
  60.1 1.4 collective-permute-start.1
  61.5 1.3 collective-permute-start.2
  62.8 5.2 %all-to-all-done = bf16[16,16,1152]{2,1,0:T(8,128)(2,1)S(1)} async-done(((bf16[16,16,1152]{2,1,0:T(8,128)(2,1)}), bf16[16,16,1152]{2,1,0:T(8,128)(2,1)S(1)}, u32[]{:S(2)}, u32[]{:S(2)}) %all-to-all-start) | async-done | bytes 589856 | tf_op jit(solution)/shard_map/all_to_all | solution.py:312
  68.0 7.7 %collective-permute-start = (bf16[256,1152]{1,0:T(8,128)(2,1)S(1)}, bf16[256,1152]{1,0:T(8,128)(2,1)S(1)}, u32[]{:S(2)}, u32[]{:S(2)}) collective-permute-start(bf16[256,1152]{1,0:T(8,128)(2,1)S(1)} %bitcast.21), channel_id=1, source_target_pairs={{0,1},{1,0},{2,3},{3,2},{4,5},{5,4},{6,7},{7,6},{8,9},{9,8},{10,11... | collective-permute-start | bytes 1769480 | tf_op jit(solution)/shard_map/ppermute | solution.py:270
  75.7 11.6 %collective-permute-done.1.w_a = bf16[288,1728]{1,0:T(8,128)(2,1)} collective-permute-done((bf16[288,1728]{1,0:T(8,128)(2,1)}, bf16[288,1728]{1,0:T(8,128)(2,1)}, u32[]{:S(2)}, u32[]{:S(2)}) %collective-permute-start.1) | collective-permute-done | bytes 995360 | tf_op jit(solution)/shard_map/ppermute | solution.py:276
  87.2 1.6 collective-permute-done.2.w_b
  88.9 6.4 %temporal.1 = (bf16[256,576]{1,0:T(8,128)(2,1)S(1)}, bf16[256,576]{1,0:T(8,128)(2,1)S(1)}) custom-call(s32[3]{0:T(128)S(1)} %pad_add_fusion.flags, bf16[256,1152]{1,0:T(8,128)(2,1)S(1)} %bitcast.22, bf16[256,1152]{1,0:T(8,128)(2,1)S(1)} %collective-permute-done.x_other, bf16[576,1728]{1,0:T(8,128)(2,1)S(1)} %copy-done.1, ...), custom_call_target="tpu_custom_call" | custom-call | flops 2147483648 | bytes 6291456 | tf_op jit(solution)/shard_map/temporal/pallas_call | solution.py:314
  95.2 3.2 %collective-permute-start.3 = (bf16[256,576]{1,0:T(8,128)(2,1)S(1)}, bf16[256,576]{1,0:T(8,128)(2,1)S(1)}, u32[]{:S(2)}, u32[]{:S(2)}) collective-permute-start(bf16[256,576]{1,0:T(8,128)(2,1)S(1)} %get-tuple-element.26), channel_id=1, source_target_pairs={{0,1},{1,0},{2,3},{3,2},{4,5},{5,4},{6,7},{7,6},{8,9},{9,8},{10,11... | collective-permute-start | bytes 884744 | tf_op jit(solution)/shard_map/ppermute | solution.py:270
  98.4 1.3 collective-permute-done.3
  99.7 1.0 pad_maximum_fusion
  100.7 5.2 %all-to-all-start.1 = ((bf16[16,16,1152]{2,1,0:T(8,128)(2,1)}), bf16[16,16,1152]{2,1,0:T(8,128)(2,1)S(1)}, u32[]{:S(2)}, u32[]{:S(2)}) async-start(bf16[16,16,1152]{2,1,0:T(8,128)(2,1)} %bitcast.6), calls=%async_computation.1 | async-start | bytes 1179648 | tf_op jit(solution)/shard_map/all_to_all | solution.py:326
  105.9 1.5 all-gather.6.cloned.1.call-done.gathered
  107.4 1.5 fusion.1
  108.8 0.5 collective-permute-start.5
  109.4 0.1 collective-permute-start.6
  109.5 2.9 %fusion = (bf16[288,864]{1,0:T(8,128)(2,1)}, bf16[288,864]{1,0:T(8,128)(2,1)}, bf16[288,864]{1,0:T(8,128)(2,1)}, bf16[288,864]{1,0:T(8,128)(2,1)}) fusion(bf16[576,3072]{1,0:T(8,128)(2,1)} %all-gather.6.cloned.1.call-done.gathered), kind=kLoop, calls=%fused_computation.2 | loop fusion | bytes 3981312 | tf_op jit(solution)/shard_map/slice | solution.py:332
  112.4 2.4 %collective-permute-start.10 = (bf16[288,864]{1,0:T(8,128)(2,1)}, bf16[288,864]{1,0:T(8,128)(2,1)}, u32[]{:S(2)}, u32[]{:S(2)}) collective-permute-start(bf16[288,864]{1,0:T(8,128)(2,1)} %get-tuple-element.45), channel_id=1, source_target_pairs={{0,136},{128,0},{8,128},{136,8},{1,137},{129,1},{9,129},{137,9},{2... | collective-permute-start | bytes 1493000 | tf_op jit(solution)/shard_map/ppermute | solution.py:332
  114.8 1.2 collective-permute-start.7
  116.0 1.5 collective-permute-start.8
  117.5 4.1 %all-to-all-done.1.chunks = bf16[16,16,1152]{2,1,0:T(8,128)(2,1)S(1)} async-done(((bf16[16,16,1152]{2,1,0:T(8,128)(2,1)}), bf16[16,16,1152]{2,1,0:T(8,128)(2,1)S(1)}, u32[]{:S(2)}, u32[]{:S(2)}) %all-to-all-start.1) | async-done | bytes 589856 | tf_op jit(solution)/shard_map/all_to_all | solution.py:326
  121.6 3.8 %middle.1 = (bf16[256,1152]{1,0:T(8,128)(2,1)}, bf16[256,1152]{1,0:T(8,128)(2,1)S(1)}, bf16[256,1152]{1,0:T(8,128)(2,1)S(1)}) custom-call(s32[3]{0:T(128)S(1)} %pad_add_fusion.flags, bf16[256,1152]{1,0:T(8,128)(2,1)S(1)} %get-tuple-element.21.h1, bf16[16,16,1152]{2,1,0:T(8,128)(2,1)S(1)} %all-to-all-done.1.chunks, ...), custom_call_target="tpu_custom_call" | custom-call | flops 1073741824 | bytes 5242880 | tf_op jit(solution)/shard_map/middle/pallas_call | solution.py:336
  125.4 4.3 %collective-permute-done.10.f3 = bf16[288,864]{1,0:T(8,128)(2,1)} collective-permute-done((bf16[288,864]{1,0:T(8,128)(2,1)}, bf16[288,864]{1,0:T(8,128)(2,1)}, u32[]{:S(2)}, u32[]{:S(2)}) %collective-permute-start.10) | collective-permute-done | bytes 497696 | tf_op jit(solution)/shard_map/ppermute | solution.py:332
  129.7 1.2 collective-permute-done.9.f2
  131.0 2.2 %collective-permute-start.11 = (bf16[256,1152]{1,0:T(8,128)(2,1)S(1)}, bf16[256,1152]{1,0:T(8,128)(2,1)S(1)}, u32[]{:S(2)}, u32[]{:S(2)}) collective-permute-start(bf16[256,1152]{1,0:T(8,128)(2,1)S(1)} %get-tuple-element.32.x_own), channel_id=1, source_target_pairs={{0,1},{1,0},{2,3},{3,2},{4,5},{5,4},{6,7},{7,6},{8,9},{9,8},{10,11... | collective-permute-start | bytes 1769480 | tf_op jit(solution)/shard_map/ppermute | solution.py:270
  133.2 1.6 collective-permute-done.11.x_other
  134.8 4.6 %spatial_qkv.1 = bf16[8,3,72,512]{3,2,1,0:T(8,128)(2,1)S(1)} custom-call(s32[3]{0:T(128)S(1)} %pad_add_fusion.flags, bf16[256,1152]{1,0:T(8,128)(2,1)S(1)} %get-tuple-element.32.x_own, bf16[256,1152]{1,0:T(8,128)(2,1)S(1)} %collective-permute-done.11.x_other, bf16[576,3072]{1,0:T(8,128)(2,1)S(1)} %copy-done, bf16[288,864]{1,0:T(8,128)(2,1)} %collective-permute-done.7.f0, ...), custom_call_target="tpu_custom_call" | custom-call | flops 2147483648 | bytes 6291456 | tf_op jit(solution)/shard_map/spatial_qkv/pallas_call | solution.py:346
  139.5 26.9 %all_to_all.20.q_ref.all_ref = bf16[8,3,72,512]{3,2,1,0:T(8,128)(2,1)S(1)} all-to-all(bf16[8,3,72,512]{3,2,1,0:T(8,128)(2,1)S(1)} %spatial_qkv.1), channel_id=1, replica_groups=mesh['xl'=2,'z'=8,'xh'=2,'y'=4,'c'=2] {'xh','y'}, dimensions={0} | all-to-all | bytes 3538944 | tf_op jit(solution)/shard_map/all_to_all | solution.py:356
  166.4 9.2 %spatial_attend.1 = bf16[8,72,512]{2,1,0:T(8,128)(2,1)} custom-call(bf16[8,3,72,512]{3,2,1,0:T(8,128)(2,1)S(1)} %all_to_all.20.q_ref.all_ref, bf16[8,3,72,512]{3,2,1,0:T(8,128)(2,1)S(1)} %all_to_all.20.q_ref.all_ref), custom_call_target="tpu_custom_call" | custom-call | flops 8589934592 | bytes 3145728 | tf_op jit(solution)/shard_map/spatial_attend/pallas_call | solution.py:219
  175.6 3.5 %all-to-all-start.3 = ((bf16[8,72,512]{2,1,0:T(8,128)(2,1)}), bf16[8,72,512]{2,1,0:T(8,128)(2,1)S(1)}, u32[]{:S(2)}, u32[]{:S(2)}) async-start(bf16[8,72,512]{2,1,0:T(8,128)(2,1)} %spatial_attend.1), calls=%async_computation.3 | async-start | bytes 1179648 | tf_op jit(solution)/shard_map/all_to_all | solution.py:360
  179.2 1.5 fusion.3
  180.7 2.2 %collective-permute-start.13 = (bf16[576,576]{1,0:T(8,128)(2,1)S(1)}, bf16[576,576]{1,0:T(8,128)(2,1)S(1)}, u32[]{:S(2)}, u32[]{:S(2)}) collective-permute-start(bf16[576,576]{1,0:T(8,128)(2,1)S(1)} %get-tuple-element.54.m0), channel_id=1, source_target_pairs={{0,1},{1,0},{2,3},{3,2},{4,5},{5,4},{6,7},{7,6},{8,9},{9,8},{10,11... | collective-permute-start | bytes 1990664 | tf_op jit(solution)/shard_map/ppermute | solution.py:270
  182.9 0.1 collective-permute-start.14
  183.0 5.2 %all-to-all-done.3 = bf16[8,72,512]{2,1,0:T(8,128)(2,1)S(1)} async-done(((bf16[8,72,512]{2,1,0:T(8,128)(2,1)}), bf16[8,72,512]{2,1,0:T(8,128)(2,1)S(1)}, u32[]{:S(2)}, u32[]{:S(2)}) %all-to-all-start.3) | async-done | bytes 589856 | tf_op jit(solution)/shard_map/all_to_all | solution.py:360
  188.2 3.7 %collective-permute-start.12 = (bf16[576,256]{1,0:T(8,128)(2,1)S(1)}, bf16[576,256]{1,0:T(8,128)(2,1)S(1)}, u32[]{:S(2)}, u32[]{:S(2)}) collective-permute-start(bf16[576,256]{1,0:T(8,128)(2,1)S(1)} %slice.52), channel_id=1, source_target_pairs={{0,1},{1,0},{2,3},{3,2},{4,5},{5,4},{6,7},{7,6},{8,9},{9,8},{10,11... | collective-permute-start | bytes 884744 | tf_op jit(solution)/shard_map/ppermute | solution.py:270
  191.9 1.2 collective-permute-done.12.a_rec
  193.2 1.1 copy-done.7
  194.2 3.8 %last.1 = (bf16[256,1152]{1,0:T(8,128)(2,1)}, bf16[256,1152]{1,0:T(8,128)(2,1)}) custom-call(s32[3]{0:T(128)S(1)} %pad_add_fusion.flags, bf16[576,512]{1,0:T(8,128)(2,1)S(1)} %bitcast.18, bf16[576,256]{1,0:T(8,128)(2,1)S(1)} %collective-permute-done.12.a_rec, bf16[576,576]{1,0:T(8,128)(2,1)S(1)} %get-tuple-element.54.m0, ...), custom_call_target="tpu_custom_call" | custom-call | flops 1073741824 | bytes 6291456 | tf_op jit(solution)/shard_map/last/pallas_call | solution.py:362
  (33 shorter events, 0.3 us)
Async XLA Ops:
  7.2 44.7 %all-gather.4.cloned.1.call-start = ((), (), s32[]{:S(2)}) async-start(), calls=%async_computation.4 | async-start | bytes 2322432 | tf_op jit(solution)/shard_map/all_gather | solution.py:282
  7.3 1.3 copy-start.2
  8.6 11.4 %copy-start.8 = (f32[2,2,3,1152]{3,1,2,0:T(2,128)S(1)}, f32[2,2,3,1152]{3,1,2,0:T(2,128)}, u32[]{:S(2)}) copy-start(f32[2,2,3,1152]{3,1,2,0:T(2,128)} %param.6) | copy-start | bytes 165892
  8.6 11.5 %copy-start.3 = (bf16[2,1,128,1152]{3,2,1,0:T(8,128)(2,1)S(1)}, bf16[2,1,128,1152]{3,2,1,0:T(8,128)(2,1)}, u32[]{:S(2)}) copy-start(bf16[2,1,128,1152]{3,2,1,0:T(8,128)(2,1)} %param.4) | copy-start | bytes 1769476
  8.6 11.5 %copy-start.4 = (bf16[2,1,128,1152]{3,2,1,0:T(8,128)(2,1)S(1)}, bf16[2,1,128,1152]{3,2,1,0:T(8,128)(2,1)}, u32[]{:S(2)}) copy-start(bf16[2,1,128,1152]{3,2,1,0:T(8,128)(2,1)} %param.5) | copy-start | bytes 1769476
  10.6 96.7 %all-gather.6.cloned.1.call-start = ((), (), s32[]{:S(2)}) async-start(), calls=%async_computation.5 | async-start | bytes 3981312 | tf_op jit(solution)/shard_map/all_gather | solution.py:282
  10.7 7.9 %collective-permute-start.4 = (bf16[72,2176]{1,0:T(8,128)(2,1)S(1)}, bf16[72,2176]{1,0:T(8,128)(2,1)S(1)}, u32[]{:S(2)}, u32[]{:S(2)}) collective-permute-start(bf16[72,2176]{1,0:T(8,128)(2,1)S(1)} %get-tuple-element.28), channel_id=1, source_target_pairs={{0,128},{128,0},{1,129},{129,1},{2,130},{130,2},{3,131},{131,3},{4... | collective-permute-start | bytes 940040 | tf_op jit(solution)/shard_map/ppermute | solution.py:304
  51.9 16.1 %all-to-all-start = ((bf16[16,16,1152]{2,1,0:T(8,128)(2,1)}), bf16[16,16,1152]{2,1,0:T(8,128)(2,1)S(1)}, u32[]{:S(2)}, u32[]{:S(2)}) async-start(bf16[16,16,1152]{2,1,0:T(8,128)(2,1)} %get-tuple-element.24), calls=%async_computation | async-start | bytes 1179648 | tf_op jit(solution)/shard_map/all_to_all | solution.py:312
  57.0 31.9 %copy-start.1 = (bf16[576,1728]{1,0:T(8,128)(2,1)S(1)}, bf16[576,1728]{1,0:T(8,128)(2,1)}, u32[]{:S(2)}) copy-start(bf16[576,1728]{1,0:T(8,128)(2,1)} %all-gather.4.cloned.1.call-done.w_own) | copy-start | bytes 5971972
  60.1 27.1 %collective-permute-start.1 = (bf16[288,1728]{1,0:T(8,128)(2,1)}, bf16[288,1728]{1,0:T(8,128)(2,1)}, u32[]{:S(2)}, u32[]{:S(2)}) collective-permute-start(bf16[288,1728]{1,0:T(8,128)(2,1)} %get-tuple-element.52), channel_id=1, source_target_pairs={{0,128},{128,8},{8,136},{136,0},{1,129},{129,9},{9,137},{137,1},{2... | collective-permute-start | bytes 2985992 | tf_op jit(solution)/shard_map/ppermute | solution.py:276
  61.5 27.4 %collective-permute-start.2 = (bf16[288,1728]{1,0:T(8,128)(2,1)}, bf16[288,1728]{1,0:T(8,128)(2,1)}, u32[]{:S(2)}, u32[]{:S(2)}) collective-permute-start(bf16[288,1728]{1,0:T(8,128)(2,1)} %get-tuple-element.51), channel_id=1, source_target_pairs={{0,136},{128,0},{8,128},{136,8},{1,137},{129,1},{9,129},{137,9},{2... | collective-permute-start | bytes 2985992 | tf_op jit(solution)/shard_map/ppermute | solution.py:277
  68.0 20.9 %collective-permute-start = (bf16[256,1152]{1,0:T(8,128)(2,1)S(1)}, bf16[256,1152]{1,0:T(8,128)(2,1)S(1)}, u32[]{:S(2)}, u32[]{:S(2)}) collective-permute-start(bf16[256,1152]{1,0:T(8,128)(2,1)S(1)} %bitcast.21), channel_id=1, source_target_pairs={{0,1},{1,0},{2,3},{3,2},{4,5},{5,4},{6,7},{7,6},{8,9},{9,8},{10,11... | collective-permute-start | bytes 1769480 | tf_op jit(solution)/shard_map/ppermute | solution.py:270
  95.2 4.5 %collective-permute-start.3 = (bf16[256,576]{1,0:T(8,128)(2,1)S(1)}, bf16[256,576]{1,0:T(8,128)(2,1)S(1)}, u32[]{:S(2)}, u32[]{:S(2)}) collective-permute-start(bf16[256,576]{1,0:T(8,128)(2,1)S(1)} %get-tuple-element.26), channel_id=1, source_target_pairs={{0,1},{1,0},{2,3},{3,2},{4,5},{5,4},{6,7},{7,6},{8,9},{9,8},{10,11... | collective-permute-start | bytes 884744 | tf_op jit(solution)/shard_map/ppermute | solution.py:270
  100.7 20.9 %all-to-all-start.1 = ((bf16[16,16,1152]{2,1,0:T(8,128)(2,1)}), bf16[16,16,1152]{2,1,0:T(8,128)(2,1)S(1)}, u32[]{:S(2)}, u32[]{:S(2)}) async-start(bf16[16,16,1152]{2,1,0:T(8,128)(2,1)} %bitcast.6), calls=%async_computation.1 | async-start | bytes 1179648 | tf_op jit(solution)/shard_map/all_to_all | solution.py:326
  105.9 73.3 %all-gather.8.cloned.1.call-start = ((), (), s32[]{:S(2)}) async-start(), calls=%async_computation.6 | async-start | bytes 1658880 | tf_op jit(solution)/shard_map/all_gather | solution.py:282
  108.8 8.6 %collective-permute-start.5 = (bf16[576,576]{1,0:T(8,128)(2,1)S(1)}, bf16[576,576]{1,0:T(8,128)(2,1)S(1)}, u32[]{:S(2)}, u32[]{:S(2)}) collective-permute-start(bf16[576,576]{1,0:T(8,128)(2,1)S(1)} %get-tuple-element.50.m0), channel_id=1, source_target_pairs={{0,1},{1,0},{2,3},{3,2},{4,5},{5,4},{6,7},{7,6},{8,9},{9,8},{10,11... | collective-permute-start | bytes 1990664 | tf_op jit(solution)/shard_map/ppermute | solution.py:270
  109.4 12.2 %collective-permute-start.6 = (bf16[576,576]{1,0:T(8,128)(2,1)S(1)}, bf16[576,576]{1,0:T(8,128)(2,1)}, u32[]{:S(2)}, u32[]{:S(2)}) collective-permute-start(bf16[576,576]{1,0:T(8,128)(2,1)S(1)} %get-tuple-element.49.m1), channel_id=1, source_target_pairs={{0,1},{1,0},{2,3},{3,2},{4,5},{5,4},{6,7},{7,6},{8,9},{9,8},{10,11... | collective-permute-start | bytes 1990664 | tf_op jit(solution)/shard_map/ppermute | solution.py:270
  112.4 17.4 %collective-permute-start.10 = (bf16[288,864]{1,0:T(8,128)(2,1)}, bf16[288,864]{1,0:T(8,128)(2,1)}, u32[]{:S(2)}, u32[]{:S(2)}) collective-permute-start(bf16[288,864]{1,0:T(8,128)(2,1)} %get-tuple-element.45), channel_id=1, source_target_pairs={{0,136},{128,0},{8,128},{136,8},{1,137},{129,1},{9,129},{137,9},{2... | collective-permute-start | bytes 1493000 | tf_op jit(solution)/shard_map/ppermute | solution.py:332
  114.8 15.0 %collective-permute-start.7 = (bf16[288,864]{1,0:T(8,128)(2,1)}, bf16[288,864]{1,0:T(8,128)(2,1)}, u32[]{:S(2)}, u32[]{:S(2)}) collective-permute-start(bf16[288,864]{1,0:T(8,128)(2,1)} %get-tuple-element.48), channel_id=1, source_target_pairs={{0,2},{2,4},{4,6},{6,0},{1,3},{3,5},{5,7},{7,1},{8,10},{10,12},{12... | collective-permute-start | bytes 1493000 | tf_op jit(solution)/shard_map/ppermute | solution.py:329
  116.0 13.8 %collective-permute-start.8 = (bf16[288,864]{1,0:T(8,128)(2,1)}, bf16[288,864]{1,0:T(8,128)(2,1)}, u32[]{:S(2)}, u32[]{:S(2)}) collective-permute-start(bf16[288,864]{1,0:T(8,128)(2,1)} %get-tuple-element.47), channel_id=1, source_target_pairs={{0,6},{2,0},{4,2},{6,4},{1,7},{3,1},{5,3},{7,5},{8,14},{10,8},{12,... | collective-permute-start | bytes 1493000 | tf_op jit(solution)/shard_map/ppermute | solution.py:330
  117.5 13.5 %collective-permute-start.9 = (bf16[288,864]{1,0:T(8,128)(2,1)}, bf16[288,864]{1,0:T(8,128)(2,1)}, u32[]{:S(2)}, u32[]{:S(2)}) collective-permute-start(bf16[288,864]{1,0:T(8,128)(2,1)} %get-tuple-element.46), channel_id=1, source_target_pairs={{0,128},{128,8},{8,136},{136,0},{1,129},{129,9},{9,137},{137,1},{2... | collective-permute-start | bytes 1493000 | tf_op jit(solution)/shard_map/ppermute | solution.py:331
  121.6 13.2 %copy-start = (bf16[576,3072]{1,0:T(8,128)(2,1)S(1)}, bf16[576,3072]{1,0:T(8,128)(2,1)}, u32[]{:S(2)}) copy-start(bf16[576,3072]{1,0:T(8,128)(2,1)} %all-gather.6.cloned.1.call-done.gathered) | copy-start | bytes 10616836
  125.4 14.0 %copy-start.6 = (bf16[256,1152]{1,0:T(8,128)(2,1)}, bf16[256,1152]{1,0:T(8,128)(2,1)S(1)}, u32[]{:S(2)}) copy-start(bf16[256,1152]{1,0:T(8,128)(2,1)S(1)} %get-tuple-element.35.h2) | copy-start | bytes 1769476
  131.0 3.8 %collective-permute-start.11 = (bf16[256,1152]{1,0:T(8,128)(2,1)S(1)}, bf16[256,1152]{1,0:T(8,128)(2,1)S(1)}, u32[]{:S(2)}, u32[]{:S(2)}) collective-permute-start(bf16[256,1152]{1,0:T(8,128)(2,1)S(1)} %get-tuple-element.32.x_own), channel_id=1, source_target_pairs={{0,1},{1,0},{2,3},{3,2},{4,5},{5,4},{6,7},{7,6},{8,9},{9,8},{10,11... | collective-permute-start | bytes 1769480 | tf_op jit(solution)/shard_map/ppermute | solution.py:270
  175.6 12.6 %all-to-all-start.3 = ((bf16[8,72,512]{2,1,0:T(8,128)(2,1)}), bf16[8,72,512]{2,1,0:T(8,128)(2,1)S(1)}, u32[]{:S(2)}, u32[]{:S(2)}) async-start(bf16[8,72,512]{2,1,0:T(8,128)(2,1)} %spatial_attend.1), calls=%async_computation.3 | async-start | bytes 1179648 | tf_op jit(solution)/shard_map/all_to_all | solution.py:360
  179.1 14.0 %copy-start.5 = (bf16[256,1152]{1,0:T(8,128)(2,1)S(1)}, bf16[256,1152]{1,0:T(8,128)(2,1)}, u32[]{:S(2)}) copy-start(bf16[256,1152]{1,0:T(8,128)(2,1)} %get-tuple-element.36.nt) | copy-start | bytes 1769476
  180.7 12.4 %collective-permute-start.13 = (bf16[576,576]{1,0:T(8,128)(2,1)S(1)}, bf16[576,576]{1,0:T(8,128)(2,1)S(1)}, u32[]{:S(2)}, u32[]{:S(2)}) collective-permute-start(bf16[576,576]{1,0:T(8,128)(2,1)S(1)} %get-tuple-element.54.m0), channel_id=1, source_target_pairs={{0,1},{1,0},{2,3},{3,2},{4,5},{5,4},{6,7},{7,6},{8,9},{9,8},{10,11... | collective-permute-start | bytes 1990664 | tf_op jit(solution)/shard_map/ppermute | solution.py:270
  182.9 10.3 %collective-permute-start.14 = (bf16[576,576]{1,0:T(8,128)(2,1)S(1)}, bf16[576,576]{1,0:T(8,128)(2,1)}, u32[]{:S(2)}, u32[]{:S(2)}) collective-permute-start(bf16[576,576]{1,0:T(8,128)(2,1)S(1)} %get-tuple-element.53.m1), channel_id=1, source_target_pairs={{0,1},{1,0},{2,3},{3,2},{4,5},{5,4},{6,7},{7,6},{8,9},{9,8},{10,11... | collective-permute-start | bytes 1990664 | tf_op jit(solution)/shard_map/ppermute | solution.py:270
  188.2 4.9 %collective-permute-start.12 = (bf16[576,256]{1,0:T(8,128)(2,1)S(1)}, bf16[576,256]{1,0:T(8,128)(2,1)S(1)}, u32[]{:S(2)}, u32[]{:S(2)}) collective-permute-start(bf16[576,256]{1,0:T(8,128)(2,1)S(1)} %slice.52), channel_id=1, source_target_pairs={{0,1},{1,0},{2,3},{3,2},{4,5},{5,4},{6,7},{7,6},{8,9},{9,8},{10,11... | collective-permute-start | bytes 884744 | tf_op jit(solution)/shard_map/ppermute | solution.py:270
  193.1 1.1 copy-start.7
Sparse Core Ops, SparseCore 0:
  10.7 41.1 all-gather.3
  54.3 53.0 all-gather.5
  139.6 32.6 all-gather.7

commit v5 on v4

--- a/solution.py
+++ b/solution.py
@@ -194,7 +194,7 @@
                     keys[b, rows] = all_ref[src, 1, :, lanes].astype(F32).T.astype(BF)
                     values[b, :, rows] = all_ref[src, 2, :, lanes]
 
-    places = [(j, b) for j in range(2) for b in range(2)]
+    places = [(j, b) for j in range(4) for b in range(2)]
 
     def lanes(b, rel):
         return slice(rel * 256 + b * 128, rel * 256 + b * 128 + 128)
@@ -205,7 +205,7 @@
 
     s = scores(*places[0])
     for i, (j, b) in enumerate(places):
-        following = scores(*places[i + 1]) if i < 3 else None
+        following = scores(*places[i + 1]) if i < 7 else None
         p = jnp.exp2(s)
         total = jnp.sum(p, axis=0, keepdims=True)
         o = jnp.dot(values[b], p.astype(BF), preferred_element_type=F32)
@@ -219,13 +219,13 @@
     return pl.pallas_call(
         spatial_kernel,
         name="spatial_attend",
-        grid=(4,),
+        grid=(2,),
         out_shape=sds(8, HD, 512),
         in_specs=[
-            pl.BlockSpec((2, 3, HD, 512), lambda j: (j, 0, 0, 0)),
+            pl.BlockSpec((4, 3, HD, 512), lambda j: (j, 0, 0, 0)),
             pl.BlockSpec((8, 3, HD, 512), lambda j: (0, 0, 0, 0)),
         ],
-        out_specs=pl.BlockSpec((2, HD, 512), lambda j: (j, 0, 0)),
+        out_specs=pl.BlockSpec((4, HD, 512), lambda j: (j, 0, 0)),
         scratch_shapes=[pltpu.VMEM((2, 2048, HD), BF), pltpu.VMEM((2, HD, 2048), BF)],
         cost_estimate=pl.CostEstimate(flops=2**33, bytes_accessed=3 * 2**20, transcendentals=2**23),
         compiler_params=pltpu.CompilerParams(vmem_limit_bytes=24 * 2**20),
@@ -258,9 +258,15 @@
 def last_kernel(flags, attn, a_rec, m0, m1, p0, p1, h2, nt, mods, block_out, ns_out):
     first = flags[1] == 0
     mine, received = attn[:, :TOK], a_rec[...]
-    low = jnp.where(first, mine, received).astype(F32).T.astype(BF)
-    high = jnp.where(first, received, mine).astype(F32).T.astype(BF)
-    ns = out_dot(flags, low, high, (m0, m1), (p0, p1))
+    a = jnp.concatenate([jnp.where(first, mine, received), jnp.where(first, received, mine)], axis=0)
+    a = a.astype(F32).T.astype(BF)
+    halves = []
+    for xl0, xl1 in ((m0, m1), (p0, p1)):
+        w = jnp.concatenate([xl0[...], xl1[...]], axis=0)
+        halves.append(jnp.dot(a, w, preferred_element_type=F32).astype(BF))
+    low = jnp.where(first, halves[0], halves[1])
+    high = jnp.where(first, halves[1], halves[0])
+    ns = jnp.concatenate([low, high], axis=1)
     ns_out[...] = ns
     h = gated(h2[...], mods[8:9], ns)
     block_out[...] = gated(h, mods[11:12], nt[...])

time: 205 us -> 205 us (level)
  no operation moved by 1% of the time
where the time goes in v5:
time: 205 us; the launch traced here: 204 us
  waiting for transfers between devices  75 us (37%)
  starting transfers between devices  43.5 us (21%)
  Pallas kernels  32 us (16%)
  blocking collectives  26.9 us (13%)
  between operations  13.9 us (7%)
  local copies, waits for them, and re-layouts  11.5 us (6%)
    all_gather x3, waiting for transfers between devices, gather_z(): return lax.all_gather(w, 'z', axis=0, tiled=True)  31.8 us
    all_to_all x1, blocking collectives, shards(): packed = lax.all_to_all(packed, ('xh', 'y'), 0, 0, tiled=True)  26.9 us
    ppermute x8, starting transfers between devices, core_swap(): return lax.ppermute(a, 'c', CORE)  19.7 us
    ppermute x1, waiting for transfers between devices, from_x(): lax.ppermute(own[:288], XX, X_UP)  11.6 us
    pallas_call x1, Pallas kernels, spatial_attend(): pl.pallas_call(spatial_kernel, name='spatial_attend', grid=(2,), out_shap...  8.77 us
    pallas_call x1, Pallas kernels, shards(): call(temporal_kernel, 'temporal', (sds(TOK, HALF), sds(TOK, HALF)), [SMEM...  6.35 us
    ppermute x1, waiting for transfers between devices, shards(): lax.ppermute(theirs, 'xl', CORE)  5.79 us
    all_to_all x1, starting transfers between devices, shards(): chunks = lax.all_to_all(attn.reshape(16, 16, D), TM, 0, 0, tiled=True)  5.19 us
  transfers between devices with their start and end apart: 21, of which 13 were waited for; matrix products, arithmetic and copies ran while one was open for 5% of the time, Pallas kernels for 11%

profile of v5, /device:TPU:1, one launch (start us, length us, event | category | flops | bytes accessed | tf_op | source)
XLA Modules:
  0.0 203.9 jit_solution(3506925864724299778)
XLA Ops:
  7.2 0.1 pad_add_fusion.flags
  7.3 1.3 copy-done.2
  8.6 2.0 prepare.1
  10.6 0.0 all-gather.6.cloned.1.call-start
  10.7 2.1 %collective-permute-start.4 = (bf16[72,2176]{1,0:T(8,128)(2,1)S(1)}, bf16[72,2176]{1,0:T(8,128)(2,1)S(1)}, u32[]{:S(2)}, u32[]{:S(2)}) collective-permute-start(bf16[72,2176]{1,0:T(8,128)(2,1)S(1)} %get-tuple-element.28), channel_id=1, source_target_pairs={{0,128},{128,0},{1,129},{129,1},{2,130},{130,2},{3,131},{131,3},{4... | collective-permute-start | bytes 940040 | tf_op jit(solution)/shard_map/ppermute | solution.py:310
  12.8 5.8 %collective-permute-done.4.other = bf16[72,2176]{1,0:T(8,128)(2,1)S(1)} collective-permute-done((bf16[72,2176]{1,0:T(8,128)(2,1)S(1)}, bf16[72,2176]{1,0:T(8,128)(2,1)S(1)}, u32[]{:S(2)}, u32[]{:S(2)}) %collective-permute-start.4) | collective-permute-done | bytes 313376 | tf_op jit(solution)/shard_map/ppermute | solution.py:310
  18.6 1.4 join.1
  20.1 1.4 first.1
  21.6 30.3 %all-gather.4.cloned.1.call-done.w_own = bf16[576,1728]{1,0:T(8,128)(2,1)} async-done(((bf16[72,1728]{1,0:T(8,128)(2,1)}), bf16[576,1728]{1,0:T(8,128)(2,1)}) %all-gather.4.cloned.1.call-update) | async-done | bytes 1990672 | tf_op jit(solution)/shard_map/all_gather | solution.py:288
  51.9 5.0 %all-to-all-start = ((bf16[16,16,1152]{2,1,0:T(8,128)(2,1)}), bf16[16,16,1152]{2,1,0:T(8,128)(2,1)S(1)}, u32[]{:S(2)}, u32[]{:S(2)}) async-start(bf16[16,16,1152]{2,1,0:T(8,128)(2,1)} %get-tuple-element.24), calls=%async_computation | async-start | bytes 1179648 | tf_op jit(solution)/shard_map/all_to_all | solution.py:318
  57.0 3.2 %fusion.2 = (bf16[288,1728]{1,0:T(8,128)(2,1)}, bf16[288,1728]{1,0:T(8,128)(2,1)}) fusion(bf16[576,1728]{1,0:T(8,128)(2,1)} %all-gather.4.cloned.1.call-done.w_own), kind=kLoop, calls=%fused_computation.4 | loop fusion | bytes 3981312 | tf_op jit(solution)/shard_map/slice | solution.py:283
  60.1 1.4 collective-permute-start.1
  61.5 1.3 collective-permute-start.2
  62.8 5.2 %all-to-all-done = bf16[16,16,1152]{2,1,0:T(8,128)(2,1)S(1)} async-done(((bf16[16,16,1152]{2,1,0:T(8,128)(2,1)}), bf16[16,16,1152]{2,1,0:T(8,128)(2,1)S(1)}, u32[]{:S(2)}, u32[]{:S(2)}) %all-to-all-start) | async-done | bytes 589856 | tf_op jit(solution)/shard_map/all_to_all | solution.py:318
  68.0 7.7 %collective-permute-start = (bf16[256,1152]{1,0:T(8,128)(2,1)S(1)}, bf16[256,1152]{1,0:T(8,128)(2,1)S(1)}, u32[]{:S(2)}, u32[]{:S(2)}) collective-permute-start(bf16[256,1152]{1,0:T(8,128)(2,1)S(1)} %bitcast.21), channel_id=1, source_target_pairs={{0,1},{1,0},{2,3},{3,2},{4,5},{5,4},{6,7},{7,6},{8,9},{9,8},{10,11... | collective-permute-start | bytes 1769480 | tf_op jit(solution)/shard_map/ppermute | solution.py:276
  75.7 11.6 %collective-permute-done.1.w_a = bf16[288,1728]{1,0:T(8,128)(2,1)} collective-permute-done((bf16[288,1728]{1,0:T(8,128)(2,1)}, bf16[288,1728]{1,0:T(8,128)(2,1)}, u32[]{:S(2)}, u32[]{:S(2)}) %collective-permute-start.1) | collective-permute-done | bytes 995360 | tf_op jit(solution)/shard_map/ppermute | solution.py:282
  87.2 1.6 collective-permute-done.2.w_b
  88.9 6.4 %temporal.1 = (bf16[256,576]{1,0:T(8,128)(2,1)S(1)}, bf16[256,576]{1,0:T(8,128)(2,1)S(1)}) custom-call(s32[3]{0:T(128)S(1)} %pad_add_fusion.flags, bf16[256,1152]{1,0:T(8,128)(2,1)S(1)} %bitcast.22, bf16[256,1152]{1,0:T(8,128)(2,1)S(1)} %collective-permute-done.x_other, bf16[576,1728]{1,0:T(8,128)(2,1)S(1)} %copy-done.1, ...), custom_call_target="tpu_custom_call" | custom-call | flops 2147483648 | bytes 6291456 | tf_op jit(solution)/shard_map/temporal/pallas_call | solution.py:320
  95.2 3.2 %collective-permute-start.3 = (bf16[256,576]{1,0:T(8,128)(2,1)S(1)}, bf16[256,576]{1,0:T(8,128)(2,1)S(1)}, u32[]{:S(2)}, u32[]{:S(2)}) collective-permute-start(bf16[256,576]{1,0:T(8,128)(2,1)S(1)} %get-tuple-element.26), channel_id=1, source_target_pairs={{0,1},{1,0},{2,3},{3,2},{4,5},{5,4},{6,7},{7,6},{8,9},{9,8},{10,11... | collective-permute-start | bytes 884744 | tf_op jit(solution)/shard_map/ppermute | solution.py:276
  98.4 1.3 collective-permute-done.3
  99.7 1.0 pad_maximum_fusion
  100.7 5.2 %all-to-all-start.1 = ((bf16[16,16,1152]{2,1,0:T(8,128)(2,1)}), bf16[16,16,1152]{2,1,0:T(8,128)(2,1)S(1)}, u32[]{:S(2)}, u32[]{:S(2)}) async-start(bf16[16,16,1152]{2,1,0:T(8,128)(2,1)} %bitcast.6), calls=%async_computation.1 | async-start | bytes 1179648 | tf_op jit(solution)/shard_map/all_to_all | solution.py:332
  105.9 1.5 all-gather.6.cloned.1.call-done.gathered
  107.4 1.5 fusion.1
  108.8 0.5 collective-permute-start.5
  109.4 0.1 collective-permute-start.6
  109.5 2.9 %fusion = (bf16[288,864]{1,0:T(8,128)(2,1)}, bf16[288,864]{1,0:T(8,128)(2,1)}, bf16[288,864]{1,0:T(8,128)(2,1)}, bf16[288,864]{1,0:T(8,128)(2,1)}) fusion(bf16[576,3072]{1,0:T(8,128)(2,1)} %all-gather.6.cloned.1.call-done.gathered), kind=kLoop, calls=%fused_computation.2 | loop fusion | bytes 3981312 | tf_op jit(solution)/shard_map/slice | solution.py:338
  112.4 2.4 %collective-permute-start.10 = (bf16[288,864]{1,0:T(8,128)(2,1)}, bf16[288,864]{1,0:T(8,128)(2,1)}, u32[]{:S(2)}, u32[]{:S(2)}) collective-permute-start(bf16[288,864]{1,0:T(8,128)(2,1)} %get-tuple-element.45), channel_id=1, source_target_pairs={{0,136},{128,0},{8,128},{136,8},{1,137},{129,1},{9,129},{137,9},{2... | collective-permute-start | bytes 1493000 | tf_op jit(solution)/shard_map/ppermute | solution.py:338
  114.8 1.2 collective-permute-start.7
  116.0 1.5 collective-permute-start.8
  117.5 4.1 %all-to-all-done.1.chunks = bf16[16,16,1152]{2,1,0:T(8,128)(2,1)S(1)} async-done(((bf16[16,16,1152]{2,1,0:T(8,128)(2,1)}), bf16[16,16,1152]{2,1,0:T(8,128)(2,1)S(1)}, u32[]{:S(2)}, u32[]{:S(2)}) %all-to-all-start.1) | async-done | bytes 589856 | tf_op jit(solution)/shard_map/all_to_all | solution.py:332
  121.6 3.8 %middle.1 = (bf16[256,1152]{1,0:T(8,128)(2,1)}, bf16[256,1152]{1,0:T(8,128)(2,1)S(1)}, bf16[256,1152]{1,0:T(8,128)(2,1)S(1)}) custom-call(s32[3]{0:T(128)S(1)} %pad_add_fusion.flags, bf16[256,1152]{1,0:T(8,128)(2,1)S(1)} %get-tuple-element.21.h1, bf16[16,16,1152]{2,1,0:T(8,128)(2,1)S(1)} %all-to-all-done.1.chunks, ...), custom_call_target="tpu_custom_call" | custom-call | flops 1073741824 | bytes 5242880 | tf_op jit(solution)/shard_map/middle/pallas_call | solution.py:342
  125.4 4.3 %collective-permute-done.10.f3 = bf16[288,864]{1,0:T(8,128)(2,1)} collective-permute-done((bf16[288,864]{1,0:T(8,128)(2,1)}, bf16[288,864]{1,0:T(8,128)(2,1)}, u32[]{:S(2)}, u32[]{:S(2)}) %collective-permute-start.10) | collective-permute-done | bytes 497696 | tf_op jit(solution)/shard_map/ppermute | solution.py:338
  129.7 1.2 collective-permute-done.9.f2
  131.0 2.2 %collective-permute-start.11 = (bf16[256,1152]{1,0:T(8,128)(2,1)S(1)}, bf16[256,1152]{1,0:T(8,128)(2,1)S(1)}, u32[]{:S(2)}, u32[]{:S(2)}) collective-permute-start(bf16[256,1152]{1,0:T(8,128)(2,1)S(1)} %get-tuple-element.32.x_own), channel_id=1, source_target_pairs={{0,1},{1,0},{2,3},{3,2},{4,5},{5,4},{6,7},{7,6},{8,9},{9,8},{10,11... | collective-permute-start | bytes 1769480 | tf_op jit(solution)/shard_map/ppermute | solution.py:276
  133.2 1.6 collective-permute-done.11.x_other
  134.8 4.6 %spatial_qkv.1 = bf16[8,3,72,512]{3,2,1,0:T(8,128)(2,1)S(1)} custom-call(s32[3]{0:T(128)S(1)} %pad_add_fusion.flags, bf16[256,1152]{1,0:T(8,128)(2,1)S(1)} %get-tuple-element.32.x_own, bf16[256,1152]{1,0:T(8,128)(2,1)S(1)} %collective-permute-done.11.x_other, bf16[576,3072]{1,0:T(8,128)(2,1)S(1)} %copy-done, bf16[288,864]{1,0:T(8,128)(2,1)} %collective-permute-done.7.f0, ...), custom_call_target="tpu_custom_call" | custom-call | flops 2147483648 | bytes 6291456 | tf_op jit(solution)/shard_map/spatial_qkv/pallas_call | solution.py:352
  139.5 26.9 %all_to_all.20.q_ref.all_ref = bf16[8,3,72,512]{3,2,1,0:T(8,128)(2,1)S(1)} all-to-all(bf16[8,3,72,512]{3,2,1,0:T(8,128)(2,1)S(1)} %spatial_qkv.1), channel_id=1, replica_groups=mesh['xl'=2,'z'=8,'xh'=2,'y'=4,'c'=2] {'xh','y'}, dimensions={0} | all-to-all | bytes 3538944 | tf_op jit(solution)/shard_map/all_to_all | solution.py:362
  166.4 8.8 %spatial_attend.1 = bf16[8,72,512]{2,1,0:T(8,128)(2,1)} custom-call(bf16[8,3,72,512]{3,2,1,0:T(8,128)(2,1)S(1)} %all_to_all.20.q_ref.all_ref, bf16[8,3,72,512]{3,2,1,0:T(8,128)(2,1)S(1)} %all_to_all.20.q_ref.all_ref), custom_call_target="tpu_custom_call" | custom-call | flops 8589934592 | bytes 3145728 | tf_op jit(solution)/shard_map/spatial_attend/pallas_call | solution.py:219
  175.2 3.5 %all-to-all-start.3 = ((bf16[8,72,512]{2,1,0:T(8,128)(2,1)}), bf16[8,72,512]{2,1,0:T(8,128)(2,1)S(1)}, u32[]{:S(2)}, u32[]{:S(2)}) async-start(bf16[8,72,512]{2,1,0:T(8,128)(2,1)} %spatial_attend.1), calls=%async_computation.3 | async-start | bytes 1179648 | tf_op jit(solution)/shard_map/all_to_all | solution.py:366
  178.7 1.5 fusion.3
  180.3 2.2 %collective-permute-start.13 = (bf16[576,576]{1,0:T(8,128)(2,1)S(1)}, bf16[576,576]{1,0:T(8,128)(2,1)S(1)}, u32[]{:S(2)}, u32[]{:S(2)}) collective-permute-start(bf16[576,576]{1,0:T(8,128)(2,1)S(1)} %get-tuple-element.54.m0), channel_id=1, source_target_pairs={{0,1},{1,0},{2,3},{3,2},{4,5},{5,4},{6,7},{7,6},{8,9},{9,8},{10,11... | collective-permute-start | bytes 1990664 | tf_op jit(solution)/shard_map/ppermute | solution.py:276
  182.5 0.1 collective-permute-start.14
  182.6 5.2 %all-to-all-done.3 = bf16[8,72,512]{2,1,0:T(8,128)(2,1)S(1)} async-done(((bf16[8,72,512]{2,1,0:T(8,128)(2,1)}), bf16[8,72,512]{2,1,0:T(8,128)(2,1)S(1)}, u32[]{:S(2)}, u32[]{:S(2)}) %all-to-all-start.3) | async-done | bytes 589856 | tf_op jit(solution)/shard_map/all_to_all | solution.py:366
  187.8 3.7 %collective-permute-start.12 = (bf16[576,256]{1,0:T(8,128)(2,1)S(1)}, bf16[576,256]{1,0:T(8,128)(2,1)S(1)}, u32[]{:S(2)}, u32[]{:S(2)}) collective-permute-start(bf16[576,256]{1,0:T(8,128)(2,1)S(1)} %slice.52), channel_id=1, source_target_pairs={{0,1},{1,0},{2,3},{3,2},{4,5},{5,4},{6,7},{7,6},{8,9},{9,8},{10,11... | collective-permute-start | bytes 884744 | tf_op jit(solution)/shard_map/ppermute | solution.py:276
  191.5 1.2 collective-permute-done.12.a_rec
  192.7 1.1 copy-done.7
  193.8 3.6 %last.1 = (bf16[256,1152]{1,0:T(8,128)(2,1)}, bf16[256,1152]{1,0:T(8,128)(2,1)}) custom-call(s32[3]{0:T(128)S(1)} %pad_add_fusion.flags, bf16[576,512]{1,0:T(8,128)(2,1)S(1)} %bitcast.18, bf16[576,256]{1,0:T(8,128)(2,1)S(1)} %collective-permute-done.12.a_rec, bf16[576,576]{1,0:T(8,128)(2,1)S(1)} %get-tuple-element.54.m0, ...), custom_call_target="tpu_custom_call" | custom-call | flops 1073741824 | bytes 6291456 | tf_op jit(solution)/shard_map/last/pallas_call | solution.py:368
  (33 shorter events, 0.3 us)
Async XLA Ops:
  7.2 44.7 %all-gather.4.cloned.1.call-start = ((), (), s32[]{:S(2)}) async-start(), calls=%async_computation.4 | async-start | bytes 2322432 | tf_op jit(solution)/shard_map/all_gather | solution.py:288
  7.3 1.3 copy-start.2
  8.6 11.4 %copy-start.8 = (f32[2,2,3,1152]{3,1,2,0:T(2,128)S(1)}, f32[2,2,3,1152]{3,1,2,0:T(2,128)}, u32[]{:S(2)}) copy-start(f32[2,2,3,1152]{3,1,2,0:T(2,128)} %param.6) | copy-start | bytes 165892
  8.6 11.5 %copy-start.3 = (bf16[2,1,128,1152]{3,2,1,0:T(8,128)(2,1)S(1)}, bf16[2,1,128,1152]{3,2,1,0:T(8,128)(2,1)}, u32[]{:S(2)}) copy-start(bf16[2,1,128,1152]{3,2,1,0:T(8,128)(2,1)} %param.4) | copy-start | bytes 1769476
  8.6 11.5 %copy-start.4 = (bf16[2,1,128,1152]{3,2,1,0:T(8,128)(2,1)S(1)}, bf16[2,1,128,1152]{3,2,1,0:T(8,128)(2,1)}, u32[]{:S(2)}) copy-start(bf16[2,1,128,1152]{3,2,1,0:T(8,128)(2,1)} %param.5) | copy-start | bytes 1769476
  10.6 96.7 %all-gather.6.cloned.1.call-start = ((), (), s32[]{:S(2)}) async-start(), calls=%async_computation.5 | async-start | bytes 3981312 | tf_op jit(solution)/shard_map/all_gather | solution.py:288
  10.7 7.9 %collective-permute-start.4 = (bf16[72,2176]{1,0:T(8,128)(2,1)S(1)}, bf16[72,2176]{1,0:T(8,128)(2,1)S(1)}, u32[]{:S(2)}, u32[]{:S(2)}) collective-permute-start(bf16[72,2176]{1,0:T(8,128)(2,1)S(1)} %get-tuple-element.28), channel_id=1, source_target_pairs={{0,128},{128,0},{1,129},{129,1},{2,130},{130,2},{3,131},{131,3},{4... | collective-permute-start | bytes 940040 | tf_op jit(solution)/shard_map/ppermute | solution.py:310
  51.9 16.1 %all-to-all-start = ((bf16[16,16,1152]{2,1,0:T(8,128)(2,1)}), bf16[16,16,1152]{2,1,0:T(8,128)(2,1)S(1)}, u32[]{:S(2)}, u32[]{:S(2)}) async-start(bf16[16,16,1152]{2,1,0:T(8,128)(2,1)} %get-tuple-element.24), calls=%async_computation | async-start | bytes 1179648 | tf_op jit(solution)/shard_map/all_to_all | solution.py:318
  57.0 31.9 %copy-start.1 = (bf16[576,1728]{1,0:T(8,128)(2,1)S(1)}, bf16[576,1728]{1,0:T(8,128)(2,1)}, u32[]{:S(2)}) copy-start(bf16[576,1728]{1,0:T(8,128)(2,1)} %all-gather.4.cloned.1.call-done.w_own) | copy-start | bytes 5971972
  60.1 27.1 %collective-permute-start.1 = (bf16[288,1728]{1,0:T(8,128)(2,1)}, bf16[288,1728]{1,0:T(8,128)(2,1)}, u32[]{:S(2)}, u32[]{:S(2)}) collective-permute-start(bf16[288,1728]{1,0:T(8,128)(2,1)} %get-tuple-element.52), channel_id=1, source_target_pairs={{0,128},{128,8},{8,136},{136,0},{1,129},{129,9},{9,137},{137,1},{2... | collective-permute-start | bytes 2985992 | tf_op jit(solution)/shard_map/ppermute | solution.py:282
  61.5 27.4 %collective-permute-start.2 = (bf16[288,1728]{1,0:T(8,128)(2,1)}, bf16[288,1728]{1,0:T(8,128)(2,1)}, u32[]{:S(2)}, u32[]{:S(2)}) collective-permute-start(bf16[288,1728]{1,0:T(8,128)(2,1)} %get-tuple-element.51), channel_id=1, source_target_pairs={{0,136},{128,0},{8,128},{136,8},{1,137},{129,1},{9,129},{137,9},{2... | collective-permute-start | bytes 2985992 | tf_op jit(solution)/shard_map/ppermute | solution.py:283
  68.0 20.9 %collective-permute-start = (bf16[256,1152]{1,0:T(8,128)(2,1)S(1)}, bf16[256,1152]{1,0:T(8,128)(2,1)S(1)}, u32[]{:S(2)}, u32[]{:S(2)}) collective-permute-start(bf16[256,1152]{1,0:T(8,128)(2,1)S(1)} %bitcast.21), channel_id=1, source_target_pairs={{0,1},{1,0},{2,3},{3,2},{4,5},{5,4},{6,7},{7,6},{8,9},{9,8},{10,11... | collective-permute-start | bytes 1769480 | tf_op jit(solution)/shard_map/ppermute | solution.py:276
  95.2 4.5 %collective-permute-start.3 = (bf16[256,576]{1,0:T(8,128)(2,1)S(1)}, bf16[256,576]{1,0:T(8,128)(2,1)S(1)}, u32[]{:S(2)}, u32[]{:S(2)}) collective-permute-start(bf16[256,576]{1,0:T(8,128)(2,1)S(1)} %get-tuple-element.26), channel_id=1, source_target_pairs={{0,1},{1,0},{2,3},{3,2},{4,5},{5,4},{6,7},{7,6},{8,9},{9,8},{10,11... | collective-permute-start | bytes 884744 | tf_op jit(solution)/shard_map/ppermute | solution.py:276
  100.7 20.9 %all-to-all-start.1 = ((bf16[16,16,1152]{2,1,0:T(8,128)(2,1)}), bf16[16,16,1152]{2,1,0:T(8,128)(2,1)S(1)}, u32[]{:S(2)}, u32[]{:S(2)}) async-start(bf16[16,16,1152]{2,1,0:T(8,128)(2,1)} %bitcast.6), calls=%async_computation.1 | async-start | bytes 1179648 | tf_op jit(solution)/shard_map/all_to_all | solution.py:332
  105.9 72.9 %all-gather.8.cloned.1.call-start = ((), (), s32[]{:S(2)}) async-start(), calls=%async_computation.6 | async-start | bytes 1658880 | tf_op jit(solution)/shard_map/all_gather | solution.py:288
  108.8 8.6 %collective-permute-start.5 = (bf16[576,576]{1,0:T(8,128)(2,1)S(1)}, bf16[576,576]{1,0:T(8,128)(2,1)S(1)}, u32[]{:S(2)}, u32[]{:S(2)}) collective-permute-start(bf16[576,576]{1,0:T(8,128)(2,1)S(1)} %get-tuple-element.50.m0), channel_id=1, source_target_pairs={{0,1},{1,0},{2,3},{3,2},{4,5},{5,4},{6,7},{7,6},{8,9},{9,8},{10,11... | collective-permute-start | bytes 1990664 | tf_op jit(solution)/shard_map/ppermute | solution.py:276
  109.4 12.2 %collective-permute-start.6 = (bf16[576,576]{1,0:T(8,128)(2,1)S(1)}, bf16[576,576]{1,0:T(8,128)(2,1)}, u32[]{:S(2)}, u32[]{:S(2)}) collective-permute-start(bf16[576,576]{1,0:T(8,128)(2,1)S(1)} %get-tuple-element.49.m1), channel_id=1, source_target_pairs={{0,1},{1,0},{2,3},{3,2},{4,5},{5,4},{6,7},{7,6},{8,9},{9,8},{10,11... | collective-permute-start | bytes 1990664 | tf_op jit(solution)/shard_map/ppermute | solution.py:276
  112.4 17.4 %collective-permute-start.10 = (bf16[288,864]{1,0:T(8,128)(2,1)}, bf16[288,864]{1,0:T(8,128)(2,1)}, u32[]{:S(2)}, u32[]{:S(2)}) collective-permute-start(bf16[288,864]{1,0:T(8,128)(2,1)} %get-tuple-element.45), channel_id=1, source_target_pairs={{0,136},{128,0},{8,128},{136,8},{1,137},{129,1},{9,129},{137,9},{2... | collective-permute-start | bytes 1493000 | tf_op jit(solution)/shard_map/ppermute | solution.py:338
  114.8 15.0 %collective-permute-start.7 = (bf16[288,864]{1,0:T(8,128)(2,1)}, bf16[288,864]{1,0:T(8,128)(2,1)}, u32[]{:S(2)}, u32[]{:S(2)}) collective-permute-start(bf16[288,864]{1,0:T(8,128)(2,1)} %get-tuple-element.48), channel_id=1, source_target_pairs={{0,2},{2,4},{4,6},{6,0},{1,3},{3,5},{5,7},{7,1},{8,10},{10,12},{12... | collective-permute-start | bytes 1493000 | tf_op jit(solution)/shard_map/ppermute | solution.py:335
  116.0 13.8 %collective-permute-start.8 = (bf16[288,864]{1,0:T(8,128)(2,1)}, bf16[288,864]{1,0:T(8,128)(2,1)}, u32[]{:S(2)}, u32[]{:S(2)}) collective-permute-start(bf16[288,864]{1,0:T(8,128)(2,1)} %get-tuple-element.47), channel_id=1, source_target_pairs={{0,6},{2,0},{4,2},{6,4},{1,7},{3,1},{5,3},{7,5},{8,14},{10,8},{12,... | collective-permute-start | bytes 1493000 | tf_op jit(solution)/shard_map/ppermute | solution.py:336
  117.5 13.5 %collective-permute-start.9 = (bf16[288,864]{1,0:T(8,128)(2,1)}, bf16[288,864]{1,0:T(8,128)(2,1)}, u32[]{:S(2)}, u32[]{:S(2)}) collective-permute-start(bf16[288,864]{1,0:T(8,128)(2,1)} %get-tuple-element.46), channel_id=1, source_target_pairs={{0,128},{128,8},{8,136},{136,0},{1,129},{129,9},{9,137},{137,1},{2... | collective-permute-start | bytes 1493000 | tf_op jit(solution)/shard_map/ppermute | solution.py:337
  121.6 13.2 %copy-start = (bf16[576,3072]{1,0:T(8,128)(2,1)S(1)}, bf16[576,3072]{1,0:T(8,128)(2,1)}, u32[]{:S(2)}) copy-start(bf16[576,3072]{1,0:T(8,128)(2,1)} %all-gather.6.cloned.1.call-done.gathered) | copy-start | bytes 10616836
  125.4 14.0 %copy-start.6 = (bf16[256,1152]{1,0:T(8,128)(2,1)}, bf16[256,1152]{1,0:T(8,128)(2,1)S(1)}, u32[]{:S(2)}) copy-start(bf16[256,1152]{1,0:T(8,128)(2,1)S(1)} %get-tuple-element.35.h2) | copy-start | bytes 1769476
  131.0 3.8 %collective-permute-start.11 = (bf16[256,1152]{1,0:T(8,128)(2,1)S(1)}, bf16[256,1152]{1,0:T(8,128)(2,1)S(1)}, u32[]{:S(2)}, u32[]{:S(2)}) collective-permute-start(bf16[256,1152]{1,0:T(8,128)(2,1)S(1)} %get-tuple-element.32.x_own), channel_id=1, source_target_pairs={{0,1},{1,0},{2,3},{3,2},{4,5},{5,4},{6,7},{7,6},{8,9},{9,8},{10,11... | collective-permute-start | bytes 1769480 | tf_op jit(solution)/shard_map/ppermute | solution.py:276
  175.2 12.6 %all-to-all-start.3 = ((bf16[8,72,512]{2,1,0:T(8,128)(2,1)}), bf16[8,72,512]{2,1,0:T(8,128)(2,1)S(1)}, u32[]{:S(2)}, u32[]{:S(2)}) async-start(bf16[8,72,512]{2,1,0:T(8,128)(2,1)} %spatial_attend.1), calls=%async_computation.3 | async-start | bytes 1179648 | tf_op jit(solution)/shard_map/all_to_all | solution.py:366
  178.7 14.0 %copy-start.5 = (bf16[256,1152]{1,0:T(8,128)(2,1)S(1)}, bf16[256,1152]{1,0:T(8,128)(2,1)}, u32[]{:S(2)}) copy-start(bf16[256,1152]{1,0:T(8,128)(2,1)} %get-tuple-element.36.nt) | copy-start | bytes 1769476
  180.3 12.4 %collective-permute-start.13 = (bf16[576,576]{1,0:T(8,128)(2,1)S(1)}, bf16[576,576]{1,0:T(8,128)(2,1)S(1)}, u32[]{:S(2)}, u32[]{:S(2)}) collective-permute-start(bf16[576,576]{1,0:T(8,128)(2,1)S(1)} %get-tuple-element.54.m0), channel_id=1, source_target_pairs={{0,1},{1,0},{2,3},{3,2},{4,5},{5,4},{6,7},{7,6},{8,9},{9,8},{10,11... | collective-permute-start | bytes 1990664 | tf_op jit(solution)/shard_map/ppermute | solution.py:276
  182.5 10.3 %collective-permute-start.14 = (bf16[576,576]{1,0:T(8,128)(2,1)S(1)}, bf16[576,576]{1,0:T(8,128)(2,1)}, u32[]{:S(2)}, u32[]{:S(2)}) collective-permute-start(bf16[576,576]{1,0:T(8,128)(2,1)S(1)} %get-tuple-element.53.m1), channel_id=1, source_target_pairs={{0,1},{1,0},{2,3},{3,2},{4,5},{5,4},{6,7},{7,6},{8,9},{9,8},{10,11... | collective-permute-start | bytes 1990664 | tf_op jit(solution)/shard_map/ppermute | solution.py:276
  187.8 4.9 %collective-permute-start.12 = (bf16[576,256]{1,0:T(8,128)(2,1)S(1)}, bf16[576,256]{1,0:T(8,128)(2,1)S(1)}, u32[]{:S(2)}, u32[]{:S(2)}) collective-permute-start(bf16[576,256]{1,0:T(8,128)(2,1)S(1)} %slice.52), channel_id=1, source_target_pairs={{0,1},{1,0},{2,3},{3,2},{4,5},{5,4},{6,7},{7,6},{8,9},{9,8},{10,11... | collective-permute-start | bytes 884744 | tf_op jit(solution)/shard_map/ppermute | solution.py:276
  192.7 1.1 copy-start.7
Sparse Core Ops, SparseCore 0:
  10.7 41.1 all-gather.3
  54.3 53.0 all-gather.5
  139.6 32.6 all-gather.7
